TPU v7x, 32 devices: a whole 2x2x4 slice. The times are simulated.
32 devices in a mesh: sensor: 4 (over z), channel: 4 (over y, x), tm: 2 (over core).
Axes of the slice: x: 2, y: 2, z: 4, core: 2. Of those that a mesh axis runs over, the one named last changes fastest.
Arguments:
- tensor: float32 [3072, 128, 512], P('sensor', 'tm', 'channel'), may hold values from -6 to 6
- core: float32 [64, 64, 32], replicated, may hold values from -0.015625 to 0.015625
- sensor_factor: float32 [3072, 64], P('sensor'), may hold values from -6 to 6
- channel_factor: float32 [512, 64], P('channel'), may hold values from -6 to 6
- time_factor: float32 [128, 32], P('tm'), may hold values from -6 to 6
- neighbour_ids: int32 [24, 4], P('sensor'), may hold values from 0 to 23
- edge_weights: int32 [24, 4, 128, 128], P('sensor'), may hold values from 0 to 3
Outputs:
- core_grad: float32 [64, 64, 32], replicated
- sensor_grad: float32 [3072, 64], P(('sensor', 'channel', 'tm'))
- channel_grad: float32 [512, 64], P('channel')
- time_grad: float32 [128, 32], P('tm')
All inputs are finite; a program needn't handle non-finite values.
Results may differ from a plain program's by a relative error of at most 0.0001.
Values sent between devices are 32-bit elements; how exact they have to be, the bound alone decides.
No kernel may reach another device: no remote copies, remote signals or barrier semaphores. Data moves between devices by JAX's collectives and lax.ppermute only.
A program may use at most 192 MiB of HBM per device.

v0:
```python
import math

import jax
import jax.numpy as jnp
from jax import lax
from jax.sharding import PartitionSpec as P

lap_weight = 1.0 / 512.0
highest = lax.Precision.HIGHEST


def pulled_rows(whole_factor, neighbour_ids, weights_float, block):
    whole = whole_factor.reshape(-1, block, whole_factor.shape[-1])
    neighbours = whole[neighbour_ids]
    return jnp.einsum("bnic,bncd->bid", weights_float, neighbours, precision=highest)


def on_device(
    tensor, core, sensor_factor, channel_factor, time_factor, neighbour_ids, edge_weights
):
    sensor_rows, time_rows, chan_rows = tensor.shape
    rank_one, rank_two, rank_three = core.shape
    n_sensor = lax.axis_size("sensor")
    n_channel = lax.axis_size("channel")
    n_time = lax.axis_size("tm")
    total_sensors = sensor_rows * n_sensor
    total_time = time_rows * n_time
    total_chan = chan_rows * n_channel
    core_time = jnp.einsum("rst,kt->rks", core, time_factor, precision=highest)
    core_both = jnp.einsum("rks,js->rkj", core_time, channel_factor, precision=highest)
    core_chan = jnp.einsum("rst,js->rtj", core, channel_factor, precision=highest)
    flat_core = core_both.reshape(rank_one, time_rows * chan_rows)
    residual = jnp.dot(sensor_factor, flat_core, precision=highest) - tensor.reshape(
        sensor_rows, time_rows * chan_rows
    )
    folded = jnp.dot(sensor_factor.T, residual, precision=highest)
    fit_part = jnp.dot(residual, flat_core.T, precision=highest) / math.sqrt(
        total_time * total_chan
    )
    folded3 = folded.reshape(rank_one, time_rows, chan_rows)
    inner = jnp.einsum("rkj,js->rks", folded3, channel_factor, precision=highest)
    core_part = jnp.einsum("rks,kt->rst", inner, time_factor, precision=highest) / math.sqrt(
        total_sensors * total_time * total_chan
    )
    chan_part = jnp.einsum("rkj,rks->js", folded3, core_time, precision=highest) / math.sqrt(
        total_sensors * total_time
    )
    time_part = jnp.einsum("rkj,rtj->kt", folded3, core_chan, precision=highest) / math.sqrt(
        total_sensors * total_chan
    )
    groups = n_channel * n_time
    share_index = lax.axis_index("channel") * n_time + lax.axis_index("tm")
    share = sensor_rows // groups
    block = edge_weights.shape[-1]
    weights_float = edge_weights.astype(jnp.float32)
    degree = jnp.sum(weights_float, axis=(1, 3)).reshape(sensor_rows)
    reduced = lax.psum_scatter(fit_part, ("channel", "tm"), scatter_dimension=0, tiled=True)
    whole_rows = lax.all_gather(sensor_factor, "sensor", axis=0, tiled=True)
    pulled = pulled_rows(whole_rows, neighbour_ids, weights_float, block).reshape(
        sensor_rows, rank_one
    )
    graph_all = lap_weight * (degree[:, None] * sensor_factor - pulled)
    graph_share = lax.dynamic_slice_in_dim(graph_all, share_index * share, share, 0)
    sensor_grad = reduced + graph_share
    core_grad = lax.psum(core_part, ("sensor", "channel", "tm"))
    channel_grad = lax.psum(chan_part, ("sensor", "tm"))
    time_grad = lax.psum(time_part, ("sensor", "channel"))
    return (core_grad, sensor_grad, channel_grad, time_grad)


def solution(mesh):
    return jax.shard_map(
        on_device,
        mesh=mesh,
        in_specs=(
            P("sensor", "tm", "channel"),
            P(),
            P("sensor", None),
            P("channel", None),
            P("tm", None),
            P("sensor", None),
            P("sensor", None, None, None),
        ),
        out_specs=(P(), P(("sensor", "channel", "tm"), None), P("channel", None), P("tm", None)),
        check_vma=False,
    )
```

profile of v0, /device:TPU:1, one launch (start us, length us, event | category | flops | bytes accessed | tf_op | source)
XLA Modules:
  0.0 270.7 jit_solution(1938350583099662974)
XLA Ops:
  8.0 0.0 copy-start
  8.0 0.0 reduce-scatter.4.cloned.1.call-start
  8.1 24.9 %copy.27 = f32[768,64,128]{0,2,1:T(8,128)} copy(f32[768,64,128]{2,1,0:T(8,128)} %param.7) | data formatting | bytes 50331648 | tf_op args[0]
  33.0 1.8 fusion.32
  34.8 0.0 copy-start.3
  34.8 1.8 fusion.5
  36.7 26.3 %bitcast_subtract_fusion = f32[768,8192]{0,1:T(8,128)} fusion(f32[768,64,128]{0,2,1:T(8,128)} %copy.27, f32[768,64]{0,1:T(8,128)S(1)} %copy-done.3, f32[8,8,64,128]{3,2,1,0:T(8,128)S(1)} %bitcast.77), kind=kOutput, calls=%fused_computation.1 | convolution fusion | flops 4838129664 | bytes 52625408 | tf_op jit(solution)/shard_map/dot_general | solution.py:33
  63.0 20.9 %fusion.14 = f32[768,64]{0,1:T(8,128)S(1)} fusion(f32[768,8192]{0,1:T(8,128)} %bitcast_subtract_fusion, f32[8,8,64,128]{3,2,1,0:T(8,128)S(1)} %bitcast.78), kind=kOutput, calls=%fused_computation.17 | convolution fusion | flops 4831887360 | bytes 27459584 | tf_op jit(solution)/shard_map/dot_general | solution.py:37
  83.8 1.0 copy.34
  84.8 0.0 reduce-scatter.4.cloned.1.call-update
  84.8 0.0 all-reduce.2.cloned.1.call-start
  84.9 27.7 %convolution_bitcast_fusion = f32[8,8,64,128]{3,1,2,0:T(8,128)S(1)} fusion(f32[768,8192]{0,1:T(8,128)} %bitcast_subtract_fusion, f32[768,64]{0,1:T(8,128)S(1)} %copy-done.3), kind=kOutput, calls=%fused_computation.11 | convolution fusion | flops 4831838208 | bytes 27459584 | tf_op jit(solution)/shard_map/dot_general | solution.py:36
  112.6 0.4 copy.39
  113.0 1.9 fusion.28
  114.8 2.2 convolution_multiply_fusion
  117.0 0.0 all-reduce.2.cloned.1.call-update
  117.1 20.2 %all_gather.3 = f32[3072,64]{0,1:T(8,128)S(1)} all-gather(f32[768,64]{0,1:T(8,128)S(1)} %copy-done.3), channel_id=1, replica_groups=mesh['sensor'=4,'channel'=4,'tm'=2] {'sensor'}, dimensions={0}, use_global_device_ids=true | all-gather | bytes 983040 | tf_op jit(solution)/shard_map/all_gather | solution.py:58
  137.3 5.8 %fusion.20 = f32[128,64]{0,1:T(8,128)} fusion(f32[64,64,128]{2,1,0:T(8,128)S(1)} %bitcast.75, f32[64,64,64]{2,0,1:T(8,128)} %copy-done.1), kind=kOutput, calls=%fused_computation.19 | convolution fusion | flops 402661376 | bytes 3178496 | tf_op jit(solution)/shard_map/rkj,rks->js/dot_general | solution.py:45
  143.1 2.0 fusion.26
  145.0 1.0 copy_bitcast_fusion
  146.1 0.1 copy.28
  146.2 0.1 reshape.31
  146.2 2.2 convert_reduce_fusion
  148.4 2.6 gather_fusion
  151.0 3.5 %fusion.11 = f32[6,8,8,128]{3,2,1,0:T(8,128)S(1)} fusion(f32[6,4,128,64]{2,3,1,0:T(8,128)} %bitcast.79, s32[6,4,128,128]{3,2,1,0:T(8,128)} %param.13), kind=kOutput, calls=%fused_computation.16 | convolution fusion | flops 302383104 | bytes 2555904 | tf_op jit(solution)/shard_map/bnic,bncd->bid/dot_general | solution.py:15
  154.6 1.7 fusion.23
  156.3 63.0 %psum.23 = f32[64,32]{0,1:T(8,128)} all-reduce(f32[64,32]{0,1:T(8,128)S(1)} %fusion.23), channel_id=1, replica_groups=mesh['sensor'=4,'channel'=4,'tm'=2] {'sensor','channel'}, use_global_device_ids=true, to_apply=%region_4.0 | all-reduce | flops 2048 | bytes 16384 | tf_op jit(solution)/shard_map/psum | solution.py:67
  219.4 0.8 dynamic-slice
  220.1 39.2 %psum.22 = f32[128,64]{0,1:T(8,128)} all-reduce(f32[128,64]{0,1:T(8,128)} %fusion.20), channel_id=1, replica_groups=mesh['sensor'=4,'channel'=4,'tm'=2] {'sensor','tm'}, use_global_device_ids=true, to_apply=%region_3.0 | all-reduce | flops 8192 | bytes 65536 | tf_op jit(solution)/shard_map/psum | solution.py:66
  259.4 0.9 copy.35
  260.2 0.7 fusion.25
  261.0 2.3 copy.54
  (17 shorter events, 0.1 us)
Async XLA Ops:
  8.0 24.9 %copy-start = (f32[64,64,32]{1,2,0:T(8,128)S(1)}, f32[64,64,32]{1,2,0:T(8,128)}, u32[]{:S(2)}) copy-start(f32[64,64,32]{1,2,0:T(8,128)} %param.8) | copy-start | bytes 1572868
  8.0 24.9 %copy-start.5 = (f32[64,32]{0,1:T(8,128)S(1)}, f32[64,32]{0,1:T(8,128)}, u32[]{:S(2)}) copy-start(f32[64,32]{0,1:T(8,128)} %param.11) | copy-start | bytes 24580
  8.0 251.3 %reduce-scatter.4.cloned.1.call-start = ((), (), s32[]{:S(2)}) async-start(), calls=%async_computation.2 | async-start | bytes 442368
  32.9 1.9 copy-start.4
  34.8 1.9 copy-start.1
  34.8 1.9 copy-start.3
  84.8 176.2 %all-reduce.2.cloned.1.call-start = ((), (), s32[]{:S(2)}) async-start(), calls=%async_computation.1 | async-start | bytes 2097152 | tf_op jit(solution)/shard_map/psum | solution.py:65
  143.1 3.0 %copy-start.6 = (s32[6,4]{0,1:T(4,128)S(1)}, s32[6,4]{0,1:T(4,128)}, u32[]{:S(2)}) copy-start(s32[6,4]{0,1:T(4,128)} %param.12) | copy-start | bytes 292
  151.0 3.5 %copy-start.2 = (f32[64,32,128]{2,1,0:T(8,128)S(1)}, f32[64,32,128]{2,1,0:T(8,128)}, u32[]{:S(2)}) copy-start(f32[64,32,128]{2,1,0:T(8,128)} %fusion.26) | copy-start | bytes 3145732
Sparse Core Ops, SparseCore 0:
  84.9 35.4 reduce-scatter.3
Sparse Core Ops, SparseCore 1:
  117.1 132.0 all-reduce.1
where the time goes:
time: 276 us; the launch traced here: 271 us
  blocking collectives  122 us (44%)
  matrix products  95.6 us (35%)
  local copies, waits for them, and re-layouts  33.9 us (12%)
  between operations  15.6 us (6%)
  other arithmetic  2.92 us (1%)
    psum x1, blocking collectives, on_device(): time_grad = lax.psum(time_part, ('sensor', 'channel'))  63 us
    psum x1, blocking collectives, on_device(): channel_grad = lax.psum(chan_part, ('sensor', 'tm'))  39.2 us
    unnamed x19, local copies, waits for them, and re-layouts  29.4 us
    dot_general x1, matrix products, on_device(): folded = jnp.dot(sensor_factor.T, residual, precision=highest)  27.7 us
    dot_general x1, matrix products, on_device(): jnp.dot(sensor_factor, flat_core, precision=highest)  26.3 us
    dot_general x1, matrix products, on_device(): jnp.dot(residual, flat_core.T, precision=highest)  20.9 us
    all_gather x1, blocking collectives, on_device(): whole_rows = lax.all_gather(sensor_factor, 'sensor', axis=0, tiled=True)  20.2 us
    dot_general x1, matrix products, on_device(): jnp.einsum('rkj,rks->js', folded3, core_time, precision=highest)  5.79 us
  transfers between devices with their start and end apart: 2, of which 0 were waited for; matrix products, arithmetic and copies ran while one was open for 20% of the time, Pallas kernels for 0%

commit v1 on v0

v1 whole, which is shorter than its diff:
```python
import functools
import math

import jax
import jax.numpy as jnp
from jax import lax
from jax.experimental import pallas as pl
from jax.experimental.pallas import tpu as pltpu
from jax.sharding import PartitionSpec as P

lap_weight = 1.0 / 512.0
f32, bf16 = jnp.float32, jnp.bfloat16
NN = (((1,), (0,)), ((), ()))
NT = (((1,), (1,)), ((), ()))
TN = (((0,), (0,)), ((), ()))
LANES = 128
vmem = pl.BlockSpec(memory_space=pltpu.VMEM)
smem = pl.BlockSpec(memory_space=pltpu.SMEM)
anywhere = pl.BlockSpec(memory_space=pl.ANY)


def split(x):
    high = x.astype(bf16)
    return high, (x - high.astype(f32)).astype(bf16)


def dot(a, b, dims=NN):
    return lax.dot_general(a, b, dims, preferred_element_type=f32)


def dot3(a, b, dims=NN):
    return dot(a[0], b[0], dims) + (dot(a[0], b[1], dims) + dot(a[1], b[0], dims))


def halves(x):
    w = x.shape[1] // 2
    return jnp.concatenate([x[:, :w], x[:, w:]], axis=0)


def paired(x):
    n = x.shape[0] // 2
    return jnp.concatenate([x[:n], x[n:]], axis=1)


class Plan:
    def __init__(self, tensor, core, n_sensor, n_channel, n_time):
        self.sensors, self.times, self.chans = tensor
        self.r1, self.r2, self.r3 = core
        self.n_sensor, self.n_channel, self.n_time = n_sensor, n_channel, n_time
        self.parts = n_channel * n_time
        self.pairs = self.r1 // 2
        self.pairs_part = self.pairs // self.parts
        self.core_rows = self.pairs_part * self.r3
        self.time_rows = self.r3 // n_channel
        self.share = self.sensors // self.parts
        self.fit_rows = self.share // 2
        self.chunk = self.core_rows + self.time_rows + self.fit_rows
        self.sum_rows = self.core_rows + self.time_rows
        self.chan_rows = self.r2 // n_time
        self.rows = n_channel * self.chunk + self.chan_rows
        total = (self.sensors * n_sensor, self.times * n_time, self.chans * n_channel)
        self.core_scale = 1.0 / math.sqrt(total[0] * total[1] * total[2])
        self.chan_scale = 1.0 / math.sqrt(total[0] * total[1])
        self.time_scale = 1.0 / math.sqrt(total[0] * total[2])
        self.fit_scale = 1.0 / math.sqrt(total[1] * total[2])


def partial_kernel(
    p, wide, slots, tall,
    place, x_hbm, core, sensor_t, chan_t, time_t, keep, send,
    buf, sem, core_pair, ct, inner_ref, fit_acc, chan_acc, time_acc, ggt, sensor_s,
):
    r1, r2, r3 = p.r1, p.r2, p.r3
    width = wide * p.chans
    steps = p.times // wide
    my_time, my_chan = place[0], place[1]

    def copies(step, slot):
        return [
            pltpu.make_async_copy(
                x_hbm.at[:, step * wide + h, :],
                buf.at[slot, :, h * p.chans : (h + 1) * p.chans],
                sem.at[slot, h],
            )
            for h in range(wide)
        ]

    for s in range(slots):
        for c in copies(s, s):
            c.start()

    time_s = split(time_t[...])
    for r in range(p.pairs):
        pair = jnp.concatenate([core[r], core[r + p.pairs]], axis=1)
        core_pair[r] = pair
        ct[r * p.times : (r + 1) * p.times, :] = dot3(time_s, split(pair), TN)
    chan_s = split(chan_t[...])
    chan_rows = chan_t[...].T
    chan_rows_s = split(chan_rows)
    sensor_f = sensor_t[...]
    sensor_h, sensor_l = split(sensor_f)
    sensor_s[0:r1, :] = sensor_h
    sensor_s[r1 : 2 * r1, :] = sensor_l
    gram_s = split(dot3((sensor_h, sensor_l), (sensor_h, sensor_l), NT))
    fit_acc[...] = jnp.zeros_like(fit_acc)
    chan_acc[...] = jnp.zeros_like(chan_acc)
    ggt[...] = jnp.zeros_like(ggt)

    def one(step, slot):
        ks = [step * wide + h for h in range(wide)]
        ct_rows = jnp.concatenate(
            [halves(ct[pl.ds(k, p.pairs, stride=p.times), :]) for k in ks], axis=0
        )
        ct_s = split(ct_rows)
        g = dot3(ct_s, chan_s)
        g_wide = jnp.concatenate([g[h * r1 : (h + 1) * r1] for h in range(wide)], axis=1)
        gw_s = split(g_wide)
        ggt[...] += dot3(gw_s, gw_s, NT)
        gt_h, gt_l = split(g.T)
        g_both = jnp.concatenate(
            [
                jnp.concatenate([gt_h[:, h * r1 : (h + 1) * r1], gt_l[:, h * r1 : (h + 1) * r1]], axis=1)
                for h in range(wide)
            ],
            axis=0,
        )
        g_high = jnp.concatenate([gt_h[:, h * r1 : (h + 1) * r1] for h in range(wide)], axis=0)
        for c in copies(step, slot):
            c.wait()
        folded = dot3(gram_s, gw_s)
        for i in range(0, p.sensors, tall):
            x_h, x_l = split(buf[slot, i : i + tall, :])
            f = dot(x_h, g_both)
            fit_acc[i : i + tall, :] += f[:, :r1] + f[:, r1:] + dot(x_l, g_high)
            a = dot(sensor_s[:, i : i + tall], x_h)
            folded = folded - (a[:r1] + a[r1:] + dot(sensor_s[0:r1, i : i + tall], x_l))
        f_rows = jnp.concatenate(
            [folded[:, h * p.chans : (h + 1) * p.chans] for h in range(wide)], axis=0
        )
        f_s = split(f_rows)
        inner = dot3(f_s, chan_rows_s)
        chan_acc[...] += dot3(ct_s, f_s, TN)
        for h, k in enumerate(ks):
            inner_ref[pl.ds(k, p.pairs, stride=p.times), :] = paired(inner[h * r1 : (h + 1) * r1])

    def outer(q, carry):
        for s in range(slots):
            step = q * slots + s
            one(step, s)

            @pl.when(step + slots < steps)
            def _():
                for c in copies(step + slots, s):
                    c.start()

        return carry

    lax.fori_loop(0, steps // slots, outer, 0)

    fit_acc[...] = (dot3(split(sensor_f), split(ggt[...]), TN) - fit_acc[...]) * p.fit_scale
    chan_acc[...] = chan_acc[...] * p.chan_scale
    time_sum = jnp.zeros((r3, p.times), f32)
    for ht, out in enumerate((keep, send)):
        half = lax.bitwise_xor(my_time, ht)
        for m in range(p.n_channel):
            quarter = lax.bitwise_xor(my_chan, m)
            base = m * p.chunk
            for rr in range(p.pairs_part):
                r = (half * p.n_channel + quarter) * p.pairs_part + rr
                rows = pl.ds(pl.multiple_of(r * p.times, p.times), p.times)
                inner_s = split(inner_ref[rows, :])
                out[base + rr * r3 : base + (rr + 1) * r3, :] = dot3(time_s, inner_s) * p.core_scale
                time_sum = time_sum + dot3(split(core_pair[r]), inner_s, NT)
            chunk = quarter * p.n_time + half
            start = pl.multiple_of(chunk * p.share, 16)
            fit = fit_acc[pl.ds(start, p.share), :]
            out[base + p.sum_rows : base + p.chunk, :] = paired(fit)
        chan_start = pl.multiple_of(half * p.chan_rows, 8)
        out[p.n_channel * p.chunk : p.rows, :] = chan_acc[pl.ds(chan_start, p.chan_rows), :]
    time_acc[...] = jnp.zeros_like(time_acc)
    time_acc[:, 0 : p.times] = time_sum * p.time_scale
    for m in range(p.n_channel):
        quarter = lax.bitwise_xor(my_chan, m)
        base = m * p.chunk + p.core_rows
        start = pl.multiple_of(quarter * p.time_rows, 8)
        keep[base : base + p.time_rows, :] = time_acc[pl.ds(start, p.time_rows), :]
        send[base : base + p.time_rows, :] = jnp.zeros((p.time_rows, LANES), f32)


def partials(p, place, tensor, core, sensor_t, chan_t, time_t):
    wide, slots = 4, 4
    tall = 256
    width = wide * p.chans
    out = jax.ShapeDtypeStruct((p.rows, LANES), f32)
    return pl.pallas_call(
        functools.partial(partial_kernel, p, wide, slots, tall),
        in_specs=[smem, anywhere, vmem, vmem, vmem, vmem],
        out_specs=[vmem, vmem],
        out_shape=[out, out],
        scratch_shapes=[
            pltpu.VMEM((slots, p.sensors, width), f32),
            pltpu.SemaphoreType.DMA((slots, wide)),
            pltpu.VMEM((p.pairs, p.r3, 2 * p.r2), f32),
            pltpu.VMEM((p.pairs * p.times, 2 * p.r2), f32),
            pltpu.VMEM((p.pairs * p.times, 2 * p.r2), f32),
            pltpu.VMEM((p.sensors, p.r1), f32),
            pltpu.VMEM((p.r2, p.chans), f32),
            pltpu.VMEM((p.r3, LANES), f32),
            pltpu.VMEM((p.r1, p.r1), f32),
            pltpu.VMEM((2 * p.r1, p.sensors), bf16),
        ],
        compiler_params=pltpu.CompilerParams(vmem_limit_bytes=56 * 2**20),
        cost_estimate=pl.CostEstimate(
            flops=12 * p.sensors * p.r1 * p.times * p.chans,
            bytes_accessed=4 * p.sensors * p.times * p.chans,
            transcendentals=0,
        ),
        name="partials",
    )(place, tensor, core, sensor_t, chan_t, time_t)


def graph_kernel(
    p, piece, slots,
    place, ids, edges, gathered, fit, out_t, weights, near, own, sem,
):
    block = edges.shape[-1]
    pieces = p.share // piece
    blocks = p.sensors // block
    first = place[2] * pieces

    def copies(g):
        at = first + g
        b = at // (block // piece)
        off = pl.multiple_of((at % (block // piece)) * piece, piece)
        moves = [pltpu.make_async_copy(edges.at[b, :, pl.ds(off, piece), :], weights.at[g], sem.at[g, 0])]
        for n in range(slots):
            other = ids[b, n]
            shard = lax.bitwise_xor(other // blocks, place[3])
            lanes = pl.ds(pl.multiple_of((other % blocks) * block, block), block)
            moves.append(
                pltpu.make_async_copy(gathered.at[shard, :, lanes], near.at[g, n], sem.at[g, 1 + n])
            )
        lanes = pl.ds(pl.multiple_of(b * block, block), block)
        moves.append(pltpu.make_async_copy(gathered.at[0, :, lanes], own.at[g], sem.at[g, 1 + slots]))
        return moves, off

    for g in range(pieces):
        for c in copies(g)[0]:
            c.start()
    parts = []
    for g in range(pieces):
        moves, off = copies(g)
        for c in moves:
            c.wait()
        pulled = jnp.zeros((piece, 2 * p.r1), f32)
        degree = jnp.zeros((piece, 1), f32)
        for n in range(slots):
            w = weights[g, n].astype(f32)
            degree = degree + jnp.sum(w, axis=1, keepdims=True)
            near_h, near_l = split(near[g, n])
            pulled = pulled + dot(w.astype(bf16), jnp.concatenate([near_h, near_l], axis=0), NT)
        near_rows = own[g].T
        rows = jnp.zeros((piece, p.r1), f32)
        for k in range(block // piece):
            rows = jnp.where(off == k * piece, near_rows[k * piece : (k + 1) * piece], rows)
        parts.append(lap_weight * (degree * rows - (pulled[:, : p.r1] + pulled[:, p.r1 :])))
    graph = jnp.concatenate(parts, axis=0)
    out_t[...] = (graph + halves(fit[...])).T


def graph_rows(p, place, ids, edges, gathered, fit):
    block = edges.shape[-1]
    slots = edges.shape[1]
    piece = math.gcd(p.share, block)
    pieces = p.share // piece
    return pl.pallas_call(
        functools.partial(graph_kernel, p, piece, slots),
        in_specs=[smem, smem, anywhere, anywhere, vmem],
        out_specs=vmem,
        out_shape=jax.ShapeDtypeStruct((p.r1, p.share), f32),
        scratch_shapes=[
            pltpu.VMEM((pieces, slots, piece, block), jnp.int32),
            pltpu.VMEM((pieces, slots, p.r1, block), f32),
            pltpu.VMEM((pieces, p.r1, block), f32),
            pltpu.SemaphoreType.DMA((pieces, 2 + slots)),
        ],
        compiler_params=pltpu.CompilerParams(vmem_limit_bytes=32 * 2**20),
        cost_estimate=pl.CostEstimate(flops=10**8, bytes_accessed=10**6, transcendentals=0),
        name="graph",
    )(place, ids, edges, gathered, fit)


def finish_kernel(p, place, *refs):
    own, others, far = refs[0], refs[1 : p.n_channel], refs[p.n_channel]
    core_out, chan_out, time_out = refs[p.n_channel + 1 :]
    my_time, my_chan = place[0], place[1]
    for ht in range(p.n_time):
        half = lax.bitwise_xor(my_time, ht)
        for m in range(p.n_channel):
            quarter = lax.bitwise_xor(my_chan, m)
            for rr in range(p.pairs_part):
                r = (half * p.n_channel + quarter) * p.pairs_part + rr
                if ht == 0:
                    rows = (own if m == 0 else others[m - 1])[rr * p.r3 : (rr + 1) * p.r3, :]
                else:
                    at = m * p.core_rows + rr * p.r3
                    rows = far[at : at + p.r3, :]
                core_out[r] = rows[:, : p.r2]
                core_out[r + p.pairs] = rows[:, p.r2 :]
            if ht == 0:
                rows = (own if m == 0 else others[m - 1])[p.core_rows : p.sum_rows, :]
                start = pl.multiple_of(quarter * p.time_rows, 8)
                time_out[pl.ds(start, p.time_rows), :] = rows[:, : p.times]
        start = pl.multiple_of(half * p.chan_rows, 8)
        if ht == 0:
            chan_out[pl.ds(start, p.chan_rows), :] = own[p.sum_rows : p.sum_rows + p.chan_rows, :]
        else:
            at = p.n_channel * p.core_rows
            chan_out[pl.ds(start, p.chan_rows), :] = far[at : at + p.chan_rows, :]


def finish(p, place, *arrays):
    return pl.pallas_call(
        functools.partial(finish_kernel, p),
        in_specs=[smem] + [vmem] * len(arrays),
        out_specs=[vmem] * 3,
        out_shape=[
            jax.ShapeDtypeStruct((p.r1, p.r3, p.r2), f32),
            jax.ShapeDtypeStruct((p.r2, p.chans), f32),
            jax.ShapeDtypeStruct((p.r3, p.times), f32),
        ],
        compiler_params=pltpu.CompilerParams(vmem_limit_bytes=32 * 2**20),
        cost_estimate=pl.CostEstimate(flops=10**6, bytes_accessed=2 * 10**6, transcendentals=0),
        name="finish",
    )(place, *arrays)


def swap(x, axis, size, mask):
    return lax.ppermute(x, axis, [(i, i ^ mask) for i in range(size)])


def on_device(
    tensor, core, sensor_factor, channel_factor, time_factor, neighbour_ids, edge_weights
):
    n_sensor = lax.axis_size("sensor")
    n_channel = lax.axis_size("channel")
    n_time = lax.axis_size("tm")
    p = Plan(tensor.shape, core.shape, n_sensor, n_channel, n_time)
    my_time, my_chan, my_sensor = (lax.axis_index(a) for a in ("tm", "channel", "sensor"))
    place = jnp.stack([my_time, my_chan, my_chan * n_time + my_time, my_sensor]).astype(jnp.int32)

    gathered = sensor_factor.T[None]
    mask = 1
    while mask < n_sensor:
        gathered = jnp.concatenate([gathered, swap(gathered, "sensor", n_sensor, mask)], axis=0)
        mask *= 2

    keep, send = partials(
        p, place, tensor, core.transpose(0, 2, 1), sensor_factor.T, channel_factor.T, time_factor.T
    )
    held = keep + swap(send, "tm", n_time, 1)
    total = held[: p.chunk]
    for m in range(1, n_channel):
        total = total + swap(held[m * p.chunk : (m + 1) * p.chunk], "channel", n_channel, m)
    fit = total[p.sum_rows :]
    total = jnp.concatenate([total[: p.sum_rows], held[n_channel * p.chunk :]], axis=0)
    mask = 1
    while mask < n_sensor:
        total = total + swap(total, "sensor", n_sensor, mask)
        mask *= 2
    others = [
        swap(total[: p.sum_rows], "channel", n_channel, m) for m in range(1, n_channel)
    ]
    near = jnp.concatenate(
        [total[: p.core_rows]] + [o[: p.core_rows] for o in others] + [total[p.sum_rows :]], axis=0
    )
    far = swap(near, "tm", n_time, 1)
    core_t, chan_t, time_t = finish(p, place, total, *others, far)
    sensor_t = graph_rows(p, place, neighbour_ids, edge_weights, gathered, fit)
    return (core_t.transpose(0, 2, 1), sensor_t.T, chan_t.T, time_t.T)


def solution(mesh):
    return jax.shard_map(
        on_device,
        mesh=mesh,
        in_specs=(
            P("sensor", "tm", "channel"),
            P(),
            P("sensor", None),
            P("channel", None),
            P("tm", None),
            P("sensor", None),
            P("sensor", None, None, None),
        ),
        out_specs=(P(), P(("sensor", "channel", "tm"), None), P("channel", None), P("tm", None)),
        check_vma=False,
    )
```

time: 276 us -> 80.8 us (0.29); the launches traced: 271 us -> 79.2 us
  blocking collectives: 122 us -> 0 us
  matrix products: 95.6 us -> 0 us
  Pallas kernels: 0 us -> 35.2 us
  local copies, waits for them, and re-layouts: 33.9 us -> 3.29 us
  waiting for transfers between devices: 0.04 us -> 21.5 us
  starting transfers between devices: 0.08 us -> 16.6 us
  between operations: 15.6 us -> 0.76 us
    psum x2 -> x0, blocking collectives: 102 us -> none  [the longest x1 63 us: on_device(): time_grad = lax.psum(time_part, ('sensor', 'channel'))]
    dot_general x11 -> x0, matrix products: 95.6 us -> none  [the longest x1 27.7 us: on_device(): folded = jnp.dot(sensor_factor.T, residual, precision=highest)]
    pallas_call x0 -> x3, Pallas kernels: none -> 35.2 us  [the longest x1 30.8 us: partials(): pl.pallas_call(functools.partial(partial_kernel, p, wide, slots, tall), i...]
    unnamed x19 -> x13, local copies, waits for them, and re-layouts: 29.4 us -> 2.65 us
    ppermute x0 -> x12, waiting for transfers between devices: none -> 21.5 us  [swap(): return lax.ppermute(x, axis, [(i, i ^ mask) for i in range(size)])]
    all_gather x1 -> x0, blocking collectives: 20.2 us -> none  [on_device(): whole_rows = lax.all_gather(sensor_factor, 'sensor', axis=0, tiled=True)]
    ppermute x0 -> x12, starting transfers between devices: none -> 16.6 us  [swap(): return lax.ppermute(x, axis, [(i, i ^ mask) for i in range(size)])]
  transfers between devices with their start and end apart: 2 -> 12, of which waited for: 0 -> 8; matrix products, arithmetic and copies ran while one was open for 20% -> 4% of each run, Pallas kernels for 0% -> 3%
where the time goes in v1:
time: 80.8 us; the launch traced here: 79.2 us
  Pallas kernels  35.2 us (44%)
  waiting for transfers between devices  21.5 us (27%)
  starting transfers between devices  16.6 us (21%)
  local copies, waits for them, and re-layouts  3.29 us (4%)
  other arithmetic  1.8 us (2%)
    pallas_call x1, Pallas kernels, partials(): pl.pallas_call(functools.partial(partial_kernel, p, wide, slots, tall), i...  30.8 us
    ppermute x12, waiting for transfers between devices, swap(): return lax.ppermute(x, axis, [(i, i ^ mask) for i in range(size)])  21.5 us
    ppermute x12, starting transfers between devices, swap(): return lax.ppermute(x, axis, [(i, i ^ mask) for i in range(size)])  16.6 us
    pallas_call x1, Pallas kernels, graph_rows(): pl.pallas_call(functools.partial(graph_kernel, p, piece, slots), in_specs...  2.71 us
    unnamed x13, local copies, waits for them, and re-layouts  2.65 us
    pallas_call x1, Pallas kernels, finish(): pl.pallas_call(functools.partial(finish_kernel, p), in_specs=[smem] + [vm...  1.72 us
  transfers between devices with their start and end apart: 12, of which 8 were waited for; matrix products, arithmetic and copies ran while one was open for 4% of the time, Pallas kernels for 3%

profile of v1, /device:TPU:1, one launch (start us, length us, event | category | flops | bytes accessed | tf_op | source)
XLA Modules:
  0.0 79.2 jit_solution(16056643322335812184)
XLA Ops:
  0.7 0.6 pad_add_fusion.place
  1.3 30.8 %partials.1 = (f32[768,128]{1,0:T(8,128)}, f32[768,128]{1,0:T(8,128)}) custom-call(s32[4]{0:T(128)} %pad_add_fusion.place, f32[768,64,128]{2,1,0:T(8,128)} %x_hbm.1, f32[64,32,64]{2,1,0:T(8,128)} %bitcast.18, f32[64,768]{1,0:T(8,128)} %bitcast.14, f32[64,128]{1,0:T(8,128)} %bitcast.19, f32[32,64]{1,0:T(8,128)} %bitcast.21), custom_call_target="tpu_custom_call" | custom-call | flops 4831838208 | bytes 25165824 | tf_op jit(solution)/shard_map/partials/pallas_call | solution.py:195
  32.0 0.1 collective-permute-start
  32.2 1.9 %collective-permute-done = f32[768,128]{1,0:T(8,128)S(1)} collective-permute-done((f32[768,128]{1,0:T(8,128)}, f32[768,128]{1,0:T(8,128)S(1)}, u32[]{:S(2)}, u32[]{:S(2)}) %collective-permute-start) | collective-permute-done | bytes 393248 | tf_op jit(solution)/shard_map/ppermute | solution.py:339
  34.0 1.1 %add.22 = f32[768,128]{1,0:T(8,128)S(1)} add(f32[768,128]{1,0:T(8,128)} %get-tuple-element.9, f32[768,128]{1,0:T(8,128)S(1)} %collective-permute-done) | non-fusion elementwise | flops 98304 | bytes 1179648 | tf_op jit(solution)/shard_map/add | solution.py:361
  35.1 2.4 %collective-permute-start.1 = (f32[184,128]{1,0:T(8,128)S(1)}, f32[184,128]{1,0:T(8,128)S(1)}, u32[]{:S(2)}, u32[]{:S(2)}) collective-permute-start(f32[184,128]{1,0:T(8,128)S(1)} %get-tuple-element.14), channel_id=1, source_target_pairs={{0,2},{2,0},{4,6},{6,4},{1,3},{3,1},{5,7},{7,5},{8,10},{10,8},{12,... | collective-permute-start | bytes 282632 | tf_op jit(solution)/shard_map/ppermute | solution.py:339
  37.5 1.2 %collective-permute-start.3 = (f32[184,128]{1,0:T(8,128)S(1)}, f32[184,128]{1,0:T(8,128)S(1)}, u32[]{:S(2)}, u32[]{:S(2)}) collective-permute-start(f32[184,128]{1,0:T(8,128)S(1)} %get-tuple-element.15), channel_id=1, source_target_pairs={{0,6},{2,4},{4,2},{6,0},{1,7},{3,5},{5,3},{7,1},{8,14},{10,12},{12... | collective-permute-start | bytes 282632 | tf_op jit(solution)/shard_map/ppermute | solution.py:339
  38.7 0.1 collective-permute-start.2
  38.8 1.5 %collective-permute-done.1 = f32[184,128]{1,0:T(8,128)S(1)} collective-permute-done((f32[184,128]{1,0:T(8,128)S(1)}, f32[184,128]{1,0:T(8,128)S(1)}, u32[]{:S(2)}, u32[]{:S(2)}) %collective-permute-start.1) | collective-permute-done | bytes 94240 | tf_op jit(solution)/shard_map/ppermute | solution.py:339
  40.3 2.9 %collective-permute-done.3 = f32[184,128]{1,0:T(8,128)S(1)} collective-permute-done((f32[184,128]{1,0:T(8,128)S(1)}, f32[184,128]{1,0:T(8,128)S(1)}, u32[]{:S(2)}, u32[]{:S(2)}) %collective-permute-start.3) | collective-permute-done | bytes 94240 | tf_op jit(solution)/shard_map/ppermute | solution.py:339
  43.2 1.4 %collective-permute-done.2 = f32[184,128]{1,0:T(8,128)S(1)} collective-permute-done((f32[184,128]{1,0:T(8,128)S(1)}, f32[184,128]{1,0:T(8,128)S(1)}, u32[]{:S(2)}, u32[]{:S(2)}) %collective-permute-start.2) | collective-permute-done | bytes 94240 | tf_op jit(solution)/shard_map/ppermute | solution.py:339
  44.7 1.4 %collective-permute-start.4 = (f32[168,128]{1,0:T(8,128)S(1)}, f32[168,128]{1,0:T(8,128)S(1)}, u32[]{:S(2)}, u32[]{:S(2)}) collective-permute-start(f32[168,128]{1,0:T(8,128)S(1)} %pad_maximum_fusion.2), channel_id=1, source_target_pairs={{0,8},{8,0},{16,24},{24,16},{1,9},{9,1},{17,25},{25,17},{2,10},{10... | collective-permute-start | bytes 258056 | tf_op jit(solution)/shard_map/ppermute | solution.py:339
  46.0 0.2 collective-permute-start.10
  46.2 1.9 %collective-permute-done.4 = f32[168,128]{1,0:T(8,128)S(1)} collective-permute-done((f32[168,128]{1,0:T(8,128)S(1)}, f32[168,128]{1,0:T(8,128)S(1)}, u32[]{:S(2)}, u32[]{:S(2)}) %collective-permute-start.4) | collective-permute-done | bytes 86048 | tf_op jit(solution)/shard_map/ppermute | solution.py:339
  48.1 2.4 %collective-permute-start.5 = (f32[168,128]{1,0:T(8,128)S(1)}, f32[168,128]{1,0:T(8,128)S(1)}, u32[]{:S(2)}, u32[]{:S(2)}) collective-permute-start(f32[168,128]{1,0:T(8,128)S(1)} %fusion.2), channel_id=1, source_target_pairs={{0,16},{8,24},{16,0},{24,8},{1,17},{9,25},{17,1},{25,9},{2,18},{10... | collective-permute-start | bytes 258056 | tf_op jit(solution)/shard_map/ppermute | solution.py:339
  50.5 3.1 %collective-permute-done.10 = f32[1,64,768]{2,1,0:T(8,128)S(1)} collective-permute-done((f32[1,64,768]{2,1,0:T(8,128)S(1)}, f32[1,64,768]{2,1,0:T(8,128)S(1)}, u32[]{:S(2)}, u32[]{:S(2)}) %collective-permute-start.10) | collective-permute-done | bytes 196640 | tf_op jit(solution)/shard_map/ppermute | solution.py:339
  53.6 1.5 %collective-permute-start.11 = (f32[2,64,768]{2,1,0:T(8,128)S(1)}, f32[2,64,768]{2,1,0:T(8,128)S(1)}, u32[]{:S(2)}, u32[]{:S(2)}) collective-permute-start(f32[2,64,768]{2,1,0:T(8,128)S(1)} %pad_maximum_fusion.1), channel_id=1, source_target_pairs={{0,16},{8,24},{16,0},{24,8},{1,17},{9,25},{17,1},{25,9},{2,18},{10... | collective-permute-start | bytes 1179656 | tf_op jit(solution)/shard_map/ppermute | solution.py:339
  55.1 1.2 %collective-permute-start.8 = (f32[136,128]{1,0:T(8,128)S(1)}, f32[136,128]{1,0:T(8,128)S(1)}, u32[]{:S(2)}, u32[]{:S(2)}) collective-permute-start(f32[136,128]{1,0:T(8,128)S(1)} %slice.60), channel_id=1, source_target_pairs={{0,6},{2,4},{4,2},{6,0},{1,7},{3,5},{5,3},{7,1},{8,14},{10,12},{12... | collective-permute-start | bytes 208904 | tf_op jit(solution)/shard_map/ppermute | solution.py:339
  56.3 1.2 %collective-permute-start.7 = (f32[136,128]{1,0:T(8,128)S(1)}, f32[136,128]{1,0:T(8,128)S(1)}, u32[]{:S(2)}, u32[]{:S(2)}) collective-permute-start(f32[136,128]{1,0:T(8,128)S(1)} %slice.60), channel_id=1, source_target_pairs={{0,4},{2,6},{4,0},{6,2},{1,5},{3,7},{5,1},{7,3},{8,12},{10,14},{12... | collective-permute-start | bytes 208904 | tf_op jit(solution)/shard_map/ppermute | solution.py:339
  57.5 0.3 collective-permute-start.6
  57.8 0.6 slice_dynamic-update-slice_fusion.3
  58.4 2.3 %collective-permute-done.6.refs_1_ = f32[136,128]{1,0:T(8,128)S(1)} collective-permute-done((f32[136,128]{1,0:T(8,128)S(1)}, f32[136,128]{1,0:T(8,128)S(1)}, u32[]{:S(2)}, u32[]{:S(2)}) %collective-permute-start.6) | collective-permute-done | bytes 69664 | tf_op jit(solution)/shard_map/ppermute | solution.py:339
  60.7 0.6 slice_dynamic-update-slice_fusion.2
  61.3 0.6 slice_dynamic-update-slice_fusion.1
  62.0 0.6 slice_dynamic-update-slice_fusion
  62.6 0.6 slice_dynamic-update-slice_fusion.4
  63.2 4.8 %collective-permute-start.9 = (f32[544,128]{1,0:T(8,128)}, f32[544,128]{1,0:T(8,128)S(1)}, u32[]{:S(2)}, u32[]{:S(2)}) collective-permute-start(f32[544,128]{1,0:T(8,128)} %slice_dynamic-update-slice_fusion.4), channel_id=1, source_target_pairs={{0,1},{1,0},{2,3},{3,2},{4,5},{5,4},{6,7},{7,6},{8,9},{9,8},{10,11... | collective-permute-start | bytes 835592 | tf_op jit(solution)/shard_map/ppermute | solution.py:339
  68.0 0.1 copy.11.ids
  68.1 6.6 %collective-permute-done.11 = f32[2,64,768]{2,1,0:T(8,128)S(1)} collective-permute-done((f32[2,64,768]{2,1,0:T(8,128)S(1)}, f32[2,64,768]{2,1,0:T(8,128)S(1)}, u32[]{:S(2)}, u32[]{:S(2)}) %collective-permute-start.11) | collective-permute-done | bytes 393248 | tf_op jit(solution)/shard_map/ppermute | solution.py:339
  74.6 0.1 pad_maximum_fusion.gathered
  74.7 2.7 %graph.1 = f32[64,96]{1,0:T(8,128)} custom-call(s32[4]{0:T(128)S(1)} %copy-done.1, s32[6,4]{1,0:T(8,128)S(1)} %copy.11.ids, s32[6,4,128,128]{3,2,1,0:T(8,128)S(1)} %copy-done, f32[4,64,768]{2,1,0:T(8,128)S(1)} %pad_maximum_fusion.gathered, f32[48,128]{1,0:T(8,128)S(1)} %slice.66.fit), custom_call_target="tpu_custom_call" | custom-call | flops 100000000 | bytes 1000000 | tf_op jit(solution)/shard_map/graph/pallas_call | solution.py:276
  77.4 1.7 %finish.1 = (f32[64,32,64]{2,1,0:T(8,128)}, f32[64,128]{1,0:T(8,128)}, f32[32,64]{1,0:T(8,128)}) custom-call(s32[4]{0:T(128)S(1)} %copy-done.1, f32[168,128]{1,0:T(8,128)S(1)} %add.27.refs_0_, f32[136,128]{1,0:T(8,128)S(1)} %collective-permute-done.6.refs_1_, f32[136,128]{1,0:T(8,128)S(1)} %collective-permute-done.7.refs_2_, ...), custom_call_target="tpu_custom_call" | custom-call | flops 1000000 | bytes 2000000 | tf_op jit(solution)/shard_map/finish/pallas_call | solution.py:323
  (22 shorter events, 0.2 us)
Async XLA Ops:
  0.6 45.4 %copy-start.2 = (f32[768,64]{0,1:T(8,128)S(1)}, f32[768,64]{0,1:T(8,128)}, u32[]{:S(2)}) copy-start(f32[768,64]{0,1:T(8,128)} %param.9) | copy-start | bytes 589828
  0.6 67.3 %copy-start.3 = (s32[6,4]{0,1:T(4,128)S(1)}, s32[6,4]{0,1:T(4,128)}, u32[]{:S(2)}) copy-start(s32[6,4]{0,1:T(4,128)} %param.12) | copy-start | bytes 292
  0.7 74.0 %copy-start = (s32[6,4,128,128]{3,2,1,0:T(8,128)S(1)}, s32[6,4,128,128]{3,2,1,0:T(8,128)}, u32[]{:S(2)}) copy-start(s32[6,4,128,128]{3,2,1,0:T(8,128)} %edges.1) | copy-start | bytes 4718596
  1.3 73.4 %copy-start.1 = (s32[4]{0:T(128)S(1)}, s32[4]{0:T(128)}, u32[]{:S(2)}) copy-start(s32[4]{0:T(128)} %pad_add_fusion.place) | copy-start | bytes 52
  32.0 2.0 %collective-permute-start = (f32[768,128]{1,0:T(8,128)}, f32[768,128]{1,0:T(8,128)S(1)}, u32[]{:S(2)}, u32[]{:S(2)}) collective-permute-start(f32[768,128]{1,0:T(8,128)} %get-tuple-element.10), channel_id=1, source_target_pairs={{0,1},{1,0},{2,3},{3,2},{4,5},{5,4},{6,7},{7,6},{8,9},{9,8},{10,11... | collective-permute-start | bytes 1179656 | tf_op jit(solution)/shard_map/ppermute | solution.py:339
  35.1 5.2 %collective-permute-start.1 = (f32[184,128]{1,0:T(8,128)S(1)}, f32[184,128]{1,0:T(8,128)S(1)}, u32[]{:S(2)}, u32[]{:S(2)}) collective-permute-start(f32[184,128]{1,0:T(8,128)S(1)} %get-tuple-element.14), channel_id=1, source_target_pairs={{0,2},{2,0},{4,6},{6,4},{1,3},{3,1},{5,7},{7,5},{8,10},{10,8},{12,... | collective-permute-start | bytes 282632 | tf_op jit(solution)/shard_map/ppermute | solution.py:339
  37.5 5.7 %collective-permute-start.3 = (f32[184,128]{1,0:T(8,128)S(1)}, f32[184,128]{1,0:T(8,128)S(1)}, u32[]{:S(2)}, u32[]{:S(2)}) collective-permute-start(f32[184,128]{1,0:T(8,128)S(1)} %get-tuple-element.15), channel_id=1, source_target_pairs={{0,6},{2,4},{4,2},{6,0},{1,7},{3,5},{5,3},{7,1},{8,14},{10,12},{12... | collective-permute-start | bytes 282632 | tf_op jit(solution)/shard_map/ppermute | solution.py:339
  38.7 5.9 %collective-permute-start.2 = (f32[184,128]{1,0:T(8,128)S(1)}, f32[184,128]{1,0:T(8,128)S(1)}, u32[]{:S(2)}, u32[]{:S(2)}) collective-permute-start(f32[184,128]{1,0:T(8,128)S(1)} %get-tuple-element.16), channel_id=1, source_target_pairs={{0,4},{2,6},{4,0},{6,2},{1,5},{3,7},{5,1},{7,3},{8,12},{10,14},{12... | collective-permute-start | bytes 282632 | tf_op jit(solution)/shard_map/ppermute | solution.py:339
  44.7 3.4 %collective-permute-start.4 = (f32[168,128]{1,0:T(8,128)S(1)}, f32[168,128]{1,0:T(8,128)S(1)}, u32[]{:S(2)}, u32[]{:S(2)}) collective-permute-start(f32[168,128]{1,0:T(8,128)S(1)} %pad_maximum_fusion.2), channel_id=1, source_target_pairs={{0,8},{8,0},{16,24},{24,16},{1,9},{9,1},{17,25},{25,17},{2,10},{10... | collective-permute-start | bytes 258056 | tf_op jit(solution)/shard_map/ppermute | solution.py:339
  46.0 7.5 %collective-permute-start.10 = (f32[1,64,768]{2,1,0:T(8,128)S(1)}, f32[1,64,768]{2,1,0:T(8,128)S(1)}, u32[]{:S(2)}, u32[]{:S(2)}) collective-permute-start(f32[1,64,768]{2,1,0:T(8,128)S(1)} %bitcast.15), channel_id=1, source_target_pairs={{0,8},{8,0},{16,24},{24,16},{1,9},{9,1},{17,25},{25,17},{2,10},{10... | collective-permute-start | bytes 589832 | tf_op jit(solution)/shard_map/ppermute | solution.py:339
  48.1 7.0 %collective-permute-start.5 = (f32[168,128]{1,0:T(8,128)S(1)}, f32[168,128]{1,0:T(8,128)S(1)}, u32[]{:S(2)}, u32[]{:S(2)}) collective-permute-start(f32[168,128]{1,0:T(8,128)S(1)} %fusion.2), channel_id=1, source_target_pairs={{0,16},{8,24},{16,0},{24,8},{1,17},{9,25},{17,1},{25,9},{2,18},{10... | collective-permute-start | bytes 258056 | tf_op jit(solution)/shard_map/ppermute | solution.py:339
  53.6 21.1 %collective-permute-start.11 = (f32[2,64,768]{2,1,0:T(8,128)S(1)}, f32[2,64,768]{2,1,0:T(8,128)S(1)}, u32[]{:S(2)}, u32[]{:S(2)}) collective-permute-start(f32[2,64,768]{2,1,0:T(8,128)S(1)} %pad_maximum_fusion.1), channel_id=1, source_target_pairs={{0,16},{8,24},{16,0},{24,8},{1,17},{9,25},{17,1},{25,9},{2,18},{10... | collective-permute-start | bytes 1179656 | tf_op jit(solution)/shard_map/ppermute | solution.py:339
  55.1 6.9 %collective-permute-start.8 = (f32[136,128]{1,0:T(8,128)S(1)}, f32[136,128]{1,0:T(8,128)S(1)}, u32[]{:S(2)}, u32[]{:S(2)}) collective-permute-start(f32[136,128]{1,0:T(8,128)S(1)} %slice.60), channel_id=1, source_target_pairs={{0,6},{2,4},{4,2},{6,0},{1,7},{3,5},{5,3},{7,1},{8,14},{10,12},{12... | collective-permute-start | bytes 208904 | tf_op jit(solution)/shard_map/ppermute | solution.py:339
  56.3 5.0 %collective-permute-start.7 = (f32[136,128]{1,0:T(8,128)S(1)}, f32[136,128]{1,0:T(8,128)S(1)}, u32[]{:S(2)}, u32[]{:S(2)}) collective-permute-start(f32[136,128]{1,0:T(8,128)S(1)} %slice.60), channel_id=1, source_target_pairs={{0,4},{2,6},{4,0},{6,2},{1,5},{3,7},{5,1},{7,3},{8,12},{10,14},{12... | collective-permute-start | bytes 208904 | tf_op jit(solution)/shard_map/ppermute | solution.py:339
  57.5 3.2 %collective-permute-start.6 = (f32[136,128]{1,0:T(8,128)S(1)}, f32[136,128]{1,0:T(8,128)S(1)}, u32[]{:S(2)}, u32[]{:S(2)}) collective-permute-start(f32[136,128]{1,0:T(8,128)S(1)} %slice.60), channel_id=1, source_target_pairs={{0,2},{2,0},{4,6},{6,4},{1,3},{3,1},{5,7},{7,5},{8,10},{10,8},{12,... | collective-permute-start | bytes 208904 | tf_op jit(solution)/shard_map/ppermute | solution.py:339
  63.2 14.2 %collective-permute-start.9 = (f32[544,128]{1,0:T(8,128)}, f32[544,128]{1,0:T(8,128)S(1)}, u32[]{:S(2)}, u32[]{:S(2)}) collective-permute-start(f32[544,128]{1,0:T(8,128)} %slice_dynamic-update-slice_fusion.4), channel_id=1, source_target_pairs={{0,1},{1,0},{2,3},{3,2},{4,5},{5,4},{6,7},{7,6},{8,9},{9,8},{10,11... | collective-permute-start | bytes 835592 | tf_op jit(solution)/shard_map/ppermute | solution.py:339

commit v2 on v1

v2 whole, which is shorter than its diff:
```python
import functools
import math

import jax
import jax.numpy as jnp
from jax import lax
from jax.experimental import pallas as pl
from jax.experimental.pallas import tpu as pltpu
from jax.sharding import PartitionSpec as P

lap_weight = 1.0 / 512.0
f32, bf16 = jnp.float32, jnp.bfloat16
NN = (((1,), (0,)), ((), ()))
NT = (((1,), (1,)), ((), ()))
TN = (((0,), (0,)), ((), ()))
LANES = 128
LAG = False
vmem = pl.BlockSpec(memory_space=pltpu.VMEM)
smem = pl.BlockSpec(memory_space=pltpu.SMEM)
anywhere = pl.BlockSpec(memory_space=pl.ANY)


def split(x):
    high = x.astype(bf16)
    return high, (x - high.astype(f32)).astype(bf16)


def dot(a, b, dims=NN):
    return lax.dot_general(a, b, dims, preferred_element_type=f32)


def dot3(a, b, dims=NN):
    return dot(a[0], b[0], dims) + (dot(a[0], b[1], dims) + dot(a[1], b[0], dims))


def halves(x):
    w = x.shape[1] // 2
    return jnp.concatenate([x[:, :w], x[:, w:]], axis=0)


def paired(x):
    n = x.shape[0] // 2
    return jnp.concatenate([x[:n], x[n:]], axis=1)


class Plan:
    def __init__(self, tensor, core, n_sensor, n_channel, n_time):
        self.sensors, self.times, self.chans = tensor
        self.r1, self.r2, self.r3 = core
        self.n_sensor, self.n_channel, self.n_time = n_sensor, n_channel, n_time
        self.parts = n_channel * n_time
        self.pairs = self.r1 // 2
        self.pairs_part = self.pairs // self.parts
        self.core_rows = self.pairs_part * self.r3
        self.time_rows = self.r3 // n_channel
        self.share = self.sensors // self.parts
        self.fit_rows = self.share // 2
        self.chunk = self.core_rows + self.time_rows + self.fit_rows
        self.sum_rows = self.core_rows + self.time_rows
        self.chan_rows = self.r2 // n_time
        self.rows = n_channel * self.chunk + self.chan_rows
        total = (self.sensors * n_sensor, self.times * n_time, self.chans * n_channel)
        self.core_scale = 1.0 / math.sqrt(total[0] * total[1] * total[2])
        self.chan_scale = 1.0 / math.sqrt(total[0] * total[1])
        self.time_scale = 1.0 / math.sqrt(total[0] * total[2])
        self.fit_scale = 1.0 / math.sqrt(total[1] * total[2])


def both(x):
    zero = jnp.zeros_like(x)
    return jnp.concatenate(
        [jnp.concatenate([x, zero], axis=1), jnp.concatenate([zero, x], axis=1)], axis=0
    )


def partial_kernel(
    p, group, wide, slots, tall,
    x_hbm, core, sensor_t, chan_t, time_t, keep, send,
    buf, sem, core_pair, ct, inner_ref, fit_acc, chan_acc, time_acc, sensor_s,
    fold, g_both, g_parts,
):
    r1, r2, r3 = p.r1, p.r2, p.r3
    width = wide * p.chans
    steps = p.times // wide
    groups = p.times // group
    inside = group // wide
    my_time, my_chan = lax.axis_index("tm"), lax.axis_index("channel")

    def copies(at, slot):
        return [
            pltpu.make_async_copy(
                x_hbm.at[:, at * group + h, :],
                buf.at[slot, :, h * p.chans : (h + 1) * p.chans],
                sem.at[slot, h],
            )
            for h in range(group)
        ]

    for s in range(slots):
        for c in copies(s, s):
            c.start()

    time_s = split(time_t[...])
    for r in range(p.pairs):
        pair = jnp.concatenate([core[r], core[r + p.pairs]], axis=1)
        pair_h, pair_l = split(pair)
        core_pair[r] = jnp.concatenate([pair_h, pair_l, pair_h], axis=1)
        ct[r * p.times : (r + 1) * p.times, :] = dot3(time_s, (pair_h, pair_l), TN)
    chan_h, chan_l = split(both(chan_t[...]))
    chan_twice = jnp.concatenate([chan_h, chan_h], axis=0)
    rows_h, rows_l = split(both(chan_t[...].T))
    rows_parts = jnp.concatenate([rows_h, rows_l], axis=1)
    sensor_f = sensor_t[...]
    sensor_h, sensor_l = split(sensor_f)
    sensor_s[0:r1, :] = sensor_h
    sensor_s[r1 : 2 * r1, :] = sensor_l
    gram_h, gram_l = split(dot3((sensor_h, sensor_l), (sensor_h, sensor_l), NT))
    gram_twice = jnp.concatenate([gram_h, gram_h], axis=1)
    fit_acc[...] = jnp.zeros_like(fit_acc)

    def ct_rows(step):
        at = [ct[pl.ds(step * wide + h, p.pairs, stride=p.times), :] for h in range(wide)]
        return split(jnp.concatenate(at, axis=0))

    def before(step):
        ct_h, ct_l = ct_rows(step)
        g = dot(jnp.concatenate([ct_h, ct_l], axis=1), chan_twice) + dot(ct_h, chan_l)
        g_h, g_l = split(
            jnp.concatenate(
                [halves(g[h * p.pairs : (h + 1) * p.pairs]) for h in range(wide)], axis=1
            )
        )
        g_hl = jnp.concatenate([g_h, g_l], axis=0)
        g_parts[:, step * width : (step + 1) * width] = g_hl
        for h in range(wide):
            at = slice(h * p.chans, (h + 1) * p.chans)
            g_both[step, at, :] = g_hl[:, at].T

    def read(step, slot):
        lanes = slice(step % inside * width, (step % inside + 1) * width)
        g_hl = g_parts[:, step * width : (step + 1) * width]
        folded = dot(gram_twice, g_hl) + dot(gram_l, g_hl[:r1])
        g = g_both[step]
        for i in range(0, p.sensors, tall):
            x_h, x_l = split(buf[slot, i : i + tall, lanes])
            fit_acc[i : i + tall, :] += dot(x_h, g) + dot(x_l, g)
            a = dot(sensor_s[:, i : i + tall], x_h)
            folded = folded - (a[:r1] + a[r1:] + dot(sensor_s[0:r1, i : i + tall], x_l))
        fold[step] = folded

    def after(step, chan_sum):
        folded = fold[step]
        rows = jnp.concatenate(
            [paired(folded[:, h * p.chans : (h + 1) * p.chans]) for h in range(wide)], axis=0
        )
        f_h, f_l = split(rows)
        inner = dot(f_h, rows_parts)
        inner = inner[:, : 2 * r2] + inner[:, 2 * r2 :] + dot(f_l, rows_h)
        for h in range(wide):
            inner_ref[pl.ds(step * wide + h, p.pairs, stride=p.times), :] = inner[h * p.pairs : (h + 1) * p.pairs]
        return chan_sum + dot3(ct_rows(step), (f_h, f_l), TN)

    for step in range(steps):
        before(step)
    chan_sum = jnp.zeros((2 * r2, 2 * p.chans), f32)
    for at in range(groups):
        slot = at % slots
        for c in copies(at, slot):
            c.wait()
        for step in range(at * inside, (at + 1) * inside):
            read(step, slot)
        if at + slots < groups:
            for c in copies(at + slots, slot):
                c.start()
        if LAG and at >= 1:
            for step in range((at - 1) * inside, at * inside):
                chan_sum = after(step, chan_sum)
    for step in range((groups - 1) * inside if LAG else 0, steps):
        chan_sum = after(step, chan_sum)

    ggt = dot(g_parts[...], g_parts[...], NT)
    ggt = ggt[:r1, :r1] + ggt[:r1, r1:] + ggt[r1:, :r1]
    rebuilt = dot3((sensor_h, sensor_l), split(ggt), TN)
    fit_acc[:, :r1] = (rebuilt - (fit_acc[:, :r1] + fit_acc[:, r1:])) * p.fit_scale
    chan_acc[...] = (chan_sum[:r2, : p.chans] + chan_sum[r2:, p.chans :]) * p.chan_scale
    time_h, time_l = time_s
    time_parts = jnp.concatenate([time_h, time_l, time_h], axis=1)
    time_sum = jnp.zeros((r3, p.times), f32)
    for ht, out in enumerate((keep, send)):
        half = lax.bitwise_xor(my_time, ht)
        for m in range(p.n_channel):
            quarter = lax.bitwise_xor(my_chan, m)
            base = m * p.chunk
            for rr in range(p.pairs_part):
                r = (half * p.n_channel + quarter) * p.pairs_part + rr
                rows = pl.ds(pl.multiple_of(r * p.times, p.times), p.times)
                in_h, in_l = split(inner_ref[rows, :])
                out[base + rr * r3 : base + (rr + 1) * r3, :] = (
                    dot(time_parts, jnp.concatenate([in_h, in_h, in_l], axis=0)) * p.core_scale
                )
                time_sum = time_sum + dot(core_pair[r], jnp.concatenate([in_h, in_h, in_l], axis=1), NT)
            chunk = quarter * p.n_time + half
            start = pl.multiple_of(chunk * p.share, 16)
            fit = fit_acc[pl.ds(start, p.share), 0:r1]
            out[base + p.sum_rows : base + p.chunk, :] = paired(fit)
        chan_start = pl.multiple_of(half * p.chan_rows, 8)
        out[p.n_channel * p.chunk : p.rows, :] = chan_acc[pl.ds(chan_start, p.chan_rows), :]
    time_acc[...] = jnp.zeros_like(time_acc)
    time_acc[:, 0 : p.times] = time_sum * p.time_scale
    for m in range(p.n_channel):
        quarter = lax.bitwise_xor(my_chan, m)
        base = m * p.chunk + p.core_rows
        start = pl.multiple_of(quarter * p.time_rows, 8)
        keep[base : base + p.time_rows, :] = time_acc[pl.ds(start, p.time_rows), :]
        send[base : base + p.time_rows, :] = jnp.zeros((p.time_rows, LANES), f32)


def partials(p, tensor, core, sensor_t, chan_t, time_t):
    group, wide, tall = 16, 4, 256
    slots = max(2, min(p.times // group, 2**25 // (4 * p.sensors * group * p.chans)))
    width = wide * p.chans
    out = jax.ShapeDtypeStruct((p.rows, LANES), f32)
    return pl.pallas_call(
        functools.partial(partial_kernel, p, group, wide, slots, tall),
        in_specs=[anywhere, vmem, vmem, vmem, vmem],
        out_specs=[vmem, vmem],
        out_shape=[out, out],
        scratch_shapes=[
            pltpu.VMEM((slots, p.sensors, group * p.chans), f32),
            pltpu.SemaphoreType.DMA((slots, group)),
            pltpu.VMEM((p.pairs, p.r3, 6 * p.r2), bf16),
            pltpu.VMEM((p.pairs * p.times, 2 * p.r2), f32),
            pltpu.VMEM((p.pairs * p.times, 2 * p.r2), f32),
            pltpu.VMEM((p.sensors, 2 * p.r1), f32),
            pltpu.VMEM((p.r2, p.chans), f32),
            pltpu.VMEM((p.r3, LANES), f32),
            pltpu.VMEM((2 * p.r1, p.sensors), bf16),
            pltpu.VMEM((p.times // wide, p.r1, width), f32),
            pltpu.VMEM((p.times // wide, width, 2 * p.r1), bf16),
            pltpu.VMEM((2 * p.r1, p.times * p.chans), bf16),
        ],
        compiler_params=pltpu.CompilerParams(vmem_limit_bytes=56 * 2**20),
        cost_estimate=pl.CostEstimate(
            flops=12 * p.sensors * p.r1 * p.times * p.chans,
            bytes_accessed=4 * p.sensors * p.times * p.chans,
            transcendentals=0,
        ),
        name="partials",
    )(tensor, core, sensor_t, chan_t, time_t)


def graph_kernel(p, piece, ids, edges, *refs):
    shards, (out, weights, near, sem) = refs[: p.n_sensor], refs[p.n_sensor :]
    slots, block = edges.shape[1], edges.shape[-1]
    in_block = block // piece
    pieces = p.share // piece
    blocks = p.sensors // block
    me = lax.axis_index("sensor")
    first = (lax.axis_index("channel") * p.n_time + lax.axis_index("tm")) * pieces

    def where(g):
        at = first + g
        return at // in_block, pl.multiple_of((at % in_block) * piece, piece)

    def edge_copy(g):
        b, off = where(g)
        return pltpu.make_async_copy(edges.at[b, :, pl.ds(off, piece), :], weights.at[g], sem.at[g, slots + 1])

    def block_copy(g, n, shard, at):
        lanes = pl.ds(pl.multiple_of(at * block, block), block)
        return pltpu.make_async_copy(shards[shard].at[:, lanes], near.at[g, :, n * block : (n + 1) * block], sem.at[g, n])

    for g in range(pieces):
        edge_copy(g).start()
        b, _ = where(g)
        block_copy(g, slots, 0, b).start()
        for n in range(slots):
            other = ids[b, n]
            rel = lax.bitwise_xor(other // blocks, me)
            for s in range(p.n_sensor):

                @pl.when(rel == s)
                def _():
                    block_copy(g, n, s, other % blocks).start()

    rows = lax.broadcasted_iota(jnp.int32, (piece, block), 0)
    cols = lax.broadcasted_iota(jnp.int32, (piece, block), 1)
    parts = []
    for g in range(pieces):
        _, off = where(g)
        edge_copy(g).wait()
        for n in range(slots + 1):
            block_copy(g, n, 0, 0).wait()
        w = [weights[g, n].astype(f32) for n in range(slots)]
        degree = jnp.sum(sum(w[1:], w[0]), axis=1, keepdims=True)
        own_h, own_l = split(jnp.where(cols == rows + off, degree, 0.0))
        left = jnp.concatenate([(-x).astype(bf16) for x in w] + [own_h, own_l], axis=1)
        high, low = split(near[g])
        right = jnp.concatenate([high, low], axis=0)
        right = jnp.concatenate([right, right[:, slots * block :]], axis=1)
        term = dot(left, right, NT)
        parts.append((term[:, : p.r1] + term[:, p.r1 :]) * lap_weight)
    out[...] = jnp.concatenate(parts, axis=0).T


def graph_rows(p, ids, edges, *shards):
    block, slots = edges.shape[-1], edges.shape[1]
    piece = math.gcd(p.share, block)
    pieces = p.share // piece
    return pl.pallas_call(
        functools.partial(graph_kernel, p, piece),
        in_specs=[smem] + [anywhere] * (1 + p.n_sensor),
        out_specs=vmem,
        out_shape=jax.ShapeDtypeStruct((p.r1, p.share), f32),
        scratch_shapes=[
            pltpu.VMEM((pieces, slots, piece, block), jnp.int32),
            pltpu.VMEM((pieces, p.r1, (slots + 1) * block), f32),
            pltpu.SemaphoreType.DMA((pieces, slots + 2)),
        ],
        compiler_params=pltpu.CompilerParams(vmem_limit_bytes=32 * 2**20),
        cost_estimate=pl.CostEstimate(flops=10**8, bytes_accessed=10**6, transcendentals=0),
        name="graph",
    )(ids, edges, *shards)


def put_half(p, ht, arrays, core_out, chan_out, core_buf, sem):
    half = lax.bitwise_xor(lax.axis_index("tm"), ht)
    copies = []
    for m in range(p.n_channel):
        for rr in range(p.pairs_part):
            rows = arrays[m][rr * p.r3 : (rr + 1) * p.r3, :]
            core_buf[m, 0, rr] = rows[:, : p.r2]
            core_buf[m, 1, rr] = rows[:, p.r2 :]
        first = (half * p.n_channel + lax.bitwise_xor(lax.axis_index("channel"), m)) * p.pairs_part
        for side in range(2):
            copies.append(
                pltpu.make_async_copy(
                    core_buf.at[m, side],
                    core_out.at[pl.ds(first + side * p.pairs, p.pairs_part)],
                    sem.at[m, side],
                )
            )
            copies[-1].start()
    start = pl.multiple_of(half * p.chan_rows, 8)
    chan_rows = arrays[0].at[p.sum_rows : p.sum_rows + p.chan_rows, :]
    copies.append(
        pltpu.make_async_copy(chan_rows, chan_out.at[pl.ds(start, p.chan_rows), :], sem.at[p.n_channel, 0])
    )
    copies[-1].start()
    return copies


def first_kernel(p, *refs):
    arrays, refs = refs[: p.n_channel], refs[p.n_channel :]
    fit, graph, core_out, chan_out, sensor_out, time_out, core_buf, sem = refs
    copies = put_half(p, 0, arrays, core_out, chan_out, core_buf, sem)
    sensor_out[...] = halves(fit[...]).T + graph[...]
    for m in range(p.n_channel):
        quarter = lax.bitwise_xor(lax.axis_index("channel"), m)
        start = pl.multiple_of(quarter * p.time_rows, 8)
        time_out[pl.ds(start, p.time_rows), :] = arrays[m][p.core_rows : p.sum_rows, : p.times]
    for c in copies:
        c.wait()


def second_kernel(p, *refs):
    arrays, (core_out, chan_out, core_buf, sem) = refs[: p.n_channel], refs[p.n_channel + 2 :]
    for c in put_half(p, 1, arrays, core_out, chan_out, core_buf, sem):
        c.wait()


def half_scratch(p):
    return [
        pltpu.VMEM((p.n_channel, 2, p.pairs_part, p.r3, p.r2), f32),
        pltpu.SemaphoreType.DMA((p.n_channel + 1, 2)),
    ]


def first_half(p, fit, graph, *arrays):
    return pl.pallas_call(
        functools.partial(first_kernel, p),
        in_specs=[vmem] * (len(arrays) + 2),
        out_specs=[anywhere] * 2 + [vmem] * 2,
        out_shape=[
            jax.ShapeDtypeStruct((p.r1, p.r3, p.r2), f32),
            jax.ShapeDtypeStruct((p.r2, p.chans), f32),
            jax.ShapeDtypeStruct((p.r1, p.share), f32),
            jax.ShapeDtypeStruct((p.r3, p.times), f32),
        ],
        scratch_shapes=half_scratch(p),
        compiler_params=pltpu.CompilerParams(vmem_limit_bytes=8 * 2**20),
        cost_estimate=pl.CostEstimate(flops=10**6, bytes_accessed=10**6, transcendentals=0),
        name="first_half",
    )(*arrays, fit, graph)


def second_half(p, core_t, chan_t, *arrays):
    return pl.pallas_call(
        functools.partial(second_kernel, p),
        in_specs=[vmem] * len(arrays) + [anywhere] * 2,
        out_specs=[anywhere] * 2,
        out_shape=[jax.ShapeDtypeStruct(core_t.shape, f32), jax.ShapeDtypeStruct(chan_t.shape, f32)],
        scratch_shapes=half_scratch(p),
        input_output_aliases={len(arrays): 0, len(arrays) + 1: 1},
        compiler_params=pltpu.CompilerParams(vmem_limit_bytes=8 * 2**20),
        cost_estimate=pl.CostEstimate(flops=10**6, bytes_accessed=10**6, transcendentals=0),
        name="second_half",
    )(*arrays, core_t, chan_t)


def swap(x, axis, size, mask):
    return lax.ppermute(x, axis, [(i, i ^ mask) for i in range(size)])


def on_device(
    tensor, core, sensor_factor, channel_factor, time_factor, neighbour_ids, edge_weights
):
    n_sensor = lax.axis_size("sensor")
    n_channel = lax.axis_size("channel")
    n_time = lax.axis_size("tm")
    p = Plan(tensor.shape, core.shape, n_sensor, n_channel, n_time)

    shards = [swap(sensor_factor.T, "sensor", n_sensor, m) for m in range(1, n_sensor)]
    keep, send = partials(
        p, tensor, core.transpose(0, 2, 1), sensor_factor.T, channel_factor.T, time_factor.T
    )
    keep, send, *shards = lax.optimization_barrier((keep, send, *shards))
    held = keep + swap(send, "tm", n_time, 1)
    total = held[: p.chunk]
    for m in range(1, n_channel):
        total = total + swap(held[m * p.chunk : (m + 1) * p.chunk], "channel", n_channel, m)
    graph = graph_rows(p, neighbour_ids, edge_weights, sensor_factor.T, *shards)
    total, graph = lax.optimization_barrier((total, graph))
    fit = total[p.sum_rows :]
    total = jnp.concatenate([total[: p.sum_rows], held[n_channel * p.chunk :]], axis=0)
    for n in range(n_sensor.bit_length() - 1):
        total = total + swap(total, "sensor", n_sensor, 1 << n)
    others = [
        swap(total[: p.sum_rows], "channel", n_channel, m) for m in range(1, n_channel)
    ]
    far = [swap(x, "tm", n_time, 1) for x in (total, *others)]
    core_t, chan_t, sensor_t, time_t = first_half(p, fit, graph, total, *others)
    core_t, chan_t = second_half(p, core_t, chan_t, *far)
    return (core_t.transpose(0, 2, 1), sensor_t.T, chan_t.T, time_t.T)


def solution(mesh):
    return jax.shard_map(
        on_device,
        mesh=mesh,
        in_specs=(
            P("sensor", "tm", "channel"),
            P(),
            P("sensor", None),
            P("channel", None),
            P("tm", None),
            P("sensor", None),
            P("sensor", None, None, None),
        ),
        out_specs=(P(), P(("sensor", "channel", "tm"), None), P("channel", None), P("tm", None)),
        check_vma=False,
    )
```

time: 80.8 us -> 61.1 us (0.76); the launches traced: 79.2 us -> 60.9 us
  waiting for transfers between devices: 21.5 us -> 9.36 us
  Pallas kernels: 35.2 us -> 25.8 us
  starting transfers between devices: 16.6 us -> 23.5 us
  local copies, waits for them, and re-layouts: 3.29 us -> 0.14 us
    ppermute x12 -> x16, waiting for transfers between devices: 21.5 us -> 9.36 us  [swap(): return lax.ppermute(x, axis, [(i, i ^ mask) for i in range(size)])]
    pallas_call x3 -> x4, Pallas kernels: 35.2 us -> 25.8 us  [the longest x1 21 us: partials(): pl.pallas_call(functools.partial(partial_kernel, p, group, wide, slots, t...]
    ppermute x12 -> x16, starting transfers between devices: 16.6 us -> 23.5 us  [swap(): return lax.ppermute(x, axis, [(i, i ^ mask) for i in range(size)])]
    unnamed x13 -> x7, local copies, waits for them, and re-layouts: 2.65 us -> 0.1 us
  transfers between devices with their start and end apart: 12 -> 16, of which waited for: 8 -> 5; matrix products, arithmetic and copies ran while one was open for 4% -> 0% of each run, Pallas kernels for 3% -> 41%
where the time goes in v2:
time: 61.1 us; the launch traced here: 60.9 us
  Pallas kernels  25.8 us (42%)
  starting transfers between devices  23.5 us (38%)
  waiting for transfers between devices  9.36 us (15%)
  other arithmetic  1.12 us (2%)
  between operations  0.96 us (2%)
    ppermute x16, starting transfers between devices, swap(): return lax.ppermute(x, axis, [(i, i ^ mask) for i in range(size)])  23.5 us
    pallas_call x1, Pallas kernels, partials(): pl.pallas_call(functools.partial(partial_kernel, p, group, wide, slots, t...  21 us
    ppermute x16, waiting for transfers between devices, swap(): return lax.ppermute(x, axis, [(i, i ^ mask) for i in range(size)])  9.36 us
    pallas_call x1, Pallas kernels, graph_rows(): pl.pallas_call(functools.partial(graph_kernel, p, piece), in_specs=[smem]...  2.32 us
    pallas_call x1, Pallas kernels, first_half(): pl.pallas_call(functools.partial(first_kernel, p), in_specs=[vmem] * (len...  1.57 us
  transfers between devices with their start and end apart: 16, of which 5 were waited for; matrix products, arithmetic and copies ran while one was open for 0% of the time, Pallas kernels for 41%

profile of v2, /device:TPU:1, one launch (start us, length us, event | category | flops | bytes accessed | tf_op | source)
XLA Modules:
  0.0 60.9 jit_solution(1258796858759568540)
XLA Ops:
  0.7 4.2 %collective-permute-start.2 = (f32[64,768]{1,0:T(8,128)}, f32[64,768]{1,0:T(8,128)S(1)}, u32[]{:S(2)}, u32[]{:S(2)}) collective-permute-start(f32[64,768]{1,0:T(8,128)} %bitcast.8), channel_id=1, source_target_pairs={{0,24},{8,16},{16,8},{24,0},{1,25},{9,17},{17,9},{25,1},{2,26},{10... | collective-permute-start | bytes 589832 | tf_op jit(solution)/shard_map/ppermute | solution.py:412
  4.9 0.4 collective-permute-start
  5.2 21.0 %partials.1 = (f32[768,128]{1,0:T(8,128)}, f32[768,128]{1,0:T(8,128)}) custom-call(f32[768,64,128]{2,1,0:T(8,128)} %x_hbm.1, f32[64,32,64]{2,1,0:T(8,128)} %bitcast.13, f32[64,768]{1,0:T(8,128)} %bitcast.11, f32[64,128]{1,0:T(8,128)} %bitcast.15, f32[32,64]{1,0:T(8,128)} %bitcast.17), custom_call_target="tpu_custom_call" | custom-call | flops 4831838208 | bytes 25165824 | tf_op jit(solution)/shard_map/partials/pallas_call | solution.py:223
  26.2 0.0 collective-permute-done.2.refs_3_
  26.2 0.0 collective-permute-done.1.refs_2_
  26.2 1.3 %collective-permute-start.3 = (f32[768,128]{1,0:T(8,128)}, f32[768,128]{1,0:T(8,128)S(1)}, u32[]{:S(2)}, u32[]{:S(2)}) collective-permute-start(f32[768,128]{1,0:T(8,128)} %get-tuple-element.22), channel_id=1, source_target_pairs={{0,1},{1,0},{2,3},{3,2},{4,5},{5,4},{6,7},{7,6},{8,9},{9,8},{10,11... | collective-permute-start | bytes 1179656 | tf_op jit(solution)/shard_map/ppermute | solution.py:412
  27.5 1.6 %collective-permute-done.3 = f32[768,128]{1,0:T(8,128)S(1)} collective-permute-done((f32[768,128]{1,0:T(8,128)}, f32[768,128]{1,0:T(8,128)S(1)}, u32[]{:S(2)}, u32[]{:S(2)}) %collective-permute-start.3) | collective-permute-done | bytes 393248 | tf_op jit(solution)/shard_map/ppermute | solution.py:412
  29.1 1.1 %add.18 = f32[768,128]{1,0:T(8,128)S(1)} add(f32[768,128]{1,0:T(8,128)} %get-tuple-element.21, f32[768,128]{1,0:T(8,128)S(1)} %collective-permute-done.3) | non-fusion elementwise | flops 98304 | bytes 1179648 | tf_op jit(solution)/shard_map/add | solution.py:428
  30.2 1.4 %collective-permute-start.4 = (f32[184,128]{1,0:T(8,128)S(1)}, f32[184,128]{1,0:T(8,128)S(1)}, u32[]{:S(2)}, u32[]{:S(2)}) collective-permute-start(f32[184,128]{1,0:T(8,128)S(1)} %get-tuple-element.34), channel_id=1, source_target_pairs={{0,2},{2,0},{4,6},{6,4},{1,3},{3,1},{5,7},{7,5},{8,10},{10,8},{12,... | collective-permute-start | bytes 282632 | tf_op jit(solution)/shard_map/ppermute | solution.py:412
  31.6 1.2 %collective-permute-start.6 = (f32[184,128]{1,0:T(8,128)S(1)}, f32[184,128]{1,0:T(8,128)S(1)}, u32[]{:S(2)}, u32[]{:S(2)}) collective-permute-start(f32[184,128]{1,0:T(8,128)S(1)} %get-tuple-element.35), channel_id=1, source_target_pairs={{0,6},{2,4},{4,2},{6,0},{1,7},{3,5},{5,3},{7,1},{8,14},{10,12},{12... | collective-permute-start | bytes 282632 | tf_op jit(solution)/shard_map/ppermute | solution.py:412
  32.8 0.1 collective-permute-start.5
  32.9 0.1 copy.13.ids
  33.0 2.3 %graph.1.refs_5_ = f32[64,96]{1,0:T(8,128)S(1)} custom-call(s32[6,4]{1,0:T(8,128)S(1)} %copy.13.ids, s32[6,4,128,128]{3,2,1,0:T(8,128)S(1)} %copy-done, f32[64,768]{1,0:T(8,128)S(1)} %bitcast.12, f32[64,768]{1,0:T(8,128)S(1)} %collective-permute-done.refs_1_, f32[64,768]{1,0:T(8,128)S(1)} %collective-permute-done.1.refs_2_, ...), custom_call_target="tpu_custom_call" | custom-call | flops 100000000 | bytes 1000000 | tf_op jit(solution)/shard_map/graph/pallas_call | solution.py:310
  35.3 0.0 collective-permute-done.4
  35.3 1.9 %collective-permute-done.6 = f32[184,128]{1,0:T(8,128)S(1)} collective-permute-done((f32[184,128]{1,0:T(8,128)S(1)}, f32[184,128]{1,0:T(8,128)S(1)}, u32[]{:S(2)}, u32[]{:S(2)}) %collective-permute-start.6) | collective-permute-done | bytes 94240 | tf_op jit(solution)/shard_map/ppermute | solution.py:412
  37.3 1.4 %collective-permute-done.5 = f32[184,128]{1,0:T(8,128)S(1)} collective-permute-done((f32[184,128]{1,0:T(8,128)S(1)}, f32[184,128]{1,0:T(8,128)S(1)}, u32[]{:S(2)}, u32[]{:S(2)}) %collective-permute-start.5) | collective-permute-done | bytes 94240 | tf_op jit(solution)/shard_map/ppermute | solution.py:412
  38.7 1.0 %collective-permute-start.7 = (f32[168,128]{1,0:T(8,128)S(1)}, f32[168,128]{1,0:T(8,128)S(1)}, u32[]{:S(2)}, u32[]{:S(2)}) collective-permute-start(f32[168,128]{1,0:T(8,128)S(1)} %pad_maximum_fusion), channel_id=1, source_target_pairs={{0,8},{8,0},{16,24},{24,16},{1,9},{9,1},{17,25},{25,17},{2,10},{10... | collective-permute-start | bytes 258056 | tf_op jit(solution)/shard_map/ppermute | solution.py:412
  39.8 2.4 %collective-permute-done.7 = f32[168,128]{1,0:T(8,128)S(1)} collective-permute-done((f32[168,128]{1,0:T(8,128)S(1)}, f32[168,128]{1,0:T(8,128)S(1)}, u32[]{:S(2)}, u32[]{:S(2)}) %collective-permute-start.7) | collective-permute-done | bytes 86048 | tf_op jit(solution)/shard_map/ppermute | solution.py:412
  42.1 2.2 %collective-permute-start.8 = (f32[168,128]{1,0:T(8,128)S(1)}, f32[168,128]{1,0:T(8,128)S(1)}, u32[]{:S(2)}, u32[]{:S(2)}) collective-permute-start(f32[168,128]{1,0:T(8,128)S(1)} %fusion.2), channel_id=1, source_target_pairs={{0,16},{8,24},{16,0},{24,8},{1,17},{9,25},{17,1},{25,9},{2,18},{10... | collective-permute-start | bytes 258056 | tf_op jit(solution)/shard_map/ppermute | solution.py:412
  44.4 2.1 %collective-permute-done.8 = f32[168,128]{1,0:T(8,128)S(1)} collective-permute-done((f32[168,128]{1,0:T(8,128)S(1)}, f32[168,128]{1,0:T(8,128)S(1)}, u32[]{:S(2)}, u32[]{:S(2)}) %collective-permute-start.8) | collective-permute-done | bytes 86048 | tf_op jit(solution)/shard_map/ppermute | solution.py:412
  46.5 1.2 %collective-permute-start.14 = (f32[136,128]{1,0:T(8,128)S(1)}, f32[136,128]{1,0:T(8,128)S(1)}, u32[]{:S(2)}, u32[]{:S(2)}) collective-permute-start(f32[136,128]{1,0:T(8,128)S(1)} %slice.39), channel_id=1, source_target_pairs={{0,6},{2,4},{4,2},{6,0},{1,7},{3,5},{5,3},{7,1},{8,14},{10,12},{12... | collective-permute-start | bytes 208904 | tf_op jit(solution)/shard_map/ppermute | solution.py:412
  47.7 1.2 %collective-permute-start.12 = (f32[136,128]{1,0:T(8,128)S(1)}, f32[136,128]{1,0:T(8,128)S(1)}, u32[]{:S(2)}, u32[]{:S(2)}) collective-permute-start(f32[136,128]{1,0:T(8,128)S(1)} %slice.39), channel_id=1, source_target_pairs={{0,4},{2,6},{4,0},{6,2},{1,5},{3,7},{5,1},{7,3},{8,12},{10,14},{12... | collective-permute-start | bytes 208904 | tf_op jit(solution)/shard_map/ppermute | solution.py:412
  48.9 0.2 collective-permute-start.10
  49.2 5.2 %collective-permute-start.9 = (f32[168,128]{1,0:T(8,128)S(1)}, f32[168,128]{1,0:T(8,128)S(1)}, u32[]{:S(2)}, u32[]{:S(2)}) collective-permute-start(f32[168,128]{1,0:T(8,128)S(1)} %add.23.refs_0_), channel_id=1, source_target_pairs={{0,1},{1,0},{2,3},{3,2},{4,5},{5,4},{6,7},{7,6},{8,9},{9,8},{10,11... | collective-permute-start | bytes 258056 | tf_op jit(solution)/shard_map/ppermute | solution.py:412
  54.4 1.7 %collective-permute-start.15 = (f32[136,128]{1,0:T(8,128)S(1)}, f32[136,128]{1,0:T(8,128)S(1)}, u32[]{:S(2)}, u32[]{:S(2)}) collective-permute-start(f32[136,128]{1,0:T(8,128)S(1)} %collective-permute-done.14.refs_3_), channel_id=1, source_target_pairs={{0,1},{1,0},{2,3},{3,2},{4,5},{5,4},{6,7},{7,6},{8,9},{9,8},{10,11... | collective-permute-start | bytes 208904 | tf_op jit(solution)/shard_map/ppermute | solution.py:412
  56.1 0.0 collective-permute-done.12.refs_2_
  56.2 0.7 %collective-permute-start.13 = (f32[136,128]{1,0:T(8,128)S(1)}, f32[136,128]{1,0:T(8,128)S(1)}, u32[]{:S(2)}, u32[]{:S(2)}) collective-permute-start(f32[136,128]{1,0:T(8,128)S(1)} %collective-permute-done.12.refs_2_), channel_id=1, source_target_pairs={{0,1},{1,0},{2,3},{3,2},{4,5},{5,4},{6,7},{7,6},{8,9},{9,8},{10,11... | collective-permute-start | bytes 208904 | tf_op jit(solution)/shard_map/ppermute | solution.py:412
  56.9 0.0 collective-permute-done.10.refs_1_
  56.9 1.3 %collective-permute-start.11 = (f32[136,128]{1,0:T(8,128)S(1)}, f32[136,128]{1,0:T(8,128)S(1)}, u32[]{:S(2)}, u32[]{:S(2)}) collective-permute-start(f32[136,128]{1,0:T(8,128)S(1)} %collective-permute-done.10.refs_1_), channel_id=1, source_target_pairs={{0,1},{1,0},{2,3},{3,2},{4,5},{5,4},{6,7},{7,6},{8,9},{9,8},{10,11... | collective-permute-start | bytes 208904 | tf_op jit(solution)/shard_map/ppermute | solution.py:412
  58.2 1.6 %first_half.1 = (f32[64,32,64]{2,1,0:T(8,128)}, f32[64,128]{1,0:T(8,128)}, f32[64,96]{1,0:T(8,128)}, f32[32,64]{1,0:T(8,128)}) custom-call(f32[168,128]{1,0:T(8,128)S(1)} %add.23.refs_0_, f32[136,128]{1,0:T(8,128)S(1)} %collective-permute-done.10.refs_1_, f32[136,128]{1,0:T(8,128)S(1)} %collective-permute-done.12.refs_2_, ...), custom_call_target="tpu_custom_call" | custom-call | flops 1000000 | bytes 1000000 | tf_op jit(solution)/shard_map/first_half/pallas_call | solution.py:380
  59.8 0.0 collective-permute-done.9.refs_0_
  59.8 1.0 %second_half.1 = (f32[64,32,64]{2,1,0:T(8,128)}, f32[64,128]{1,0:T(8,128)}) custom-call(f32[168,128]{1,0:T(8,128)S(1)} %collective-permute-done.9.refs_0_, f32[136,128]{1,0:T(8,128)S(1)} %collective-permute-done.11.refs_1_, f32[136,128]{1,0:T(8,128)S(1)} %collective-permute-done.13.refs_2_, ...), custom_call_target="tpu_custom_call", output_to_operand_aliasing={{0}: (4, {}), {1}: (5, {})} | custom-call | flops 1000000 | bytes 1000000 | tf_op jit(solution)/shard_map/second_half/pallas_call | solution.py:398
  (21 shorter events, 0.1 us)
Async XLA Ops:
  0.6 32.4 %copy-start.1 = (f32[768,64]{0,1:T(8,128)S(1)}, f32[768,64]{0,1:T(8,128)}, u32[]{:S(2)}) copy-start(f32[768,64]{0,1:T(8,128)} %param.9) | copy-start | bytes 589828
  0.6 32.3 %copy-start.2 = (s32[6,4]{0,1:T(4,128)S(1)}, s32[6,4]{0,1:T(4,128)}, u32[]{:S(2)}) copy-start(s32[6,4]{0,1:T(4,128)} %param.12) | copy-start | bytes 292
  0.7 32.3 %copy-start = (s32[6,4,128,128]{3,2,1,0:T(8,128)S(1)}, s32[6,4,128,128]{3,2,1,0:T(8,128)}, u32[]{:S(2)}) copy-start(s32[6,4,128,128]{3,2,1,0:T(8,128)} %edges.1) | copy-start | bytes 4718596
  0.7 25.5 %collective-permute-start.2 = (f32[64,768]{1,0:T(8,128)}, f32[64,768]{1,0:T(8,128)S(1)}, u32[]{:S(2)}, u32[]{:S(2)}) collective-permute-start(f32[64,768]{1,0:T(8,128)} %bitcast.8), channel_id=1, source_target_pairs={{0,24},{8,16},{16,8},{24,0},{1,25},{9,17},{17,9},{25,1},{2,26},{10... | collective-permute-start | bytes 589832 | tf_op jit(solution)/shard_map/ppermute | solution.py:412
  4.9 21.3 %collective-permute-start.1 = (f32[64,768]{1,0:T(8,128)}, f32[64,768]{1,0:T(8,128)S(1)}, u32[]{:S(2)}, u32[]{:S(2)}) collective-permute-start(f32[64,768]{1,0:T(8,128)} %bitcast.9), channel_id=1, source_target_pairs={{0,16},{8,24},{16,0},{24,8},{1,17},{9,25},{17,1},{25,9},{2,18},{10... | collective-permute-start | bytes 589832 | tf_op jit(solution)/shard_map/ppermute | solution.py:412
  4.9 21.3 %collective-permute-start = (f32[64,768]{1,0:T(8,128)}, f32[64,768]{1,0:T(8,128)S(1)}, u32[]{:S(2)}, u32[]{:S(2)}) collective-permute-start(f32[64,768]{1,0:T(8,128)} %bitcast.10), channel_id=1, source_target_pairs={{0,8},{8,0},{16,24},{24,16},{1,9},{9,1},{17,25},{25,17},{2,10},{10... | collective-permute-start | bytes 589832 | tf_op jit(solution)/shard_map/ppermute | solution.py:412
  26.2 2.9 %collective-permute-start.3 = (f32[768,128]{1,0:T(8,128)}, f32[768,128]{1,0:T(8,128)S(1)}, u32[]{:S(2)}, u32[]{:S(2)}) collective-permute-start(f32[768,128]{1,0:T(8,128)} %get-tuple-element.22), channel_id=1, source_target_pairs={{0,1},{1,0},{2,3},{3,2},{4,5},{5,4},{6,7},{7,6},{8,9},{9,8},{10,11... | collective-permute-start | bytes 1179656 | tf_op jit(solution)/shard_map/ppermute | solution.py:412
  30.2 5.2 %collective-permute-start.4 = (f32[184,128]{1,0:T(8,128)S(1)}, f32[184,128]{1,0:T(8,128)S(1)}, u32[]{:S(2)}, u32[]{:S(2)}) collective-permute-start(f32[184,128]{1,0:T(8,128)S(1)} %get-tuple-element.34), channel_id=1, source_target_pairs={{0,2},{2,0},{4,6},{6,4},{1,3},{3,1},{5,7},{7,5},{8,10},{10,8},{12,... | collective-permute-start | bytes 282632 | tf_op jit(solution)/shard_map/ppermute | solution.py:412
  31.6 5.7 %collective-permute-start.6 = (f32[184,128]{1,0:T(8,128)S(1)}, f32[184,128]{1,0:T(8,128)S(1)}, u32[]{:S(2)}, u32[]{:S(2)}) collective-permute-start(f32[184,128]{1,0:T(8,128)S(1)} %get-tuple-element.35), channel_id=1, source_target_pairs={{0,6},{2,4},{4,2},{6,0},{1,7},{3,5},{5,3},{7,1},{8,14},{10,12},{12... | collective-permute-start | bytes 282632 | tf_op jit(solution)/shard_map/ppermute | solution.py:412
  32.8 5.9 %collective-permute-start.5 = (f32[184,128]{1,0:T(8,128)S(1)}, f32[184,128]{1,0:T(8,128)S(1)}, u32[]{:S(2)}, u32[]{:S(2)}) collective-permute-start(f32[184,128]{1,0:T(8,128)S(1)} %get-tuple-element.36), channel_id=1, source_target_pairs={{0,4},{2,6},{4,0},{6,2},{1,5},{3,7},{5,1},{7,3},{8,12},{10,14},{12... | collective-permute-start | bytes 282632 | tf_op jit(solution)/shard_map/ppermute | solution.py:412
  38.7 3.4 %collective-permute-start.7 = (f32[168,128]{1,0:T(8,128)S(1)}, f32[168,128]{1,0:T(8,128)S(1)}, u32[]{:S(2)}, u32[]{:S(2)}) collective-permute-start(f32[168,128]{1,0:T(8,128)S(1)} %pad_maximum_fusion), channel_id=1, source_target_pairs={{0,8},{8,0},{16,24},{24,16},{1,9},{9,1},{17,25},{25,17},{2,10},{10... | collective-permute-start | bytes 258056 | tf_op jit(solution)/shard_map/ppermute | solution.py:412
  42.1 4.3 %collective-permute-start.8 = (f32[168,128]{1,0:T(8,128)S(1)}, f32[168,128]{1,0:T(8,128)S(1)}, u32[]{:S(2)}, u32[]{:S(2)}) collective-permute-start(f32[168,128]{1,0:T(8,128)S(1)} %fusion.2), channel_id=1, source_target_pairs={{0,16},{8,24},{16,0},{24,8},{1,17},{9,25},{17,1},{25,9},{2,18},{10... | collective-permute-start | bytes 258056 | tf_op jit(solution)/shard_map/ppermute | solution.py:412
  46.5 7.9 %collective-permute-start.14 = (f32[136,128]{1,0:T(8,128)S(1)}, f32[136,128]{1,0:T(8,128)S(1)}, u32[]{:S(2)}, u32[]{:S(2)}) collective-permute-start(f32[136,128]{1,0:T(8,128)S(1)} %slice.39), channel_id=1, source_target_pairs={{0,6},{2,4},{4,2},{6,0},{1,7},{3,5},{5,3},{7,1},{8,14},{10,12},{12... | collective-permute-start | bytes 208904 | tf_op jit(solution)/shard_map/ppermute | solution.py:412
  47.7 8.4 %collective-permute-start.12 = (f32[136,128]{1,0:T(8,128)S(1)}, f32[136,128]{1,0:T(8,128)S(1)}, u32[]{:S(2)}, u32[]{:S(2)}) collective-permute-start(f32[136,128]{1,0:T(8,128)S(1)} %slice.39), channel_id=1, source_target_pairs={{0,4},{2,6},{4,0},{6,2},{1,5},{3,7},{5,1},{7,3},{8,12},{10,14},{12... | collective-permute-start | bytes 208904 | tf_op jit(solution)/shard_map/ppermute | solution.py:412
  48.9 7.9 %collective-permute-start.10 = (f32[136,128]{1,0:T(8,128)S(1)}, f32[136,128]{1,0:T(8,128)S(1)}, u32[]{:S(2)}, u32[]{:S(2)}) collective-permute-start(f32[136,128]{1,0:T(8,128)S(1)} %slice.39), channel_id=1, source_target_pairs={{0,2},{2,0},{4,6},{6,4},{1,3},{3,1},{5,7},{7,5},{8,10},{10,8},{12,... | collective-permute-start | bytes 208904 | tf_op jit(solution)/shard_map/ppermute | solution.py:412
  49.2 10.6 %collective-permute-start.9 = (f32[168,128]{1,0:T(8,128)S(1)}, f32[168,128]{1,0:T(8,128)S(1)}, u32[]{:S(2)}, u32[]{:S(2)}) collective-permute-start(f32[168,128]{1,0:T(8,128)S(1)} %add.23.refs_0_), channel_id=1, source_target_pairs={{0,1},{1,0},{2,3},{3,2},{4,5},{5,4},{6,7},{7,6},{8,9},{9,8},{10,11... | collective-permute-start | bytes 258056 | tf_op jit(solution)/shard_map/ppermute | solution.py:412
  54.4 5.4 %collective-permute-start.15 = (f32[136,128]{1,0:T(8,128)S(1)}, f32[136,128]{1,0:T(8,128)S(1)}, u32[]{:S(2)}, u32[]{:S(2)}) collective-permute-start(f32[136,128]{1,0:T(8,128)S(1)} %collective-permute-done.14.refs_3_), channel_id=1, source_target_pairs={{0,1},{1,0},{2,3},{3,2},{4,5},{5,4},{6,7},{7,6},{8,9},{9,8},{10,11... | collective-permute-start | bytes 208904 | tf_op jit(solution)/shard_map/ppermute | solution.py:412
  56.2 3.6 %collective-permute-start.13 = (f32[136,128]{1,0:T(8,128)S(1)}, f32[136,128]{1,0:T(8,128)S(1)}, u32[]{:S(2)}, u32[]{:S(2)}) collective-permute-start(f32[136,128]{1,0:T(8,128)S(1)} %collective-permute-done.12.refs_2_), channel_id=1, source_target_pairs={{0,1},{1,0},{2,3},{3,2},{4,5},{5,4},{6,7},{7,6},{8,9},{9,8},{10,11... | collective-permute-start | bytes 208904 | tf_op jit(solution)/shard_map/ppermute | solution.py:412
  56.9 2.9 %collective-permute-start.11 = (f32[136,128]{1,0:T(8,128)S(1)}, f32[136,128]{1,0:T(8,128)S(1)}, u32[]{:S(2)}, u32[]{:S(2)}) collective-permute-start(f32[136,128]{1,0:T(8,128)S(1)} %collective-permute-done.10.refs_1_), channel_id=1, source_target_pairs={{0,1},{1,0},{2,3},{3,2},{4,5},{5,4},{6,7},{7,6},{8,9},{9,8},{10,11... | collective-permute-start | bytes 208904 | tf_op jit(solution)/shard_map/ppermute | solution.py:412

commit v3 on v2

--- a/solution.py
+++ b/solution.py
@@ -14,7 +14,7 @@
 NT = (((1,), (1,)), ((), ()))
 TN = (((0,), (0,)), ((), ()))
 LANES = 128
-LAG = False
+BEFORE = 16
 vmem = pl.BlockSpec(memory_space=pltpu.VMEM)
 smem = pl.BlockSpec(memory_space=pltpu.SMEM)
 anywhere = pl.BlockSpec(memory_space=pl.ANY)
@@ -74,139 +74,156 @@
 
 
 def partial_kernel(
-    p, group, wide, slots, tall,
-    x_hbm, core, sensor_t, chan_t, time_t, keep, send,
-    buf, sem, core_pair, ct, inner_ref, fit_acc, chan_acc, time_acc, sensor_s,
-    fold, g_both, g_parts,
+    p, groups, wide, tall,
+    x_hbm, core_hbm, sensor_hbm, chan_hbm, time_hbm, *refs,
 ):
+    keep, send, refs = refs[0], refs[1], refs[2:]
+    buf, sem, core, sensor_t, chan_t, time_t, small_sem, core_turned, ct, inner_ref, fit_acc, chan_acc, time_acc, sensor_s = refs[:14]
+    fold, g_both, g_parts = refs[14:]
     r1, r2, r3 = p.r1, p.r2, p.r3
     width = wide * p.chans
     steps = p.times // wide
-    groups = p.times // group
-    inside = group // wide
     my_time, my_chan = lax.axis_index("tm"), lax.axis_index("channel")
 
-    def copies(at, slot):
+    def copies(at):
+        first, count, place, _ = groups[at]
         return [
             pltpu.make_async_copy(
-                x_hbm.at[:, at * group + h, :],
-                buf.at[slot, :, h * p.chans : (h + 1) * p.chans],
-                sem.at[slot, h],
+                x_hbm.at[:, first + h, :],
+                buf.at[:, (place + h) * p.chans : (place + h + 1) * p.chans],
+                sem.at[place + h],
             )
-            for h in range(group)
+            for h in range(count)
         ]
 
-    for s in range(slots):
-        for c in copies(s, s):
-            c.start()
-
+    pairs = ((sensor_hbm, sensor_t), (chan_hbm, chan_t), (time_hbm, time_t), (core_hbm, core))
+    small = [pltpu.make_async_copy(a, b, small_sem.at[n]) for n, (a, b) in enumerate(pairs)]
+    for c in small:
+        c.start()
+    behind = {g[3] for g in groups}
+    for at in range(len(groups)):
+        if at not in behind:
+            for c in copies(at):
+                c.start()
+
+    for c in small[:3]:
+        c.wait()
     time_s = split(time_t[...])
-    for r in range(p.pairs):
-        pair = jnp.concatenate([core[r], core[r + p.pairs]], axis=1)
-        pair_h, pair_l = split(pair)
-        core_pair[r] = jnp.concatenate([pair_h, pair_l, pair_h], axis=1)
-        ct[r * p.times : (r + 1) * p.times, :] = dot3(time_s, (pair_h, pair_l), TN)
+    time_rows_s = split(time_t[...].T)
     chan_h, chan_l = split(both(chan_t[...]))
     chan_twice = jnp.concatenate([chan_h, chan_h], axis=0)
     rows_h, rows_l = split(both(chan_t[...].T))
     rows_parts = jnp.concatenate([rows_h, rows_l], axis=1)
-    sensor_f = sensor_t[...]
-    sensor_h, sensor_l = split(sensor_f)
+    sensor_h, sensor_l = split(sensor_t[...])
     sensor_s[0:r1, :] = sensor_h
     sensor_s[r1 : 2 * r1, :] = sensor_l
     gram_h, gram_l = split(dot3((sensor_h, sensor_l), (sensor_h, sensor_l), NT))
     gram_twice = jnp.concatenate([gram_h, gram_h], axis=1)
-    fit_acc[...] = jnp.zeros_like(fit_acc)
-
-    def ct_rows(step):
-        at = [ct[pl.ds(step * wide + h, p.pairs, stride=p.times), :] for h in range(wide)]
+
+    small[3].wait()
+    for first in range(0, p.pairs, p.pairs_part):
+        pairs = []
+        for r in range(first, first + p.pairs_part):
+            pairs.append(jnp.concatenate([core[r], core[r + p.pairs]], axis=1))
+            turned_h, turned_l = split(pairs[-1].T)
+            core_turned[r] = jnp.concatenate([turned_h, turned_l], axis=1)
+        product = dot3(time_rows_s, split(jnp.concatenate(pairs, axis=1)))
+        for n in range(p.pairs_part):
+            rows = slice((first + n) * p.times, (first + n + 1) * p.times)
+            ct[rows, :] = product[:, n * 2 * r2 : (n + 1) * 2 * r2]
+
+    def ct_rows(first, count):
+        at = [ct[pl.ds(k, p.pairs, stride=p.times), :] for k in range(first, first + count)]
         return split(jnp.concatenate(at, axis=0))
 
-    def before(step):
-        ct_h, ct_l = ct_rows(step)
+    def before(first, count):
+        ct_h, ct_l = ct_rows(first, count)
         g = dot(jnp.concatenate([ct_h, ct_l], axis=1), chan_twice) + dot(ct_h, chan_l)
         g_h, g_l = split(
             jnp.concatenate(
-                [halves(g[h * p.pairs : (h + 1) * p.pairs]) for h in range(wide)], axis=1
+                [halves(g[h * p.pairs : (h + 1) * p.pairs]) for h in range(count)], axis=1
             )
         )
         g_hl = jnp.concatenate([g_h, g_l], axis=0)
-        g_parts[:, step * width : (step + 1) * width] = g_hl
-        for h in range(wide):
-            at = slice(h * p.chans, (h + 1) * p.chans)
-            g_both[step, at, :] = g_hl[:, at].T
-
-    def read(step, slot):
-        lanes = slice(step % inside * width, (step % inside + 1) * width)
+        g_parts[:, first * p.chans : (first + count) * p.chans] = g_hl
+        for h in range(count):
+            at = slice((first + h) * p.chans, (first + h + 1) * p.chans)
+            g_both[at, :] = g_hl[:, h * p.chans : (h + 1) * p.chans].T
+
+    def read(step, place):
+        lanes = slice(place * p.chans, place * p.chans + width)
         g_hl = g_parts[:, step * width : (step + 1) * width]
         folded = dot(gram_twice, g_hl) + dot(gram_l, g_hl[:r1])
-        g = g_both[step]
+        g = g_both[step * width : (step + 1) * width, :]
         for i in range(0, p.sensors, tall):
-            x_h, x_l = split(buf[slot, i : i + tall, lanes])
+            x_h, x_l = split(buf[i : i + tall, lanes])
             fit_acc[i : i + tall, :] += dot(x_h, g) + dot(x_l, g)
             a = dot(sensor_s[:, i : i + tall], x_h)
             folded = folded - (a[:r1] + a[r1:] + dot(sensor_s[0:r1, i : i + tall], x_l))
         fold[step] = folded
 
-    def after(step, chan_sum):
-        folded = fold[step]
-        rows = jnp.concatenate(
-            [paired(folded[:, h * p.chans : (h + 1) * p.chans]) for h in range(wide)], axis=0
-        )
-        f_h, f_l = split(rows)
+    def after(first, count, chan_sum):
+        rows = []
+        for step in range(first // wide, (first + count) // wide):
+            folded = fold[step]
+            rows.extend(paired(folded[:, h * p.chans : (h + 1) * p.chans]) for h in range(wide))
+        f_h, f_l = split(jnp.concatenate(rows, axis=0))
         inner = dot(f_h, rows_parts)
         inner = inner[:, : 2 * r2] + inner[:, 2 * r2 :] + dot(f_l, rows_h)
-        for h in range(wide):
-            inner_ref[pl.ds(step * wide + h, p.pairs, stride=p.times), :] = inner[h * p.pairs : (h + 1) * p.pairs]
-        return chan_sum + dot3(ct_rows(step), (f_h, f_l), TN)
-
-    for step in range(steps):
-        before(step)
+        for h in range(count):
+            inner_ref[pl.ds(first + h, p.pairs, stride=p.times), :] = inner[h * p.pairs : (h + 1) * p.pairs]
+        return chan_sum + dot3(ct_rows(first, count), (f_h, f_l), TN)
+
+    for first in range(0, p.times, BEFORE):
+        before(first, BEFORE)
+    ggt = dot(g_parts[...], g_both[...])
+    ggt = ggt[:r1, :r1] + ggt[:r1, r1:] + ggt[r1:, :r1]
+    fit_acc[:, :r1] = -(dot3(split(ggt), (sensor_h, sensor_l)).T)
+    fit_acc[:, r1:] = jnp.zeros((p.sensors, r1), f32)
+
     chan_sum = jnp.zeros((2 * r2, 2 * p.chans), f32)
-    for at in range(groups):
-        slot = at % slots
-        for c in copies(at, slot):
+    for at, (first, count, place, start_next) in enumerate(groups):
+        for c in copies(at):
             c.wait()
-        for step in range(at * inside, (at + 1) * inside):
-            read(step, slot)
-        if at + slots < groups:
-            for c in copies(at + slots, slot):
+        mine = range(first // wide, (first + count) // wide)
+        for n, step in enumerate(mine):
+            read(step, place + n * wide)
+        if start_next is not None:
+            for c in copies(start_next):
                 c.start()
-        if LAG and at >= 1:
-            for step in range((at - 1) * inside, at * inside):
-                chan_sum = after(step, chan_sum)
-    for step in range((groups - 1) * inside if LAG else 0, steps):
-        chan_sum = after(step, chan_sum)
-
-    ggt = dot(g_parts[...], g_parts[...], NT)
-    ggt = ggt[:r1, :r1] + ggt[:r1, r1:] + ggt[r1:, :r1]
-    rebuilt = dot3((sensor_h, sensor_l), split(ggt), TN)
-    fit_acc[:, :r1] = (rebuilt - (fit_acc[:, :r1] + fit_acc[:, r1:])) * p.fit_scale
+        if at > 0:
+            chan_sum = after(*groups[at - 1][:2], chan_sum)
+    chan_sum = after(*groups[-1][:2], chan_sum)
+
     chan_acc[...] = (chan_sum[:r2, : p.chans] + chan_sum[r2:, p.chans :]) * p.chan_scale
     time_h, time_l = time_s
     time_parts = jnp.concatenate([time_h, time_l, time_h], axis=1)
-    time_sum = jnp.zeros((r3, p.times), f32)
+    time_sum = jnp.zeros((p.times, 2 * r3), f32)
+    time_low = jnp.zeros((p.times, r3), f32)
     for ht, out in enumerate((keep, send)):
         half = lax.bitwise_xor(my_time, ht)
         for m in range(p.n_channel):
             quarter = lax.bitwise_xor(my_chan, m)
             base = m * p.chunk
-            for rr in range(p.pairs_part):
-                r = (half * p.n_channel + quarter) * p.pairs_part + rr
-                rows = pl.ds(pl.multiple_of(r * p.times, p.times), p.times)
-                in_h, in_l = split(inner_ref[rows, :])
-                out[base + rr * r3 : base + (rr + 1) * r3, :] = (
-                    dot(time_parts, jnp.concatenate([in_h, in_h, in_l], axis=0)) * p.core_scale
-                )
-                time_sum = time_sum + dot(core_pair[r], jnp.concatenate([in_h, in_h, in_l], axis=1), NT)
-            chunk = quarter * p.n_time + half
-            start = pl.multiple_of(chunk * p.share, 16)
-            fit = fit_acc[pl.ds(start, p.share), 0:r1]
-            out[base + p.sum_rows : base + p.chunk, :] = paired(fit)
+            first = (half * p.n_channel + quarter) * p.pairs_part
+            inner = [
+                inner_ref[pl.ds(pl.multiple_of((first + n) * p.times, p.times), p.times), :]
+                for n in range(p.pairs_part)
+            ]
+            in_h, in_l = split(jnp.concatenate(inner, axis=1))
+            rows = dot(time_parts, jnp.concatenate([in_h, in_h, in_l], axis=0)) * p.core_scale
+            for n in range(p.pairs_part):
+                out[base + n * r3 : base + (n + 1) * r3, :] = rows[:, n * 2 * r2 : (n + 1) * 2 * r2]
+            turned = jnp.concatenate([core_turned[first + n] for n in range(p.pairs_part)], axis=0)
+            time_sum = time_sum + dot(in_h, turned)
+            time_low = time_low + dot(in_l, turned[:, :r3])
+            start = pl.multiple_of((quarter * p.n_time + half) * p.share, 16)
+            fit = fit_acc[pl.ds(start, p.share), :]
+            out[base + p.sum_rows : base + p.chunk, :] = paired((fit[:, :r1] + fit[:, r1:]) * -p.fit_scale)
         chan_start = pl.multiple_of(half * p.chan_rows, 8)
         out[p.n_channel * p.chunk : p.rows, :] = chan_acc[pl.ds(chan_start, p.chan_rows), :]
     time_acc[...] = jnp.zeros_like(time_acc)
-    time_acc[:, 0 : p.times] = time_sum * p.time_scale
+    time_acc[:, 0 : p.times] = (time_sum[:, :r3] + time_sum[:, r3:] + time_low).T * p.time_scale
     for m in range(p.n_channel):
         quarter = lax.bitwise_xor(my_chan, m)
         base = m * p.chunk + p.core_rows
@@ -216,19 +233,30 @@
 
 
 def partials(p, tensor, core, sensor_t, chan_t, time_t):
-    group, wide, tall = 16, 4, 256
-    slots = max(2, min(p.times // group, 2**25 // (4 * p.sensors * group * p.chans)))
+    wide, tall, unit = 4, 256, 16
     width = wide * p.chans
-    out = jax.ShapeDtypeStruct((p.rows, LANES), f32)
+    if 4 * p.sensors * p.times * p.chans <= 2**25:
+        sizes, places = [8, 16, 16, 16, 8], p.times
+        assert sum(sizes) == p.times
+        groups = [(sum(sizes[:n]), size, sum(sizes[:n]), None) for n, size in enumerate(sizes)]
+    else:
+        count = p.times // unit
+        places = 2 * unit
+        groups = [(n * unit, unit, n % 2 * unit, n + 2 if n + 2 < count else None) for n in range(count)]
     return pl.pallas_call(
-        functools.partial(partial_kernel, p, group, wide, slots, tall),
-        in_specs=[anywhere, vmem, vmem, vmem, vmem],
-        out_specs=[vmem, vmem],
-        out_shape=[out, out],
+        functools.partial(partial_kernel, p, groups, wide, tall),
+        in_specs=[anywhere] * 5,
+        out_specs=[vmem] * 2,
+        out_shape=[jax.ShapeDtypeStruct((p.rows, LANES), f32)] * 2,
         scratch_shapes=[
-            pltpu.VMEM((slots, p.sensors, group * p.chans), f32),
-            pltpu.SemaphoreType.DMA((slots, group)),
-            pltpu.VMEM((p.pairs, p.r3, 6 * p.r2), bf16),
+            pltpu.VMEM((p.sensors, places * p.chans), f32),
+            pltpu.SemaphoreType.DMA((places,)),
+            pltpu.VMEM((p.r1, p.r3, p.r2), f32),
+            pltpu.VMEM(sensor_t.shape, f32),
+            pltpu.VMEM(chan_t.shape, f32),
+            pltpu.VMEM(time_t.shape, f32),
+            pltpu.SemaphoreType.DMA((4,)),
+            pltpu.VMEM((p.pairs, 2 * p.r2, 2 * p.r3), bf16),
             pltpu.VMEM((p.pairs * p.times, 2 * p.r2), f32),
             pltpu.VMEM((p.pairs * p.times, 2 * p.r2), f32),
             pltpu.VMEM((p.sensors, 2 * p.r1), f32),
@@ -236,7 +264,7 @@
             pltpu.VMEM((p.r3, LANES), f32),
             pltpu.VMEM((2 * p.r1, p.sensors), bf16),
             pltpu.VMEM((p.times // wide, p.r1, width), f32),
-            pltpu.VMEM((p.times // wide, width, 2 * p.r1), bf16),
+            pltpu.VMEM((p.times * p.chans, 2 * p.r1), bf16),
             pltpu.VMEM((2 * p.r1, p.times * p.chans), bf16),
         ],
         compiler_params=pltpu.CompilerParams(vmem_limit_bytes=56 * 2**20),

time: 61.1 us -> 59.3 us (0.971)
  Pallas kernels: 25.8 us -> 24 us
    pallas_call x1, Pallas kernels: 21 us -> 19.2 us  [partials(): pl.pallas_call(functools.partial(partial_kernel, p, groups, wide, tall),...]
  transfers between devices with their start and end apart: 16 -> 16, of which waited for: 5 -> 5; matrix products, arithmetic and copies ran while one was open for 0% -> 0% of each run, Pallas kernels for 41% -> 39%
where the time goes in v3:
time: 59.3 us; the launch traced here: 59.1 us
  Pallas kernels  24 us (40%)
  starting transfers between devices  23.5 us (40%)
  waiting for transfers between devices  9.38 us (16%)
  other arithmetic  1.12 us (2%)
  between operations  0.96 us (2%)
    ppermute x16, starting transfers between devices, swap(): return lax.ppermute(x, axis, [(i, i ^ mask) for i in range(size)])  23.5 us
    pallas_call x1, Pallas kernels, partials(): pl.pallas_call(functools.partial(partial_kernel, p, groups, wide, tall),...  19.2 us
    ppermute x16, waiting for transfers between devices, swap(): return lax.ppermute(x, axis, [(i, i ^ mask) for i in range(size)])  9.38 us
    pallas_call x1, Pallas kernels, graph_rows(): pl.pallas_call(functools.partial(graph_kernel, p, piece), in_specs=[smem]...  2.32 us
    pallas_call x1, Pallas kernels, first_half(): pl.pallas_call(functools.partial(first_kernel, p), in_specs=[vmem] * (len...  1.57 us
  transfers between devices with their start and end apart: 16, of which 5 were waited for; matrix products, arithmetic and copies ran while one was open for 0% of the time, Pallas kernels for 39%

profile of v3, /device:TPU:1, one launch (start us, length us, event | category | flops | bytes accessed | tf_op | source)
XLA Modules:
  0.0 59.1 jit_solution(7695135202595093945)
XLA Ops:
  0.7 4.2 %collective-permute-start.2 = (f32[64,768]{1,0:T(8,128)}, f32[64,768]{1,0:T(8,128)S(1)}, u32[]{:S(2)}, u32[]{:S(2)}) collective-permute-start(f32[64,768]{1,0:T(8,128)} %bitcast.8), channel_id=1, source_target_pairs={{0,24},{8,16},{16,8},{24,0},{1,25},{9,17},{17,9},{25,1},{2,26},{10... | collective-permute-start | bytes 589832 | tf_op jit(solution)/shard_map/ppermute | solution.py:440
  4.9 0.0 collective-permute-start.1
  4.9 0.4 collective-permute-start
  5.2 19.2 %partials.1 = (f32[768,128]{1,0:T(8,128)}, f32[768,128]{1,0:T(8,128)}) custom-call(f32[768,64,128]{2,1,0:T(8,128)} %x_hbm.1, f32[64,32,64]{2,1,0:T(8,128)} %bitcast.13, f32[64,768]{1,0:T(8,128)} %bitcast.11, f32[64,128]{1,0:T(8,128)} %bitcast.15, f32[32,64]{1,0:T(8,128)} %bitcast.17), custom_call_target="tpu_custom_call" | custom-call | flops 4831838208 | bytes 25165824 | tf_op jit(solution)/shard_map/partials/pallas_call | solution.py:246
  24.4 0.0 collective-permute-done.2.refs_3_
  24.4 0.0 collective-permute-done.refs_1_
  24.4 1.3 %collective-permute-start.3 = (f32[768,128]{1,0:T(8,128)}, f32[768,128]{1,0:T(8,128)S(1)}, u32[]{:S(2)}, u32[]{:S(2)}) collective-permute-start(f32[768,128]{1,0:T(8,128)} %get-tuple-element.22), channel_id=1, source_target_pairs={{0,1},{1,0},{2,3},{3,2},{4,5},{5,4},{6,7},{7,6},{8,9},{9,8},{10,11... | collective-permute-start | bytes 1179656 | tf_op jit(solution)/shard_map/ppermute | solution.py:440
  25.7 1.6 %collective-permute-done.3 = f32[768,128]{1,0:T(8,128)S(1)} collective-permute-done((f32[768,128]{1,0:T(8,128)}, f32[768,128]{1,0:T(8,128)S(1)}, u32[]{:S(2)}, u32[]{:S(2)}) %collective-permute-start.3) | collective-permute-done | bytes 393248 | tf_op jit(solution)/shard_map/ppermute | solution.py:440
  27.3 1.1 %add.18 = f32[768,128]{1,0:T(8,128)S(1)} add(f32[768,128]{1,0:T(8,128)} %get-tuple-element.21, f32[768,128]{1,0:T(8,128)S(1)} %collective-permute-done.3) | non-fusion elementwise | flops 98304 | bytes 1179648 | tf_op jit(solution)/shard_map/add | solution.py:456
  28.4 1.4 %collective-permute-start.4 = (f32[184,128]{1,0:T(8,128)S(1)}, f32[184,128]{1,0:T(8,128)S(1)}, u32[]{:S(2)}, u32[]{:S(2)}) collective-permute-start(f32[184,128]{1,0:T(8,128)S(1)} %get-tuple-element.34), channel_id=1, source_target_pairs={{0,2},{2,0},{4,6},{6,4},{1,3},{3,1},{5,7},{7,5},{8,10},{10,8},{12,... | collective-permute-start | bytes 282632 | tf_op jit(solution)/shard_map/ppermute | solution.py:440
  29.8 1.2 %collective-permute-start.6 = (f32[184,128]{1,0:T(8,128)S(1)}, f32[184,128]{1,0:T(8,128)S(1)}, u32[]{:S(2)}, u32[]{:S(2)}) collective-permute-start(f32[184,128]{1,0:T(8,128)S(1)} %get-tuple-element.35), channel_id=1, source_target_pairs={{0,6},{2,4},{4,2},{6,0},{1,7},{3,5},{5,3},{7,1},{8,14},{10,12},{12... | collective-permute-start | bytes 282632 | tf_op jit(solution)/shard_map/ppermute | solution.py:440
  31.0 0.1 collective-permute-start.5
  31.1 0.1 copy.13.ids
  31.2 2.3 %graph.1.refs_5_ = f32[64,96]{1,0:T(8,128)S(1)} custom-call(s32[6,4]{1,0:T(8,128)S(1)} %copy.13.ids, s32[6,4,128,128]{3,2,1,0:T(8,128)S(1)} %copy-done, f32[64,768]{1,0:T(8,128)S(1)} %bitcast.12, f32[64,768]{1,0:T(8,128)S(1)} %collective-permute-done.refs_1_, f32[64,768]{1,0:T(8,128)S(1)} %collective-permute-done.1.refs_2_, ...), custom_call_target="tpu_custom_call" | custom-call | flops 100000000 | bytes 1000000 | tf_op jit(solution)/shard_map/graph/pallas_call | solution.py:338
  33.5 0.0 collective-permute-done.4
  33.5 1.9 %collective-permute-done.6 = f32[184,128]{1,0:T(8,128)S(1)} collective-permute-done((f32[184,128]{1,0:T(8,128)S(1)}, f32[184,128]{1,0:T(8,128)S(1)}, u32[]{:S(2)}, u32[]{:S(2)}) %collective-permute-start.6) | collective-permute-done | bytes 94240 | tf_op jit(solution)/shard_map/ppermute | solution.py:440
  35.5 1.4 %collective-permute-done.5 = f32[184,128]{1,0:T(8,128)S(1)} collective-permute-done((f32[184,128]{1,0:T(8,128)S(1)}, f32[184,128]{1,0:T(8,128)S(1)}, u32[]{:S(2)}, u32[]{:S(2)}) %collective-permute-start.5) | collective-permute-done | bytes 94240 | tf_op jit(solution)/shard_map/ppermute | solution.py:440
  36.9 1.0 %collective-permute-start.7 = (f32[168,128]{1,0:T(8,128)S(1)}, f32[168,128]{1,0:T(8,128)S(1)}, u32[]{:S(2)}, u32[]{:S(2)}) collective-permute-start(f32[168,128]{1,0:T(8,128)S(1)} %pad_maximum_fusion), channel_id=1, source_target_pairs={{0,8},{8,0},{16,24},{24,16},{1,9},{9,1},{17,25},{25,17},{2,10},{10... | collective-permute-start | bytes 258056 | tf_op jit(solution)/shard_map/ppermute | solution.py:440
  38.0 2.4 %collective-permute-done.7 = f32[168,128]{1,0:T(8,128)S(1)} collective-permute-done((f32[168,128]{1,0:T(8,128)S(1)}, f32[168,128]{1,0:T(8,128)S(1)}, u32[]{:S(2)}, u32[]{:S(2)}) %collective-permute-start.7) | collective-permute-done | bytes 86048 | tf_op jit(solution)/shard_map/ppermute | solution.py:440
  40.3 2.2 %collective-permute-start.8 = (f32[168,128]{1,0:T(8,128)S(1)}, f32[168,128]{1,0:T(8,128)S(1)}, u32[]{:S(2)}, u32[]{:S(2)}) collective-permute-start(f32[168,128]{1,0:T(8,128)S(1)} %fusion.2), channel_id=1, source_target_pairs={{0,16},{8,24},{16,0},{24,8},{1,17},{9,25},{17,1},{25,9},{2,18},{10... | collective-permute-start | bytes 258056 | tf_op jit(solution)/shard_map/ppermute | solution.py:440
  42.6 2.1 %collective-permute-done.8 = f32[168,128]{1,0:T(8,128)S(1)} collective-permute-done((f32[168,128]{1,0:T(8,128)S(1)}, f32[168,128]{1,0:T(8,128)S(1)}, u32[]{:S(2)}, u32[]{:S(2)}) %collective-permute-start.8) | collective-permute-done | bytes 86048 | tf_op jit(solution)/shard_map/ppermute | solution.py:440
  44.7 1.2 %collective-permute-start.14 = (f32[136,128]{1,0:T(8,128)S(1)}, f32[136,128]{1,0:T(8,128)S(1)}, u32[]{:S(2)}, u32[]{:S(2)}) collective-permute-start(f32[136,128]{1,0:T(8,128)S(1)} %slice.39), channel_id=1, source_target_pairs={{0,6},{2,4},{4,2},{6,0},{1,7},{3,5},{5,3},{7,1},{8,14},{10,12},{12... | collective-permute-start | bytes 208904 | tf_op jit(solution)/shard_map/ppermute | solution.py:440
  45.9 1.2 %collective-permute-start.12 = (f32[136,128]{1,0:T(8,128)S(1)}, f32[136,128]{1,0:T(8,128)S(1)}, u32[]{:S(2)}, u32[]{:S(2)}) collective-permute-start(f32[136,128]{1,0:T(8,128)S(1)} %slice.39), channel_id=1, source_target_pairs={{0,4},{2,6},{4,0},{6,2},{1,5},{3,7},{5,1},{7,3},{8,12},{10,14},{12... | collective-permute-start | bytes 208904 | tf_op jit(solution)/shard_map/ppermute | solution.py:440
  47.1 0.3 collective-permute-start.10
  47.4 5.2 %collective-permute-start.9 = (f32[168,128]{1,0:T(8,128)S(1)}, f32[168,128]{1,0:T(8,128)S(1)}, u32[]{:S(2)}, u32[]{:S(2)}) collective-permute-start(f32[168,128]{1,0:T(8,128)S(1)} %add.23.refs_0_), channel_id=1, source_target_pairs={{0,1},{1,0},{2,3},{3,2},{4,5},{5,4},{6,7},{7,6},{8,9},{9,8},{10,11... | collective-permute-start | bytes 258056 | tf_op jit(solution)/shard_map/ppermute | solution.py:440
  52.6 0.0 collective-permute-done.14.refs_3_
  52.6 1.7 %collective-permute-start.15 = (f32[136,128]{1,0:T(8,128)S(1)}, f32[136,128]{1,0:T(8,128)S(1)}, u32[]{:S(2)}, u32[]{:S(2)}) collective-permute-start(f32[136,128]{1,0:T(8,128)S(1)} %collective-permute-done.14.refs_3_), channel_id=1, source_target_pairs={{0,1},{1,0},{2,3},{3,2},{4,5},{5,4},{6,7},{7,6},{8,9},{9,8},{10,11... | collective-permute-start | bytes 208904 | tf_op jit(solution)/shard_map/ppermute | solution.py:440
  54.4 0.7 %collective-permute-start.13 = (f32[136,128]{1,0:T(8,128)S(1)}, f32[136,128]{1,0:T(8,128)S(1)}, u32[]{:S(2)}, u32[]{:S(2)}) collective-permute-start(f32[136,128]{1,0:T(8,128)S(1)} %collective-permute-done.12.refs_2_), channel_id=1, source_target_pairs={{0,1},{1,0},{2,3},{3,2},{4,5},{5,4},{6,7},{7,6},{8,9},{9,8},{10,11... | collective-permute-start | bytes 208904 | tf_op jit(solution)/shard_map/ppermute | solution.py:440
  55.1 0.0 collective-permute-done.10.refs_1_
  55.1 1.3 %collective-permute-start.11 = (f32[136,128]{1,0:T(8,128)S(1)}, f32[136,128]{1,0:T(8,128)S(1)}, u32[]{:S(2)}, u32[]{:S(2)}) collective-permute-start(f32[136,128]{1,0:T(8,128)S(1)} %collective-permute-done.10.refs_1_), channel_id=1, source_target_pairs={{0,1},{1,0},{2,3},{3,2},{4,5},{5,4},{6,7},{7,6},{8,9},{9,8},{10,11... | collective-permute-start | bytes 208904 | tf_op jit(solution)/shard_map/ppermute | solution.py:440
  56.4 1.6 %first_half.1 = (f32[64,32,64]{2,1,0:T(8,128)}, f32[64,128]{1,0:T(8,128)}, f32[64,96]{1,0:T(8,128)}, f32[32,64]{1,0:T(8,128)}) custom-call(f32[168,128]{1,0:T(8,128)S(1)} %add.23.refs_0_, f32[136,128]{1,0:T(8,128)S(1)} %collective-permute-done.10.refs_1_, f32[136,128]{1,0:T(8,128)S(1)} %collective-permute-done.12.refs_2_, ...), custom_call_target="tpu_custom_call" | custom-call | flops 1000000 | bytes 1000000 | tf_op jit(solution)/shard_map/first_half/pallas_call | solution.py:408
  58.0 1.0 %second_half.1 = (f32[64,32,64]{2,1,0:T(8,128)}, f32[64,128]{1,0:T(8,128)}) custom-call(f32[168,128]{1,0:T(8,128)S(1)} %collective-permute-done.9.refs_0_, f32[136,128]{1,0:T(8,128)S(1)} %collective-permute-done.11.refs_1_, f32[136,128]{1,0:T(8,128)S(1)} %collective-permute-done.13.refs_2_, ...), custom_call_target="tpu_custom_call", output_to_operand_aliasing={{0}: (4, {}), {1}: (5, {})} | custom-call | flops 1000000 | bytes 1000000 | tf_op jit(solution)/shard_map/second_half/pallas_call | solution.py:426
  (21 shorter events, 0.1 us)
Async XLA Ops:
  0.6 30.6 %copy-start.1 = (f32[768,64]{0,1:T(8,128)S(1)}, f32[768,64]{0,1:T(8,128)}, u32[]{:S(2)}) copy-start(f32[768,64]{0,1:T(8,128)} %param.9) | copy-start | bytes 589828
  0.6 30.5 %copy-start.2 = (s32[6,4]{0,1:T(4,128)S(1)}, s32[6,4]{0,1:T(4,128)}, u32[]{:S(2)}) copy-start(s32[6,4]{0,1:T(4,128)} %param.12) | copy-start | bytes 292
  0.7 30.5 %copy-start = (s32[6,4,128,128]{3,2,1,0:T(8,128)S(1)}, s32[6,4,128,128]{3,2,1,0:T(8,128)}, u32[]{:S(2)}) copy-start(s32[6,4,128,128]{3,2,1,0:T(8,128)} %edges.1) | copy-start | bytes 4718596
  0.7 23.7 %collective-permute-start.2 = (f32[64,768]{1,0:T(8,128)}, f32[64,768]{1,0:T(8,128)S(1)}, u32[]{:S(2)}, u32[]{:S(2)}) collective-permute-start(f32[64,768]{1,0:T(8,128)} %bitcast.8), channel_id=1, source_target_pairs={{0,24},{8,16},{16,8},{24,0},{1,25},{9,17},{17,9},{25,1},{2,26},{10... | collective-permute-start | bytes 589832 | tf_op jit(solution)/shard_map/ppermute | solution.py:440
  4.9 19.5 %collective-permute-start.1 = (f32[64,768]{1,0:T(8,128)}, f32[64,768]{1,0:T(8,128)S(1)}, u32[]{:S(2)}, u32[]{:S(2)}) collective-permute-start(f32[64,768]{1,0:T(8,128)} %bitcast.9), channel_id=1, source_target_pairs={{0,16},{8,24},{16,0},{24,8},{1,17},{9,25},{17,1},{25,9},{2,18},{10... | collective-permute-start | bytes 589832 | tf_op jit(solution)/shard_map/ppermute | solution.py:440
  4.9 19.5 %collective-permute-start = (f32[64,768]{1,0:T(8,128)}, f32[64,768]{1,0:T(8,128)S(1)}, u32[]{:S(2)}, u32[]{:S(2)}) collective-permute-start(f32[64,768]{1,0:T(8,128)} %bitcast.10), channel_id=1, source_target_pairs={{0,8},{8,0},{16,24},{24,16},{1,9},{9,1},{17,25},{25,17},{2,10},{10... | collective-permute-start | bytes 589832 | tf_op jit(solution)/shard_map/ppermute | solution.py:440
  24.4 2.9 %collective-permute-start.3 = (f32[768,128]{1,0:T(8,128)}, f32[768,128]{1,0:T(8,128)S(1)}, u32[]{:S(2)}, u32[]{:S(2)}) collective-permute-start(f32[768,128]{1,0:T(8,128)} %get-tuple-element.22), channel_id=1, source_target_pairs={{0,1},{1,0},{2,3},{3,2},{4,5},{5,4},{6,7},{7,6},{8,9},{9,8},{10,11... | collective-permute-start | bytes 1179656 | tf_op jit(solution)/shard_map/ppermute | solution.py:440
  28.4 5.2 %collective-permute-start.4 = (f32[184,128]{1,0:T(8,128)S(1)}, f32[184,128]{1,0:T(8,128)S(1)}, u32[]{:S(2)}, u32[]{:S(2)}) collective-permute-start(f32[184,128]{1,0:T(8,128)S(1)} %get-tuple-element.34), channel_id=1, source_target_pairs={{0,2},{2,0},{4,6},{6,4},{1,3},{3,1},{5,7},{7,5},{8,10},{10,8},{12,... | collective-permute-start | bytes 282632 | tf_op jit(solution)/shard_map/ppermute | solution.py:440
  29.8 5.7 %collective-permute-start.6 = (f32[184,128]{1,0:T(8,128)S(1)}, f32[184,128]{1,0:T(8,128)S(1)}, u32[]{:S(2)}, u32[]{:S(2)}) collective-permute-start(f32[184,128]{1,0:T(8,128)S(1)} %get-tuple-element.35), channel_id=1, source_target_pairs={{0,6},{2,4},{4,2},{6,0},{1,7},{3,5},{5,3},{7,1},{8,14},{10,12},{12... | collective-permute-start | bytes 282632 | tf_op jit(solution)/shard_map/ppermute | solution.py:440
  31.0 5.9 %collective-permute-start.5 = (f32[184,128]{1,0:T(8,128)S(1)}, f32[184,128]{1,0:T(8,128)S(1)}, u32[]{:S(2)}, u32[]{:S(2)}) collective-permute-start(f32[184,128]{1,0:T(8,128)S(1)} %get-tuple-element.36), channel_id=1, source_target_pairs={{0,4},{2,6},{4,0},{6,2},{1,5},{3,7},{5,1},{7,3},{8,12},{10,14},{12... | collective-permute-start | bytes 282632 | tf_op jit(solution)/shard_map/ppermute | solution.py:440
  36.9 3.4 %collective-permute-start.7 = (f32[168,128]{1,0:T(8,128)S(1)}, f32[168,128]{1,0:T(8,128)S(1)}, u32[]{:S(2)}, u32[]{:S(2)}) collective-permute-start(f32[168,128]{1,0:T(8,128)S(1)} %pad_maximum_fusion), channel_id=1, source_target_pairs={{0,8},{8,0},{16,24},{24,16},{1,9},{9,1},{17,25},{25,17},{2,10},{10... | collective-permute-start | bytes 258056 | tf_op jit(solution)/shard_map/ppermute | solution.py:440
  40.3 4.3 %collective-permute-start.8 = (f32[168,128]{1,0:T(8,128)S(1)}, f32[168,128]{1,0:T(8,128)S(1)}, u32[]{:S(2)}, u32[]{:S(2)}) collective-permute-start(f32[168,128]{1,0:T(8,128)S(1)} %fusion.2), channel_id=1, source_target_pairs={{0,16},{8,24},{16,0},{24,8},{1,17},{9,25},{17,1},{25,9},{2,18},{10... | collective-permute-start | bytes 258056 | tf_op jit(solution)/shard_map/ppermute | solution.py:440
  44.7 7.9 %collective-permute-start.14 = (f32[136,128]{1,0:T(8,128)S(1)}, f32[136,128]{1,0:T(8,128)S(1)}, u32[]{:S(2)}, u32[]{:S(2)}) collective-permute-start(f32[136,128]{1,0:T(8,128)S(1)} %slice.39), channel_id=1, source_target_pairs={{0,6},{2,4},{4,2},{6,0},{1,7},{3,5},{5,3},{7,1},{8,14},{10,12},{12... | collective-permute-start | bytes 208904 | tf_op jit(solution)/shard_map/ppermute | solution.py:440
  45.9 8.5 %collective-permute-start.12 = (f32[136,128]{1,0:T(8,128)S(1)}, f32[136,128]{1,0:T(8,128)S(1)}, u32[]{:S(2)}, u32[]{:S(2)}) collective-permute-start(f32[136,128]{1,0:T(8,128)S(1)} %slice.39), channel_id=1, source_target_pairs={{0,4},{2,6},{4,0},{6,2},{1,5},{3,7},{5,1},{7,3},{8,12},{10,14},{12... | collective-permute-start | bytes 208904 | tf_op jit(solution)/shard_map/ppermute | solution.py:440
  47.1 7.9 %collective-permute-start.10 = (f32[136,128]{1,0:T(8,128)S(1)}, f32[136,128]{1,0:T(8,128)S(1)}, u32[]{:S(2)}, u32[]{:S(2)}) collective-permute-start(f32[136,128]{1,0:T(8,128)S(1)} %slice.39), channel_id=1, source_target_pairs={{0,2},{2,0},{4,6},{6,4},{1,3},{3,1},{5,7},{7,5},{8,10},{10,8},{12,... | collective-permute-start | bytes 208904 | tf_op jit(solution)/shard_map/ppermute | solution.py:440
  47.4 10.6 %collective-permute-start.9 = (f32[168,128]{1,0:T(8,128)S(1)}, f32[168,128]{1,0:T(8,128)S(1)}, u32[]{:S(2)}, u32[]{:S(2)}) collective-permute-start(f32[168,128]{1,0:T(8,128)S(1)} %add.23.refs_0_), channel_id=1, source_target_pairs={{0,1},{1,0},{2,3},{3,2},{4,5},{5,4},{6,7},{7,6},{8,9},{9,8},{10,11... | collective-permute-start | bytes 258056 | tf_op jit(solution)/shard_map/ppermute | solution.py:440
  52.6 5.4 %collective-permute-start.15 = (f32[136,128]{1,0:T(8,128)S(1)}, f32[136,128]{1,0:T(8,128)S(1)}, u32[]{:S(2)}, u32[]{:S(2)}) collective-permute-start(f32[136,128]{1,0:T(8,128)S(1)} %collective-permute-done.14.refs_3_), channel_id=1, source_target_pairs={{0,1},{1,0},{2,3},{3,2},{4,5},{5,4},{6,7},{7,6},{8,9},{9,8},{10,11... | collective-permute-start | bytes 208904 | tf_op jit(solution)/shard_map/ppermute | solution.py:440
  54.4 3.6 %collective-permute-start.13 = (f32[136,128]{1,0:T(8,128)S(1)}, f32[136,128]{1,0:T(8,128)S(1)}, u32[]{:S(2)}, u32[]{:S(2)}) collective-permute-start(f32[136,128]{1,0:T(8,128)S(1)} %collective-permute-done.12.refs_2_), channel_id=1, source_target_pairs={{0,1},{1,0},{2,3},{3,2},{4,5},{5,4},{6,7},{7,6},{8,9},{9,8},{10,11... | collective-permute-start | bytes 208904 | tf_op jit(solution)/shard_map/ppermute | solution.py:440
  55.1 2.9 %collective-permute-start.11 = (f32[136,128]{1,0:T(8,128)S(1)}, f32[136,128]{1,0:T(8,128)S(1)}, u32[]{:S(2)}, u32[]{:S(2)}) collective-permute-start(f32[136,128]{1,0:T(8,128)S(1)} %collective-permute-done.10.refs_1_), channel_id=1, source_target_pairs={{0,1},{1,0},{2,3},{3,2},{4,5},{5,4},{6,7},{7,6},{8,9},{9,8},{10,11... | collective-permute-start | bytes 208904 | tf_op jit(solution)/shard_map/ppermute | solution.py:440

commit v4 on v3

--- a/solution.py
+++ b/solution.py
@@ -118,7 +118,7 @@
     sensor_s[0:r1, :] = sensor_h
     sensor_s[r1 : 2 * r1, :] = sensor_l
     gram_h, gram_l = split(dot3((sensor_h, sensor_l), (sensor_h, sensor_l), NT))
-    gram_twice = jnp.concatenate([gram_h, gram_h], axis=1)
+    gram = jnp.concatenate([gram_h, gram_h, gram_l], axis=1)
 
     small[3].wait()
     for first in range(0, p.pairs, p.pairs_part):
@@ -153,7 +153,7 @@
     def read(step, place):
         lanes = slice(place * p.chans, place * p.chans + width)
         g_hl = g_parts[:, step * width : (step + 1) * width]
-        folded = dot(gram_twice, g_hl) + dot(gram_l, g_hl[:r1])
+        folded = dot(gram, jnp.concatenate([g_hl, g_hl[:r1]], axis=0))
         g = g_both[step * width : (step + 1) * width, :]
         for i in range(0, p.sensors, tall):
             x_h, x_l = split(buf[i : i + tall, lanes])
@@ -172,7 +172,8 @@
         inner = inner[:, : 2 * r2] + inner[:, 2 * r2 :] + dot(f_l, rows_h)
         for h in range(count):
             inner_ref[pl.ds(first + h, p.pairs, stride=p.times), :] = inner[h * p.pairs : (h + 1) * p.pairs]
-        return chan_sum + dot3(ct_rows(first, count), (f_h, f_l), TN)
+        ct_h, ct_l = (c.T for c in ct_rows(first, count))
+        return chan_sum + dot3((ct_h, ct_l), (f_h, f_l))
 
     for first in range(0, p.times, BEFORE):
         before(first, BEFORE)
@@ -436,6 +437,21 @@
     )(*arrays, core_t, chan_t)
 
 
+def settle(x):
+    def body(x_ref, out):
+        out[...] = x_ref[...]
+
+    return pl.pallas_call(
+        body,
+        in_specs=[vmem],
+        out_specs=vmem,
+        out_shape=jax.ShapeDtypeStruct(x.shape, x.dtype),
+        compiler_params=pltpu.CompilerParams(vmem_limit_bytes=4 * 2**20),
+        cost_estimate=pl.CostEstimate(flops=10**5, bytes_accessed=10**6, transcendentals=0),
+        name="settle",
+    )(x)
+
+
 def swap(x, axis, size, mask):
     return lax.ppermute(x, axis, [(i, i ^ mask) for i in range(size)])
 
@@ -453,16 +469,21 @@
         p, tensor, core.transpose(0, 2, 1), sensor_factor.T, channel_factor.T, time_factor.T
     )
     keep, send, *shards = lax.optimization_barrier((keep, send, *shards))
-    held = keep + swap(send, "tm", n_time, 1)
-    total = held[: p.chunk]
+    held = settle(keep) + swap(send, "tm", n_time, 1)
+    total = held[: p.sum_rows]
     for m in range(1, n_channel):
-        total = total + swap(held[m * p.chunk : (m + 1) * p.chunk], "channel", n_channel, m)
+        at = m * p.chunk
+        total = total + swap(held[at : at + p.sum_rows], "channel", n_channel, m)
     graph = graph_rows(p, neighbour_ids, edge_weights, sensor_factor.T, *shards)
-    total, graph = lax.optimization_barrier((total, graph))
-    fit = total[p.sum_rows :]
-    total = jnp.concatenate([total[: p.sum_rows], held[n_channel * p.chunk :]], axis=0)
+    total, graph, held = lax.optimization_barrier((total, graph, held))
+    fit = held[p.sum_rows : p.chunk]
+    for m in range(1, n_channel):
+        at = m * p.chunk
+        fit = fit + swap(held[at + p.sum_rows : at + p.chunk], "channel", n_channel, m)
+    total = jnp.concatenate([total, held[n_channel * p.chunk :]], axis=0)
     for n in range(n_sensor.bit_length() - 1):
         total = total + swap(total, "sensor", n_sensor, 1 << n)
+    total, fit = lax.optimization_barrier((total, fit))
     others = [
         swap(total[: p.sum_rows], "channel", n_channel, m) for m in range(1, n_channel)
     ]

time: 59.3 us -> 57 us (0.961)
  waiting for transfers between devices: 9.38 us -> 5.93 us
  starting transfers between devices: 23.5 us -> 24.9 us
  other arithmetic: 1.12 us -> 0.11 us
  local copies, waits for them, and re-layouts: 0.14 us -> 1.13 us
    ppermute x16 -> x19, waiting for transfers between devices: 9.38 us -> 5.93 us  [swap(): return lax.ppermute(x, axis, [(i, i ^ mask) for i in range(size)])]
    ppermute x16 -> x19, starting transfers between devices: 23.5 us -> 24.9 us  [swap(): return lax.ppermute(x, axis, [(i, i ^ mask) for i in range(size)])]
    add x2 -> x3, other arithmetic: 1.08 us -> 0.08 us  [the longest x1 0.04 us: on_device(): held = settle(keep) + swap(send, 'tm', n_time, 1)]
    unnamed x7 -> x9, local copies, waits for them, and re-layouts: 0.1 us -> 1.1 us
  transfers between devices with their start and end apart: 16 -> 19, of which waited for: 5 -> 4; matrix products, arithmetic and copies ran while one was open for 0% -> 0% of each run, Pallas kernels for 39% -> 40%
where the time goes in v4:
time: 57 us; the launch traced here: 56.9 us
  starting transfers between devices  24.9 us (44%)
  Pallas kernels  23.8 us (42%)
  waiting for transfers between devices  5.93 us (10%)
  local copies, waits for them, and re-layouts  1.13 us (2%)
  between operations  0.97 us (2%)
    ppermute x19, starting transfers between devices, swap(): return lax.ppermute(x, axis, [(i, i ^ mask) for i in range(size)])  24.9 us
    pallas_call x1, Pallas kernels, partials(): pl.pallas_call(functools.partial(partial_kernel, p, groups, wide, tall),...  19 us
    ppermute x19, waiting for transfers between devices, swap(): return lax.ppermute(x, axis, [(i, i ^ mask) for i in range(size)])  5.93 us
    pallas_call x1, Pallas kernels, graph_rows(): pl.pallas_call(functools.partial(graph_kernel, p, piece), in_specs=[smem]...  2.32 us
    pallas_call x1, Pallas kernels, first_half(): pl.pallas_call(functools.partial(first_kernel, p), in_specs=[vmem] * (len...  1.57 us
  transfers between devices with their start and end apart: 19, of which 4 were waited for; matrix products, arithmetic and copies ran while one was open for 0% of the time, Pallas kernels for 40%

profile of v4, /device:TPU:1, one launch (start us, length us, event | category | flops | bytes accessed | tf_op | source)
XLA Modules:
  0.0 56.9 jit_solution(14814860445108819273)
XLA Ops:
  0.7 4.2 %collective-permute-start.2 = (f32[64,768]{1,0:T(8,128)}, f32[64,768]{1,0:T(8,128)S(1)}, u32[]{:S(2)}, u32[]{:S(2)}) collective-permute-start(f32[64,768]{1,0:T(8,128)} %bitcast.8), channel_id=1, source_target_pairs={{0,24},{8,16},{16,8},{24,0},{1,25},{9,17},{17,9},{25,1},{2,26},{10... | collective-permute-start | bytes 589832 | tf_op jit(solution)/shard_map/ppermute | solution.py:456
  4.9 0.4 collective-permute-start
  5.2 19.0 %partials.1 = (f32[768,128]{1,0:T(8,128)}, f32[768,128]{1,0:T(8,128)}) custom-call(f32[768,64,128]{2,1,0:T(8,128)} %x_hbm.1, f32[64,32,64]{2,1,0:T(8,128)} %bitcast.13, f32[64,768]{1,0:T(8,128)} %bitcast.11, f32[64,128]{1,0:T(8,128)} %bitcast.15, f32[32,64]{1,0:T(8,128)} %bitcast.17), custom_call_target="tpu_custom_call" | custom-call | flops 4831838208 | bytes 25165824 | tf_op jit(solution)/shard_map/partials/pallas_call | solution.py:247
  24.2 0.0 collective-permute-done.2.refs_3_
  24.2 0.0 collective-permute-done.1.refs_2_
  24.3 1.3 %collective-permute-start.3 = (f32[768,128]{1,0:T(8,128)}, f32[768,128]{1,0:T(8,128)S(1)}, u32[]{:S(2)}, u32[]{:S(2)}) collective-permute-start(f32[768,128]{1,0:T(8,128)} %get-tuple-element.25), channel_id=1, source_target_pairs={{0,1},{1,0},{2,3},{3,2},{4,5},{5,4},{6,7},{7,6},{8,9},{9,8},{10,11... | collective-permute-start | bytes 1179656 | tf_op jit(solution)/shard_map/ppermute | solution.py:456
  25.6 1.0 %copy-done.2 = f32[768,128]{1,0:T(8,128)S(1)} copy-done((f32[768,128]{1,0:T(8,128)S(1)}, f32[768,128]{1,0:T(8,128)}, u32[]{:S(2)}) %copy-start.2) | copy-done | bytes 393240
  26.6 0.5 collective-permute-done.3
  27.2 1.4 %collective-permute-start.4 = (f32[136,128]{1,0:T(8,128)S(1)}, f32[136,128]{1,0:T(8,128)S(1)}, u32[]{:S(2)}, u32[]{:S(2)}) collective-permute-start(f32[136,128]{1,0:T(8,128)S(1)} %get-tuple-element.43), channel_id=1, source_target_pairs={{0,2},{2,0},{4,6},{6,4},{1,3},{3,1},{5,7},{7,5},{8,10},{10,8},{12,... | collective-permute-start | bytes 208904 | tf_op jit(solution)/shard_map/ppermute | solution.py:456
  28.6 1.2 %collective-permute-start.6 = (f32[136,128]{1,0:T(8,128)S(1)}, f32[136,128]{1,0:T(8,128)S(1)}, u32[]{:S(2)}, u32[]{:S(2)}) collective-permute-start(f32[136,128]{1,0:T(8,128)S(1)} %get-tuple-element.44), channel_id=1, source_target_pairs={{0,6},{2,4},{4,2},{6,0},{1,7},{3,5},{5,3},{7,1},{8,14},{10,12},{12... | collective-permute-start | bytes 208904 | tf_op jit(solution)/shard_map/ppermute | solution.py:456
  29.8 0.1 collective-permute-start.5
  29.9 0.1 copy.13.ids
  30.0 2.3 %graph.1.refs_5_ = f32[64,96]{1,0:T(8,128)S(1)} custom-call(s32[6,4]{1,0:T(8,128)S(1)} %copy.13.ids, s32[6,4,128,128]{3,2,1,0:T(8,128)S(1)} %copy-done, f32[64,768]{1,0:T(8,128)S(1)} %bitcast.12, f32[64,768]{1,0:T(8,128)S(1)} %collective-permute-done.refs_1_, f32[64,768]{1,0:T(8,128)S(1)} %collective-permute-done.1.refs_2_, ...), custom_call_target="tpu_custom_call" | custom-call | flops 100000000 | bytes 1000000 | tf_op jit(solution)/shard_map/graph/pallas_call | solution.py:339
  32.3 0.0 collective-permute-done.4
  32.3 1.1 %collective-permute-done.6 = f32[136,128]{1,0:T(8,128)S(1)} collective-permute-done((f32[136,128]{1,0:T(8,128)S(1)}, f32[136,128]{1,0:T(8,128)S(1)}, u32[]{:S(2)}, u32[]{:S(2)}) %collective-permute-start.6) | collective-permute-done | bytes 69664 | tf_op jit(solution)/shard_map/ppermute | solution.py:456
  33.4 1.5 %collective-permute-done.5 = f32[136,128]{1,0:T(8,128)S(1)} collective-permute-done((f32[136,128]{1,0:T(8,128)S(1)}, f32[136,128]{1,0:T(8,128)S(1)}, u32[]{:S(2)}, u32[]{:S(2)}) %collective-permute-start.5) | collective-permute-done | bytes 69664 | tf_op jit(solution)/shard_map/ppermute | solution.py:456
  35.0 1.0 %collective-permute-start.7 = (f32[168,128]{1,0:T(8,128)S(1)}, f32[168,128]{1,0:T(8,128)S(1)}, u32[]{:S(2)}, u32[]{:S(2)}) collective-permute-start(f32[168,128]{1,0:T(8,128)S(1)} %pad_maximum_fusion), channel_id=1, source_target_pairs={{0,8},{8,0},{16,24},{24,16},{1,9},{9,1},{17,25},{25,17},{2,10},{10... | collective-permute-start | bytes 258056 | tf_op jit(solution)/shard_map/ppermute | solution.py:456
  36.0 0.8 %collective-permute-start.9 = (f32[48,128]{1,0:T(8,128)S(1)}, f32[48,128]{1,0:T(8,128)S(1)}, u32[]{:S(2)}, u32[]{:S(2)}) collective-permute-start(f32[48,128]{1,0:T(8,128)S(1)} %get-tuple-element.40), channel_id=1, source_target_pairs={{0,2},{2,0},{4,6},{6,4},{1,3},{3,1},{5,7},{7,5},{8,10},{10,8},{12,... | collective-permute-start | bytes 73736 | tf_op jit(solution)/shard_map/ppermute | solution.py:456
  36.8 0.4 collective-permute-start.11
  37.2 1.5 %collective-permute-start.10 = (f32[48,128]{1,0:T(8,128)S(1)}, f32[48,128]{1,0:T(8,128)S(1)}, u32[]{:S(2)}, u32[]{:S(2)}) collective-permute-start(f32[48,128]{1,0:T(8,128)S(1)} %get-tuple-element.42), channel_id=1, source_target_pairs={{0,4},{2,6},{4,0},{6,2},{1,5},{3,7},{5,1},{7,3},{8,12},{10,14},{12... | collective-permute-start | bytes 73736 | tf_op jit(solution)/shard_map/ppermute | solution.py:456
  38.7 0.0 collective-permute-done.7
  38.7 2.7 %collective-permute-start.8 = (f32[168,128]{1,0:T(8,128)S(1)}, f32[168,128]{1,0:T(8,128)S(1)}, u32[]{:S(2)}, u32[]{:S(2)}) collective-permute-start(f32[168,128]{1,0:T(8,128)S(1)} %fusion.2), channel_id=1, source_target_pairs={{0,16},{8,24},{16,0},{24,8},{1,17},{9,25},{17,1},{25,9},{2,18},{10... | collective-permute-start | bytes 258056 | tf_op jit(solution)/shard_map/ppermute | solution.py:456
  41.4 2.8 %collective-permute-done.8 = f32[168,128]{1,0:T(8,128)S(1)} collective-permute-done((f32[168,128]{1,0:T(8,128)S(1)}, f32[168,128]{1,0:T(8,128)S(1)}, u32[]{:S(2)}, u32[]{:S(2)}) %collective-permute-start.8) | collective-permute-done | bytes 86048 | tf_op jit(solution)/shard_map/ppermute | solution.py:456
  44.2 1.2 %collective-permute-start.17 = (f32[136,128]{1,0:T(8,128)S(1)}, f32[136,128]{1,0:T(8,128)S(1)}, u32[]{:S(2)}, u32[]{:S(2)}) collective-permute-start(f32[136,128]{1,0:T(8,128)S(1)} %slice.41), channel_id=1, source_target_pairs={{0,6},{2,4},{4,2},{6,0},{1,7},{3,5},{5,3},{7,1},{8,14},{10,12},{12... | collective-permute-start | bytes 208904 | tf_op jit(solution)/shard_map/ppermute | solution.py:456
  45.4 0.9 %collective-permute-start.15 = (f32[136,128]{1,0:T(8,128)S(1)}, f32[136,128]{1,0:T(8,128)S(1)}, u32[]{:S(2)}, u32[]{:S(2)}) collective-permute-start(f32[136,128]{1,0:T(8,128)S(1)} %slice.41), channel_id=1, source_target_pairs={{0,4},{2,6},{4,0},{6,2},{1,5},{3,7},{5,1},{7,3},{8,12},{10,14},{12... | collective-permute-start | bytes 208904 | tf_op jit(solution)/shard_map/ppermute | solution.py:456
  46.3 0.6 %collective-permute-start.13 = (f32[136,128]{1,0:T(8,128)S(1)}, f32[136,128]{1,0:T(8,128)S(1)}, u32[]{:S(2)}, u32[]{:S(2)}) collective-permute-start(f32[136,128]{1,0:T(8,128)S(1)} %slice.41), channel_id=1, source_target_pairs={{0,2},{2,0},{4,6},{6,4},{1,3},{3,1},{5,7},{7,5},{8,10},{10,8},{12,... | collective-permute-start | bytes 208904 | tf_op jit(solution)/shard_map/ppermute | solution.py:456
  46.9 3.6 %collective-permute-start.12 = (f32[168,128]{1,0:T(8,128)S(1)}, f32[168,128]{1,0:T(8,128)S(1)}, u32[]{:S(2)}, u32[]{:S(2)}) collective-permute-start(f32[168,128]{1,0:T(8,128)S(1)} %add.32.refs_0_), channel_id=1, source_target_pairs={{0,1},{1,0},{2,3},{3,2},{4,5},{5,4},{6,7},{7,6},{8,9},{9,8},{10,11... | collective-permute-start | bytes 258056 | tf_op jit(solution)/shard_map/ppermute | solution.py:456
  50.6 1.7 %collective-permute-start.18 = (f32[136,128]{1,0:T(8,128)S(1)}, f32[136,128]{1,0:T(8,128)S(1)}, u32[]{:S(2)}, u32[]{:S(2)}) collective-permute-start(f32[136,128]{1,0:T(8,128)S(1)} %collective-permute-done.17.refs_3_), channel_id=1, source_target_pairs={{0,1},{1,0},{2,3},{3,2},{4,5},{5,4},{6,7},{7,6},{8,9},{9,8},{10,11... | collective-permute-start | bytes 208904 | tf_op jit(solution)/shard_map/ppermute | solution.py:456
  52.3 0.7 %collective-permute-start.16 = (f32[136,128]{1,0:T(8,128)S(1)}, f32[136,128]{1,0:T(8,128)S(1)}, u32[]{:S(2)}, u32[]{:S(2)}) collective-permute-start(f32[136,128]{1,0:T(8,128)S(1)} %collective-permute-done.15.refs_2_), channel_id=1, source_target_pairs={{0,1},{1,0},{2,3},{3,2},{4,5},{5,4},{6,7},{7,6},{8,9},{9,8},{10,11... | collective-permute-start | bytes 208904 | tf_op jit(solution)/shard_map/ppermute | solution.py:456
  53.0 1.1 %collective-permute-start.14 = (f32[136,128]{1,0:T(8,128)S(1)}, f32[136,128]{1,0:T(8,128)S(1)}, u32[]{:S(2)}, u32[]{:S(2)}) collective-permute-start(f32[136,128]{1,0:T(8,128)S(1)} %collective-permute-done.13.refs_1_), channel_id=1, source_target_pairs={{0,1},{1,0},{2,3},{3,2},{4,5},{5,4},{6,7},{7,6},{8,9},{9,8},{10,11... | collective-permute-start | bytes 208904 | tf_op jit(solution)/shard_map/ppermute | solution.py:456
  54.1 1.6 %first_half.1 = (f32[64,32,64]{2,1,0:T(8,128)}, f32[64,128]{1,0:T(8,128)}, f32[64,96]{1,0:T(8,128)}, f32[32,64]{1,0:T(8,128)}) custom-call(f32[168,128]{1,0:T(8,128)S(1)} %add.32.refs_0_, f32[136,128]{1,0:T(8,128)S(1)} %collective-permute-done.13.refs_1_, f32[136,128]{1,0:T(8,128)S(1)} %collective-permute-done.15.refs_2_, ...), custom_call_target="tpu_custom_call" | custom-call | flops 1000000 | bytes 1000000 | tf_op jit(solution)/shard_map/first_half/pallas_call | solution.py:409
  55.7 1.0 %second_half.1 = (f32[64,32,64]{2,1,0:T(8,128)}, f32[64,128]{1,0:T(8,128)}) custom-call(f32[168,128]{1,0:T(8,128)S(1)} %collective-permute-done.12.refs_0_, f32[136,128]{1,0:T(8,128)S(1)} %collective-permute-done.14.refs_1_, f32[136,128]{1,0:T(8,128)S(1)} %collective-permute-done.16.refs_2_, ...), custom_call_target="tpu_custom_call", output_to_operand_aliasing={{0}: (4, {}), {1}: (5, {})} | custom-call | flops 1000000 | bytes 1000000 | tf_op jit(solution)/shard_map/second_half/pallas_call | solution.py:427
  (30 shorter events, 0.2 us)
Async XLA Ops:
  0.6 29.4 %copy-start.1 = (f32[768,64]{0,1:T(8,128)S(1)}, f32[768,64]{0,1:T(8,128)}, u32[]{:S(2)}) copy-start(f32[768,64]{0,1:T(8,128)} %param.9) | copy-start | bytes 589828
  0.6 29.3 %copy-start.3 = (s32[6,4]{0,1:T(4,128)S(1)}, s32[6,4]{0,1:T(4,128)}, u32[]{:S(2)}) copy-start(s32[6,4]{0,1:T(4,128)} %param.12) | copy-start | bytes 292
  0.7 29.4 %copy-start = (s32[6,4,128,128]{3,2,1,0:T(8,128)S(1)}, s32[6,4,128,128]{3,2,1,0:T(8,128)}, u32[]{:S(2)}) copy-start(s32[6,4,128,128]{3,2,1,0:T(8,128)} %edges.1) | copy-start | bytes 4718596
  0.7 23.6 %collective-permute-start.2 = (f32[64,768]{1,0:T(8,128)}, f32[64,768]{1,0:T(8,128)S(1)}, u32[]{:S(2)}, u32[]{:S(2)}) collective-permute-start(f32[64,768]{1,0:T(8,128)} %bitcast.8), channel_id=1, source_target_pairs={{0,24},{8,16},{16,8},{24,0},{1,25},{9,17},{17,9},{25,1},{2,26},{10... | collective-permute-start | bytes 589832 | tf_op jit(solution)/shard_map/ppermute | solution.py:456
  4.9 19.4 %collective-permute-start.1 = (f32[64,768]{1,0:T(8,128)}, f32[64,768]{1,0:T(8,128)S(1)}, u32[]{:S(2)}, u32[]{:S(2)}) collective-permute-start(f32[64,768]{1,0:T(8,128)} %bitcast.9), channel_id=1, source_target_pairs={{0,16},{8,24},{16,0},{24,8},{1,17},{9,25},{17,1},{25,9},{2,18},{10... | collective-permute-start | bytes 589832 | tf_op jit(solution)/shard_map/ppermute | solution.py:456
  4.9 19.4 %collective-permute-start = (f32[64,768]{1,0:T(8,128)}, f32[64,768]{1,0:T(8,128)S(1)}, u32[]{:S(2)}, u32[]{:S(2)}) collective-permute-start(f32[64,768]{1,0:T(8,128)} %bitcast.10), channel_id=1, source_target_pairs={{0,8},{8,0},{16,24},{24,16},{1,9},{9,1},{17,25},{25,17},{2,10},{10... | collective-permute-start | bytes 589832 | tf_op jit(solution)/shard_map/ppermute | solution.py:456
  24.3 2.9 %collective-permute-start.3 = (f32[768,128]{1,0:T(8,128)}, f32[768,128]{1,0:T(8,128)S(1)}, u32[]{:S(2)}, u32[]{:S(2)}) collective-permute-start(f32[768,128]{1,0:T(8,128)} %get-tuple-element.25), channel_id=1, source_target_pairs={{0,1},{1,0},{2,3},{3,2},{4,5},{5,4},{6,7},{7,6},{8,9},{9,8},{10,11... | collective-permute-start | bytes 1179656 | tf_op jit(solution)/shard_map/ppermute | solution.py:456
  25.6 1.0 %copy-start.2 = (f32[768,128]{1,0:T(8,128)S(1)}, f32[768,128]{1,0:T(8,128)}, u32[]{:S(2)}) copy-start(f32[768,128]{1,0:T(8,128)} %get-tuple-element.24.x_ref) | copy-start | bytes 1179652
  27.2 5.1 %collective-permute-start.4 = (f32[136,128]{1,0:T(8,128)S(1)}, f32[136,128]{1,0:T(8,128)S(1)}, u32[]{:S(2)}, u32[]{:S(2)}) collective-permute-start(f32[136,128]{1,0:T(8,128)S(1)} %get-tuple-element.43), channel_id=1, source_target_pairs={{0,2},{2,0},{4,6},{6,4},{1,3},{3,1},{5,7},{7,5},{8,10},{10,8},{12,... | collective-permute-start | bytes 208904 | tf_op jit(solution)/shard_map/ppermute | solution.py:456
  28.6 4.8 %collective-permute-start.6 = (f32[136,128]{1,0:T(8,128)S(1)}, f32[136,128]{1,0:T(8,128)S(1)}, u32[]{:S(2)}, u32[]{:S(2)}) collective-permute-start(f32[136,128]{1,0:T(8,128)S(1)} %get-tuple-element.44), channel_id=1, source_target_pairs={{0,6},{2,4},{4,2},{6,0},{1,7},{3,5},{5,3},{7,1},{8,14},{10,12},{12... | collective-permute-start | bytes 208904 | tf_op jit(solution)/shard_map/ppermute | solution.py:456
  29.8 5.1 %collective-permute-start.5 = (f32[136,128]{1,0:T(8,128)S(1)}, f32[136,128]{1,0:T(8,128)S(1)}, u32[]{:S(2)}, u32[]{:S(2)}) collective-permute-start(f32[136,128]{1,0:T(8,128)S(1)} %get-tuple-element.45), channel_id=1, source_target_pairs={{0,4},{2,6},{4,0},{6,2},{1,5},{3,7},{5,1},{7,3},{8,12},{10,14},{12... | collective-permute-start | bytes 208904 | tf_op jit(solution)/shard_map/ppermute | solution.py:456
  35.0 3.7 %collective-permute-start.7 = (f32[168,128]{1,0:T(8,128)S(1)}, f32[168,128]{1,0:T(8,128)S(1)}, u32[]{:S(2)}, u32[]{:S(2)}) collective-permute-start(f32[168,128]{1,0:T(8,128)S(1)} %pad_maximum_fusion), channel_id=1, source_target_pairs={{0,8},{8,0},{16,24},{24,16},{1,9},{9,1},{17,25},{25,17},{2,10},{10... | collective-permute-start | bytes 258056 | tf_op jit(solution)/shard_map/ppermute | solution.py:456
  36.0 5.4 %collective-permute-start.9 = (f32[48,128]{1,0:T(8,128)S(1)}, f32[48,128]{1,0:T(8,128)S(1)}, u32[]{:S(2)}, u32[]{:S(2)}) collective-permute-start(f32[48,128]{1,0:T(8,128)S(1)} %get-tuple-element.40), channel_id=1, source_target_pairs={{0,2},{2,0},{4,6},{6,4},{1,3},{3,1},{5,7},{7,5},{8,10},{10,8},{12,... | collective-permute-start | bytes 73736 | tf_op jit(solution)/shard_map/ppermute | solution.py:456
  36.8 4.6 %collective-permute-start.11 = (f32[48,128]{1,0:T(8,128)S(1)}, f32[48,128]{1,0:T(8,128)S(1)}, u32[]{:S(2)}, u32[]{:S(2)}) collective-permute-start(f32[48,128]{1,0:T(8,128)S(1)} %get-tuple-element.41), channel_id=1, source_target_pairs={{0,6},{2,4},{4,2},{6,0},{1,7},{3,5},{5,3},{7,1},{8,14},{10,12},{12... | collective-permute-start | bytes 73736 | tf_op jit(solution)/shard_map/ppermute | solution.py:456
  37.2 4.2 %collective-permute-start.10 = (f32[48,128]{1,0:T(8,128)S(1)}, f32[48,128]{1,0:T(8,128)S(1)}, u32[]{:S(2)}, u32[]{:S(2)}) collective-permute-start(f32[48,128]{1,0:T(8,128)S(1)} %get-tuple-element.42), channel_id=1, source_target_pairs={{0,4},{2,6},{4,0},{6,2},{1,5},{3,7},{5,1},{7,3},{8,12},{10,14},{12... | collective-permute-start | bytes 73736 | tf_op jit(solution)/shard_map/ppermute | solution.py:456
  38.7 5.5 %collective-permute-start.8 = (f32[168,128]{1,0:T(8,128)S(1)}, f32[168,128]{1,0:T(8,128)S(1)}, u32[]{:S(2)}, u32[]{:S(2)}) collective-permute-start(f32[168,128]{1,0:T(8,128)S(1)} %fusion.2), channel_id=1, source_target_pairs={{0,16},{8,24},{16,0},{24,8},{1,17},{9,25},{17,1},{25,9},{2,18},{10... | collective-permute-start | bytes 258056 | tf_op jit(solution)/shard_map/ppermute | solution.py:456
  44.2 6.4 %collective-permute-start.17 = (f32[136,128]{1,0:T(8,128)S(1)}, f32[136,128]{1,0:T(8,128)S(1)}, u32[]{:S(2)}, u32[]{:S(2)}) collective-permute-start(f32[136,128]{1,0:T(8,128)S(1)} %slice.41), channel_id=1, source_target_pairs={{0,6},{2,4},{4,2},{6,0},{1,7},{3,5},{5,3},{7,1},{8,14},{10,12},{12... | collective-permute-start | bytes 208904 | tf_op jit(solution)/shard_map/ppermute | solution.py:456
  45.4 6.9 %collective-permute-start.15 = (f32[136,128]{1,0:T(8,128)S(1)}, f32[136,128]{1,0:T(8,128)S(1)}, u32[]{:S(2)}, u32[]{:S(2)}) collective-permute-start(f32[136,128]{1,0:T(8,128)S(1)} %slice.41), channel_id=1, source_target_pairs={{0,4},{2,6},{4,0},{6,2},{1,5},{3,7},{5,1},{7,3},{8,12},{10,14},{12... | collective-permute-start | bytes 208904 | tf_op jit(solution)/shard_map/ppermute | solution.py:456
  46.3 6.7 %collective-permute-start.13 = (f32[136,128]{1,0:T(8,128)S(1)}, f32[136,128]{1,0:T(8,128)S(1)}, u32[]{:S(2)}, u32[]{:S(2)}) collective-permute-start(f32[136,128]{1,0:T(8,128)S(1)} %slice.41), channel_id=1, source_target_pairs={{0,2},{2,0},{4,6},{6,4},{1,3},{3,1},{5,7},{7,5},{8,10},{10,8},{12,... | collective-permute-start | bytes 208904 | tf_op jit(solution)/shard_map/ppermute | solution.py:456
  46.9 8.8 %collective-permute-start.12 = (f32[168,128]{1,0:T(8,128)S(1)}, f32[168,128]{1,0:T(8,128)S(1)}, u32[]{:S(2)}, u32[]{:S(2)}) collective-permute-start(f32[168,128]{1,0:T(8,128)S(1)} %add.32.refs_0_), channel_id=1, source_target_pairs={{0,1},{1,0},{2,3},{3,2},{4,5},{5,4},{6,7},{7,6},{8,9},{9,8},{10,11... | collective-permute-start | bytes 258056 | tf_op jit(solution)/shard_map/ppermute | solution.py:456
  50.6 5.1 %collective-permute-start.18 = (f32[136,128]{1,0:T(8,128)S(1)}, f32[136,128]{1,0:T(8,128)S(1)}, u32[]{:S(2)}, u32[]{:S(2)}) collective-permute-start(f32[136,128]{1,0:T(8,128)S(1)} %collective-permute-done.17.refs_3_), channel_id=1, source_target_pairs={{0,1},{1,0},{2,3},{3,2},{4,5},{5,4},{6,7},{7,6},{8,9},{9,8},{10,11... | collective-permute-start | bytes 208904 | tf_op jit(solution)/shard_map/ppermute | solution.py:456
  52.3 3.4 %collective-permute-start.16 = (f32[136,128]{1,0:T(8,128)S(1)}, f32[136,128]{1,0:T(8,128)S(1)}, u32[]{:S(2)}, u32[]{:S(2)}) collective-permute-start(f32[136,128]{1,0:T(8,128)S(1)} %collective-permute-done.15.refs_2_), channel_id=1, source_target_pairs={{0,1},{1,0},{2,3},{3,2},{4,5},{5,4},{6,7},{7,6},{8,9},{9,8},{10,11... | collective-permute-start | bytes 208904 | tf_op jit(solution)/shard_map/ppermute | solution.py:456
  53.0 2.7 %collective-permute-start.14 = (f32[136,128]{1,0:T(8,128)S(1)}, f32[136,128]{1,0:T(8,128)S(1)}, u32[]{:S(2)}, u32[]{:S(2)}) collective-permute-start(f32[136,128]{1,0:T(8,128)S(1)} %collective-permute-done.13.refs_1_), channel_id=1, source_target_pairs={{0,1},{1,0},{2,3},{3,2},{4,5},{5,4},{6,7},{7,6},{8,9},{9,8},{10,11... | collective-permute-start | bytes 208904 | tf_op jit(solution)/shard_map/ppermute | solution.py:456

commit v5 on v4

--- a/solution.py
+++ b/solution.py
@@ -381,9 +381,8 @@
 
 def first_kernel(p, *refs):
     arrays, refs = refs[: p.n_channel], refs[p.n_channel :]
-    fit, graph, core_out, chan_out, sensor_out, time_out, core_buf, sem = refs
+    core_out, chan_out, time_out, core_buf, sem = refs
     copies = put_half(p, 0, arrays, core_out, chan_out, core_buf, sem)
-    sensor_out[...] = halves(fit[...]).T + graph[...]
     for m in range(p.n_channel):
         quarter = lax.bitwise_xor(lax.axis_index("channel"), m)
         start = pl.multiple_of(quarter * p.time_rows, 8)
@@ -405,22 +404,36 @@
     ]
 
 
-def first_half(p, fit, graph, *arrays):
+def sensor_rows(fit, graph):
+    def body(fit_ref, graph_ref, out):
+        out[...] = halves(fit_ref[...]).T + graph_ref[...]
+
+    return pl.pallas_call(
+        body,
+        in_specs=[vmem] * 2,
+        out_specs=vmem,
+        out_shape=jax.ShapeDtypeStruct(graph.shape, f32),
+        compiler_params=pltpu.CompilerParams(vmem_limit_bytes=4 * 2**20),
+        cost_estimate=pl.CostEstimate(flops=10**5, bytes_accessed=10**5, transcendentals=0),
+        name="sensor_rows",
+    )(fit, graph)
+
+
+def first_half(p, *arrays):
     return pl.pallas_call(
         functools.partial(first_kernel, p),
-        in_specs=[vmem] * (len(arrays) + 2),
-        out_specs=[anywhere] * 2 + [vmem] * 2,
+        in_specs=[vmem] * len(arrays),
+        out_specs=[anywhere] * 2 + [vmem],
         out_shape=[
             jax.ShapeDtypeStruct((p.r1, p.r3, p.r2), f32),
             jax.ShapeDtypeStruct((p.r2, p.chans), f32),
-            jax.ShapeDtypeStruct((p.r1, p.share), f32),
             jax.ShapeDtypeStruct((p.r3, p.times), f32),
         ],
         scratch_shapes=half_scratch(p),
         compiler_params=pltpu.CompilerParams(vmem_limit_bytes=8 * 2**20),
         cost_estimate=pl.CostEstimate(flops=10**6, bytes_accessed=10**6, transcendentals=0),
         name="first_half",
-    )(*arrays, fit, graph)
+    )(*arrays)
 
 
 def second_half(p, core_t, chan_t, *arrays):
@@ -483,12 +496,12 @@
     total = jnp.concatenate([total, held[n_channel * p.chunk :]], axis=0)
     for n in range(n_sensor.bit_length() - 1):
         total = total + swap(total, "sensor", n_sensor, 1 << n)
-    total, fit = lax.optimization_barrier((total, fit))
+    total, sensor_t = lax.optimization_barrier((total, sensor_rows(fit, graph)))
     others = [
         swap(total[: p.sum_rows], "channel", n_channel, m) for m in range(1, n_channel)
     ]
     far = [swap(x, "tm", n_time, 1) for x in (total, *others)]
-    core_t, chan_t, sensor_t, time_t = first_half(p, fit, graph, total, *others)
+    core_t, chan_t, time_t = first_half(p, total, *others)
     core_t, chan_t = second_half(p, core_t, chan_t, *far)
     return (core_t.transpose(0, 2, 1), sensor_t.T, chan_t.T, time_t.T)
 

time: 57 us -> 57 us (level)
  Pallas kernels: 23.8 us -> 24.6 us
  waiting for transfers between devices: 5.93 us -> 5.18 us
    ppermute x19, waiting for transfers between devices: 5.93 us -> 5.18 us  [swap(): return lax.ppermute(x, axis, [(i, i ^ mask) for i in range(size)])]
    pallas_call x1 -> x2, Pallas kernels: 1.57 us -> 2.31 us  [the longest x1 1.55 us: first_half(): pl.pallas_call(functools.partial(first_kernel, p), in_specs=[vmem] * len(...]
  transfers between devices with their start and end apart: 19 -> 19, of which waited for: 4 -> 4; matrix products, arithmetic and copies ran while one was open for 0% -> 0% of each run, Pallas kernels for 40% -> 42%
where the time goes in v5:
time: 57 us; the launch traced here: 56.8 us
  starting transfers between devices  24.9 us (44%)
  Pallas kernels  24.6 us (43%)
  waiting for transfers between devices  5.18 us (9%)
  local copies, waits for them, and re-layouts  1.13 us (2%)
  between operations  0.97 us (2%)
    ppermute x19, starting transfers between devices, swap(): return lax.ppermute(x, axis, [(i, i ^ mask) for i in range(size)])  24.9 us
    pallas_call x1, Pallas kernels, partials(): pl.pallas_call(functools.partial(partial_kernel, p, groups, wide, tall),...  19 us
    ppermute x19, waiting for transfers between devices, swap(): return lax.ppermute(x, axis, [(i, i ^ mask) for i in range(size)])  5.18 us
    pallas_call x1, Pallas kernels, graph_rows(): pl.pallas_call(functools.partial(graph_kernel, p, piece), in_specs=[smem]...  2.32 us
    pallas_call x1, Pallas kernels, first_half(): pl.pallas_call(functools.partial(first_kernel, p), in_specs=[vmem] * len(...  1.55 us
  transfers between devices with their start and end apart: 19, of which 4 were waited for; matrix products, arithmetic and copies ran while one was open for 0% of the time, Pallas kernels for 42%

profile of v5, /device:TPU:1, one launch (start us, length us, event | category | flops | bytes accessed | tf_op | source)
XLA Modules:
  0.0 56.8 jit_solution(12545183802123837347)
XLA Ops:
  0.7 4.2 %collective-permute-start.2 = (f32[64,768]{1,0:T(8,128)}, f32[64,768]{1,0:T(8,128)S(1)}, u32[]{:S(2)}, u32[]{:S(2)}) collective-permute-start(f32[64,768]{1,0:T(8,128)} %bitcast.8), channel_id=1, source_target_pairs={{0,24},{8,16},{16,8},{24,0},{1,25},{9,17},{17,9},{25,1},{2,26},{10... | collective-permute-start | bytes 589832 | tf_op jit(solution)/shard_map/ppermute | solution.py:469
  4.9 0.4 collective-permute-start
  5.2 19.0 %partials.1 = (f32[768,128]{1,0:T(8,128)}, f32[768,128]{1,0:T(8,128)}) custom-call(f32[768,64,128]{2,1,0:T(8,128)} %x_hbm.1, f32[64,32,64]{2,1,0:T(8,128)} %bitcast.13, f32[64,768]{1,0:T(8,128)} %bitcast.11, f32[64,128]{1,0:T(8,128)} %bitcast.15, f32[32,64]{1,0:T(8,128)} %bitcast.18), custom_call_target="tpu_custom_call" | custom-call | flops 4831838208 | bytes 25165824 | tf_op jit(solution)/shard_map/partials/pallas_call | solution.py:247
  24.2 0.0 collective-permute-done.2.refs_3_
  24.2 0.0 collective-permute-done.1.refs_2_
  24.3 1.3 %collective-permute-start.3 = (f32[768,128]{1,0:T(8,128)}, f32[768,128]{1,0:T(8,128)S(1)}, u32[]{:S(2)}, u32[]{:S(2)}) collective-permute-start(f32[768,128]{1,0:T(8,128)} %get-tuple-element.24), channel_id=1, source_target_pairs={{0,1},{1,0},{2,3},{3,2},{4,5},{5,4},{6,7},{7,6},{8,9},{9,8},{10,11... | collective-permute-start | bytes 1179656 | tf_op jit(solution)/shard_map/ppermute | solution.py:469
  25.6 1.0 %copy-done.2 = f32[768,128]{1,0:T(8,128)S(1)} copy-done((f32[768,128]{1,0:T(8,128)S(1)}, f32[768,128]{1,0:T(8,128)}, u32[]{:S(2)}) %copy-start.2) | copy-done | bytes 393240
  26.6 0.5 collective-permute-done.3
  27.2 1.4 %collective-permute-start.4 = (f32[136,128]{1,0:T(8,128)S(1)}, f32[136,128]{1,0:T(8,128)S(1)}, u32[]{:S(2)}, u32[]{:S(2)}) collective-permute-start(f32[136,128]{1,0:T(8,128)S(1)} %get-tuple-element.41), channel_id=1, source_target_pairs={{0,2},{2,0},{4,6},{6,4},{1,3},{3,1},{5,7},{7,5},{8,10},{10,8},{12,... | collective-permute-start | bytes 208904 | tf_op jit(solution)/shard_map/ppermute | solution.py:469
  28.6 1.2 %collective-permute-start.6 = (f32[136,128]{1,0:T(8,128)S(1)}, f32[136,128]{1,0:T(8,128)S(1)}, u32[]{:S(2)}, u32[]{:S(2)}) collective-permute-start(f32[136,128]{1,0:T(8,128)S(1)} %get-tuple-element.42), channel_id=1, source_target_pairs={{0,6},{2,4},{4,2},{6,0},{1,7},{3,5},{5,3},{7,1},{8,14},{10,12},{12... | collective-permute-start | bytes 208904 | tf_op jit(solution)/shard_map/ppermute | solution.py:469
  29.8 0.1 collective-permute-start.5
  29.9 0.1 copy.13.ids
  30.0 2.3 %graph.1.graph_ref = f32[64,96]{1,0:T(8,128)S(1)} custom-call(s32[6,4]{1,0:T(8,128)S(1)} %copy.13.ids, s32[6,4,128,128]{3,2,1,0:T(8,128)S(1)} %copy-done, f32[64,768]{1,0:T(8,128)S(1)} %bitcast.12, f32[64,768]{1,0:T(8,128)S(1)} %collective-permute-done.refs_1_, f32[64,768]{1,0:T(8,128)S(1)} %collective-permute-done.1.refs_2_, ...), custom_call_target="tpu_custom_call" | custom-call | flops 100000000 | bytes 1000000 | tf_op jit(solution)/shard_map/graph/pallas_call | solution.py:339
  32.3 0.0 collective-permute-done.4
  32.3 1.1 %collective-permute-done.6 = f32[136,128]{1,0:T(8,128)S(1)} collective-permute-done((f32[136,128]{1,0:T(8,128)S(1)}, f32[136,128]{1,0:T(8,128)S(1)}, u32[]{:S(2)}, u32[]{:S(2)}) %collective-permute-start.6) | collective-permute-done | bytes 69664 | tf_op jit(solution)/shard_map/ppermute | solution.py:469
  33.4 1.5 %collective-permute-done.5 = f32[136,128]{1,0:T(8,128)S(1)} collective-permute-done((f32[136,128]{1,0:T(8,128)S(1)}, f32[136,128]{1,0:T(8,128)S(1)}, u32[]{:S(2)}, u32[]{:S(2)}) %collective-permute-start.5) | collective-permute-done | bytes 69664 | tf_op jit(solution)/shard_map/ppermute | solution.py:469
  35.0 1.0 %collective-permute-start.7 = (f32[168,128]{1,0:T(8,128)S(1)}, f32[168,128]{1,0:T(8,128)S(1)}, u32[]{:S(2)}, u32[]{:S(2)}) collective-permute-start(f32[168,128]{1,0:T(8,128)S(1)} %pad_maximum_fusion), channel_id=1, source_target_pairs={{0,8},{8,0},{16,24},{24,16},{1,9},{9,1},{17,25},{25,17},{2,10},{10... | collective-permute-start | bytes 258056 | tf_op jit(solution)/shard_map/ppermute | solution.py:469
  36.0 0.8 %collective-permute-start.9 = (f32[48,128]{1,0:T(8,128)S(1)}, f32[48,128]{1,0:T(8,128)S(1)}, u32[]{:S(2)}, u32[]{:S(2)}) collective-permute-start(f32[48,128]{1,0:T(8,128)S(1)} %get-tuple-element.38), channel_id=1, source_target_pairs={{0,2},{2,0},{4,6},{6,4},{1,3},{3,1},{5,7},{7,5},{8,10},{10,8},{12,... | collective-permute-start | bytes 73736 | tf_op jit(solution)/shard_map/ppermute | solution.py:469
  36.8 0.4 collective-permute-start.11
  37.2 1.5 %collective-permute-start.10 = (f32[48,128]{1,0:T(8,128)S(1)}, f32[48,128]{1,0:T(8,128)S(1)}, u32[]{:S(2)}, u32[]{:S(2)}) collective-permute-start(f32[48,128]{1,0:T(8,128)S(1)} %get-tuple-element.40), channel_id=1, source_target_pairs={{0,4},{2,6},{4,0},{6,2},{1,5},{3,7},{5,1},{7,3},{8,12},{10,14},{12... | collective-permute-start | bytes 73736 | tf_op jit(solution)/shard_map/ppermute | solution.py:469
  38.7 2.7 %collective-permute-start.8 = (f32[168,128]{1,0:T(8,128)S(1)}, f32[168,128]{1,0:T(8,128)S(1)}, u32[]{:S(2)}, u32[]{:S(2)}) collective-permute-start(f32[168,128]{1,0:T(8,128)S(1)} %fusion.2), channel_id=1, source_target_pairs={{0,16},{8,24},{16,0},{24,8},{1,17},{9,25},{17,1},{25,9},{2,18},{10... | collective-permute-start | bytes 258056 | tf_op jit(solution)/shard_map/ppermute | solution.py:469
  41.4 0.8 %sensor_rows.1 = f32[64,96]{1,0:T(8,128)} custom-call(f32[48,128]{1,0:T(8,128)S(1)} %add_add_fusion.fit_ref, f32[64,96]{1,0:T(8,128)S(1)} %graph.1.graph_ref), custom_call_target="tpu_custom_call" | custom-call | flops 100000 | bytes 100000 | tf_op jit(solution)/shard_map/sensor_rows/pallas_call | solution.py:411
  42.2 2.0 %collective-permute-done.8 = f32[168,128]{1,0:T(8,128)S(1)} collective-permute-done((f32[168,128]{1,0:T(8,128)S(1)}, f32[168,128]{1,0:T(8,128)S(1)}, u32[]{:S(2)}, u32[]{:S(2)}) %collective-permute-start.8) | collective-permute-done | bytes 86048 | tf_op jit(solution)/shard_map/ppermute | solution.py:469
  44.2 1.2 %collective-permute-start.17 = (f32[136,128]{1,0:T(8,128)S(1)}, f32[136,128]{1,0:T(8,128)S(1)}, u32[]{:S(2)}, u32[]{:S(2)}) collective-permute-start(f32[136,128]{1,0:T(8,128)S(1)} %slice.41), channel_id=1, source_target_pairs={{0,6},{2,4},{4,2},{6,0},{1,7},{3,5},{5,3},{7,1},{8,14},{10,12},{12... | collective-permute-start | bytes 208904 | tf_op jit(solution)/shard_map/ppermute | solution.py:469
  45.4 0.9 %collective-permute-start.15 = (f32[136,128]{1,0:T(8,128)S(1)}, f32[136,128]{1,0:T(8,128)S(1)}, u32[]{:S(2)}, u32[]{:S(2)}) collective-permute-start(f32[136,128]{1,0:T(8,128)S(1)} %slice.41), channel_id=1, source_target_pairs={{0,4},{2,6},{4,0},{6,2},{1,5},{3,7},{5,1},{7,3},{8,12},{10,14},{12... | collective-permute-start | bytes 208904 | tf_op jit(solution)/shard_map/ppermute | solution.py:469
  46.3 0.6 %collective-permute-start.13 = (f32[136,128]{1,0:T(8,128)S(1)}, f32[136,128]{1,0:T(8,128)S(1)}, u32[]{:S(2)}, u32[]{:S(2)}) collective-permute-start(f32[136,128]{1,0:T(8,128)S(1)} %slice.41), channel_id=1, source_target_pairs={{0,2},{2,0},{4,6},{6,4},{1,3},{3,1},{5,7},{7,5},{8,10},{10,8},{12,... | collective-permute-start | bytes 208904 | tf_op jit(solution)/shard_map/ppermute | solution.py:469
  46.9 3.6 %collective-permute-start.12 = (f32[168,128]{1,0:T(8,128)S(1)}, f32[168,128]{1,0:T(8,128)S(1)}, u32[]{:S(2)}, u32[]{:S(2)}) collective-permute-start(f32[168,128]{1,0:T(8,128)S(1)} %add.32.refs_0_), channel_id=1, source_target_pairs={{0,1},{1,0},{2,3},{3,2},{4,5},{5,4},{6,7},{7,6},{8,9},{9,8},{10,11... | collective-permute-start | bytes 258056 | tf_op jit(solution)/shard_map/ppermute | solution.py:469
  50.6 1.7 %collective-permute-start.18 = (f32[136,128]{1,0:T(8,128)S(1)}, f32[136,128]{1,0:T(8,128)S(1)}, u32[]{:S(2)}, u32[]{:S(2)}) collective-permute-start(f32[136,128]{1,0:T(8,128)S(1)} %collective-permute-done.17.refs_3_), channel_id=1, source_target_pairs={{0,1},{1,0},{2,3},{3,2},{4,5},{5,4},{6,7},{7,6},{8,9},{9,8},{10,11... | collective-permute-start | bytes 208904 | tf_op jit(solution)/shard_map/ppermute | solution.py:469
  52.3 0.7 %collective-permute-start.16 = (f32[136,128]{1,0:T(8,128)S(1)}, f32[136,128]{1,0:T(8,128)S(1)}, u32[]{:S(2)}, u32[]{:S(2)}) collective-permute-start(f32[136,128]{1,0:T(8,128)S(1)} %collective-permute-done.15.refs_2_), channel_id=1, source_target_pairs={{0,1},{1,0},{2,3},{3,2},{4,5},{5,4},{6,7},{7,6},{8,9},{9,8},{10,11... | collective-permute-start | bytes 208904 | tf_op jit(solution)/shard_map/ppermute | solution.py:469
  53.0 1.1 %collective-permute-start.14 = (f32[136,128]{1,0:T(8,128)S(1)}, f32[136,128]{1,0:T(8,128)S(1)}, u32[]{:S(2)}, u32[]{:S(2)}) collective-permute-start(f32[136,128]{1,0:T(8,128)S(1)} %collective-permute-done.13.refs_1_), channel_id=1, source_target_pairs={{0,1},{1,0},{2,3},{3,2},{4,5},{5,4},{6,7},{7,6},{8,9},{9,8},{10,11... | collective-permute-start | bytes 208904 | tf_op jit(solution)/shard_map/ppermute | solution.py:469
  54.1 1.6 %first_half.1 = (f32[64,32,64]{2,1,0:T(8,128)}, f32[64,128]{1,0:T(8,128)}, f32[32,64]{1,0:T(8,128)}) custom-call(f32[168,128]{1,0:T(8,128)S(1)} %add.32.refs_0_, f32[136,128]{1,0:T(8,128)S(1)} %collective-permute-done.13.refs_1_, f32[136,128]{1,0:T(8,128)S(1)} %collective-permute-done.15.refs_2_, f32[136,128]{1,0:T(8,128)S(1)} %collective-permute-done.17.refs_3_), custom_call_target="tpu_custom_call" | custom-call | flops 1000000 | bytes 1000000 | tf_op jit(solution)/shard_map/first_half/pallas_call | solution.py:423
  55.7 1.0 %second_half.1 = (f32[64,32,64]{2,1,0:T(8,128)}, f32[64,128]{1,0:T(8,128)}) custom-call(f32[168,128]{1,0:T(8,128)S(1)} %collective-permute-done.12.refs_0_, f32[136,128]{1,0:T(8,128)S(1)} %collective-permute-done.14.refs_1_, f32[136,128]{1,0:T(8,128)S(1)} %collective-permute-done.16.refs_2_, ...), custom_call_target="tpu_custom_call", output_to_operand_aliasing={{0}: (4, {}), {1}: (5, {})} | custom-call | flops 1000000 | bytes 1000000 | tf_op jit(solution)/shard_map/second_half/pallas_call | solution.py:440
  (31 shorter events, 0.2 us)
Async XLA Ops:
  0.6 29.4 %copy-start.1 = (f32[768,64]{0,1:T(8,128)S(1)}, f32[768,64]{0,1:T(8,128)}, u32[]{:S(2)}) copy-start(f32[768,64]{0,1:T(8,128)} %param.9) | copy-start | bytes 589828
  0.6 29.3 %copy-start.3 = (s32[6,4]{0,1:T(4,128)S(1)}, s32[6,4]{0,1:T(4,128)}, u32[]{:S(2)}) copy-start(s32[6,4]{0,1:T(4,128)} %param.12) | copy-start | bytes 292
  0.7 29.4 %copy-start = (s32[6,4,128,128]{3,2,1,0:T(8,128)S(1)}, s32[6,4,128,128]{3,2,1,0:T(8,128)}, u32[]{:S(2)}) copy-start(s32[6,4,128,128]{3,2,1,0:T(8,128)} %edges.1) | copy-start | bytes 4718596
  0.7 23.6 %collective-permute-start.2 = (f32[64,768]{1,0:T(8,128)}, f32[64,768]{1,0:T(8,128)S(1)}, u32[]{:S(2)}, u32[]{:S(2)}) collective-permute-start(f32[64,768]{1,0:T(8,128)} %bitcast.8), channel_id=1, source_target_pairs={{0,24},{8,16},{16,8},{24,0},{1,25},{9,17},{17,9},{25,1},{2,26},{10... | collective-permute-start | bytes 589832 | tf_op jit(solution)/shard_map/ppermute | solution.py:469
  4.9 19.4 %collective-permute-start.1 = (f32[64,768]{1,0:T(8,128)}, f32[64,768]{1,0:T(8,128)S(1)}, u32[]{:S(2)}, u32[]{:S(2)}) collective-permute-start(f32[64,768]{1,0:T(8,128)} %bitcast.9), channel_id=1, source_target_pairs={{0,16},{8,24},{16,0},{24,8},{1,17},{9,25},{17,1},{25,9},{2,18},{10... | collective-permute-start | bytes 589832 | tf_op jit(solution)/shard_map/ppermute | solution.py:469
  4.9 19.4 %collective-permute-start = (f32[64,768]{1,0:T(8,128)}, f32[64,768]{1,0:T(8,128)S(1)}, u32[]{:S(2)}, u32[]{:S(2)}) collective-permute-start(f32[64,768]{1,0:T(8,128)} %bitcast.10), channel_id=1, source_target_pairs={{0,8},{8,0},{16,24},{24,16},{1,9},{9,1},{17,25},{25,17},{2,10},{10... | collective-permute-start | bytes 589832 | tf_op jit(solution)/shard_map/ppermute | solution.py:469
  24.3 2.9 %collective-permute-start.3 = (f32[768,128]{1,0:T(8,128)}, f32[768,128]{1,0:T(8,128)S(1)}, u32[]{:S(2)}, u32[]{:S(2)}) collective-permute-start(f32[768,128]{1,0:T(8,128)} %get-tuple-element.24), channel_id=1, source_target_pairs={{0,1},{1,0},{2,3},{3,2},{4,5},{5,4},{6,7},{7,6},{8,9},{9,8},{10,11... | collective-permute-start | bytes 1179656 | tf_op jit(solution)/shard_map/ppermute | solution.py:469
  25.6 1.0 %copy-start.2 = (f32[768,128]{1,0:T(8,128)S(1)}, f32[768,128]{1,0:T(8,128)}, u32[]{:S(2)}) copy-start(f32[768,128]{1,0:T(8,128)} %get-tuple-element.23.x_ref) | copy-start | bytes 1179652
  27.2 5.1 %collective-permute-start.4 = (f32[136,128]{1,0:T(8,128)S(1)}, f32[136,128]{1,0:T(8,128)S(1)}, u32[]{:S(2)}, u32[]{:S(2)}) collective-permute-start(f32[136,128]{1,0:T(8,128)S(1)} %get-tuple-element.41), channel_id=1, source_target_pairs={{0,2},{2,0},{4,6},{6,4},{1,3},{3,1},{5,7},{7,5},{8,10},{10,8},{12,... | collective-permute-start | bytes 208904 | tf_op jit(solution)/shard_map/ppermute | solution.py:469
  28.6 4.8 %collective-permute-start.6 = (f32[136,128]{1,0:T(8,128)S(1)}, f32[136,128]{1,0:T(8,128)S(1)}, u32[]{:S(2)}, u32[]{:S(2)}) collective-permute-start(f32[136,128]{1,0:T(8,128)S(1)} %get-tuple-element.42), channel_id=1, source_target_pairs={{0,6},{2,4},{4,2},{6,0},{1,7},{3,5},{5,3},{7,1},{8,14},{10,12},{12... | collective-permute-start | bytes 208904 | tf_op jit(solution)/shard_map/ppermute | solution.py:469
  29.8 5.1 %collective-permute-start.5 = (f32[136,128]{1,0:T(8,128)S(1)}, f32[136,128]{1,0:T(8,128)S(1)}, u32[]{:S(2)}, u32[]{:S(2)}) collective-permute-start(f32[136,128]{1,0:T(8,128)S(1)} %get-tuple-element.43), channel_id=1, source_target_pairs={{0,4},{2,6},{4,0},{6,2},{1,5},{3,7},{5,1},{7,3},{8,12},{10,14},{12... | collective-permute-start | bytes 208904 | tf_op jit(solution)/shard_map/ppermute | solution.py:469
  35.0 3.7 %collective-permute-start.7 = (f32[168,128]{1,0:T(8,128)S(1)}, f32[168,128]{1,0:T(8,128)S(1)}, u32[]{:S(2)}, u32[]{:S(2)}) collective-permute-start(f32[168,128]{1,0:T(8,128)S(1)} %pad_maximum_fusion), channel_id=1, source_target_pairs={{0,8},{8,0},{16,24},{24,16},{1,9},{9,1},{17,25},{25,17},{2,10},{10... | collective-permute-start | bytes 258056 | tf_op jit(solution)/shard_map/ppermute | solution.py:469
  36.0 5.4 %collective-permute-start.9 = (f32[48,128]{1,0:T(8,128)S(1)}, f32[48,128]{1,0:T(8,128)S(1)}, u32[]{:S(2)}, u32[]{:S(2)}) collective-permute-start(f32[48,128]{1,0:T(8,128)S(1)} %get-tuple-element.38), channel_id=1, source_target_pairs={{0,2},{2,0},{4,6},{6,4},{1,3},{3,1},{5,7},{7,5},{8,10},{10,8},{12,... | collective-permute-start | bytes 73736 | tf_op jit(solution)/shard_map/ppermute | solution.py:469
  36.8 4.6 %collective-permute-start.11 = (f32[48,128]{1,0:T(8,128)S(1)}, f32[48,128]{1,0:T(8,128)S(1)}, u32[]{:S(2)}, u32[]{:S(2)}) collective-permute-start(f32[48,128]{1,0:T(8,128)S(1)} %get-tuple-element.39), channel_id=1, source_target_pairs={{0,6},{2,4},{4,2},{6,0},{1,7},{3,5},{5,3},{7,1},{8,14},{10,12},{12... | collective-permute-start | bytes 73736 | tf_op jit(solution)/shard_map/ppermute | solution.py:469
  37.2 4.2 %collective-permute-start.10 = (f32[48,128]{1,0:T(8,128)S(1)}, f32[48,128]{1,0:T(8,128)S(1)}, u32[]{:S(2)}, u32[]{:S(2)}) collective-permute-start(f32[48,128]{1,0:T(8,128)S(1)} %get-tuple-element.40), channel_id=1, source_target_pairs={{0,4},{2,6},{4,0},{6,2},{1,5},{3,7},{5,1},{7,3},{8,12},{10,14},{12... | collective-permute-start | bytes 73736 | tf_op jit(solution)/shard_map/ppermute | solution.py:469
  38.7 5.5 %collective-permute-start.8 = (f32[168,128]{1,0:T(8,128)S(1)}, f32[168,128]{1,0:T(8,128)S(1)}, u32[]{:S(2)}, u32[]{:S(2)}) collective-permute-start(f32[168,128]{1,0:T(8,128)S(1)} %fusion.2), channel_id=1, source_target_pairs={{0,16},{8,24},{16,0},{24,8},{1,17},{9,25},{17,1},{25,9},{2,18},{10... | collective-permute-start | bytes 258056 | tf_op jit(solution)/shard_map/ppermute | solution.py:469
  44.2 6.4 %collective-permute-start.17 = (f32[136,128]{1,0:T(8,128)S(1)}, f32[136,128]{1,0:T(8,128)S(1)}, u32[]{:S(2)}, u32[]{:S(2)}) collective-permute-start(f32[136,128]{1,0:T(8,128)S(1)} %slice.41), channel_id=1, source_target_pairs={{0,6},{2,4},{4,2},{6,0},{1,7},{3,5},{5,3},{7,1},{8,14},{10,12},{12... | collective-permute-start | bytes 208904 | tf_op jit(solution)/shard_map/ppermute | solution.py:469
  45.4 6.9 %collective-permute-start.15 = (f32[136,128]{1,0:T(8,128)S(1)}, f32[136,128]{1,0:T(8,128)S(1)}, u32[]{:S(2)}, u32[]{:S(2)}) collective-permute-start(f32[136,128]{1,0:T(8,128)S(1)} %slice.41), channel_id=1, source_target_pairs={{0,4},{2,6},{4,0},{6,2},{1,5},{3,7},{5,1},{7,3},{8,12},{10,14},{12... | collective-permute-start | bytes 208904 | tf_op jit(solution)/shard_map/ppermute | solution.py:469
  46.3 6.7 %collective-permute-start.13 = (f32[136,128]{1,0:T(8,128)S(1)}, f32[136,128]{1,0:T(8,128)S(1)}, u32[]{:S(2)}, u32[]{:S(2)}) collective-permute-start(f32[136,128]{1,0:T(8,128)S(1)} %slice.41), channel_id=1, source_target_pairs={{0,2},{2,0},{4,6},{6,4},{1,3},{3,1},{5,7},{7,5},{8,10},{10,8},{12,... | collective-permute-start | bytes 208904 | tf_op jit(solution)/shard_map/ppermute | solution.py:469
  46.9 8.8 %collective-permute-start.12 = (f32[168,128]{1,0:T(8,128)S(1)}, f32[168,128]{1,0:T(8,128)S(1)}, u32[]{:S(2)}, u32[]{:S(2)}) collective-permute-start(f32[168,128]{1,0:T(8,128)S(1)} %add.32.refs_0_), channel_id=1, source_target_pairs={{0,1},{1,0},{2,3},{3,2},{4,5},{5,4},{6,7},{7,6},{8,9},{9,8},{10,11... | collective-permute-start | bytes 258056 | tf_op jit(solution)/shard_map/ppermute | solution.py:469
  50.6 5.1 %collective-permute-start.18 = (f32[136,128]{1,0:T(8,128)S(1)}, f32[136,128]{1,0:T(8,128)S(1)}, u32[]{:S(2)}, u32[]{:S(2)}) collective-permute-start(f32[136,128]{1,0:T(8,128)S(1)} %collective-permute-done.17.refs_3_), channel_id=1, source_target_pairs={{0,1},{1,0},{2,3},{3,2},{4,5},{5,4},{6,7},{7,6},{8,9},{9,8},{10,11... | collective-permute-start | bytes 208904 | tf_op jit(solution)/shard_map/ppermute | solution.py:469
  52.3 3.4 %collective-permute-start.16 = (f32[136,128]{1,0:T(8,128)S(1)}, f32[136,128]{1,0:T(8,128)S(1)}, u32[]{:S(2)}, u32[]{:S(2)}) collective-permute-start(f32[136,128]{1,0:T(8,128)S(1)} %collective-permute-done.15.refs_2_), channel_id=1, source_target_pairs={{0,1},{1,0},{2,3},{3,2},{4,5},{5,4},{6,7},{7,6},{8,9},{9,8},{10,11... | collective-permute-start | bytes 208904 | tf_op jit(solution)/shard_map/ppermute | solution.py:469
  53.0 2.7 %collective-permute-start.14 = (f32[136,128]{1,0:T(8,128)S(1)}, f32[136,128]{1,0:T(8,128)S(1)}, u32[]{:S(2)}, u32[]{:S(2)}) collective-permute-start(f32[136,128]{1,0:T(8,128)S(1)} %collective-permute-done.13.refs_1_), channel_id=1, source_target_pairs={{0,1},{1,0},{2,3},{3,2},{4,5},{5,4},{6,7},{7,6},{8,9},{9,8},{10,11... | collective-permute-start | bytes 208904 | tf_op jit(solution)/shard_map/ppermute | solution.py:469
